TPU v7x, 32 devices: a whole 2x2x4 slice. The times are simulated.
32 devices in a mesh: section: 2 (over y), dp: 2 (over core), expert: 4 (over z), tensor: 2 (over x).
Axes of the slice: x: 2, y: 2, z: 4, core: 2. Of those that a mesh axis runs over, the one named last changes fastest.
Arguments:
- boundary: bfloat16 [2, 2, 4096, 1536], P('section', None, ('dp', 'expert')), may hold values from -6 to 6
- segments: int32 [2, 4096], P(None, ('dp', 'expert')), may hold values from 0 to 19, never falling along the last dimension, each value on 1 to 800 neighbouring positions
- expert_ids: int32 [2, 2, 4096, 8], P('section', None, ('dp', 'expert', 'tensor')), may hold values from 0 to 31, all different within a row; in each aligned block of 256 rows (0 to 255, 256 to 511, ..., all dimensions but the last counted through in order) at most 96 rows name the same one
- attn_gain: float32 [2, 1536], P('section'), may hold values from 0.5 to 1.5
- query_weight: bfloat16 [2, 1536, 1536], P('section', None, 'tensor'), may hold values from -0.15625 to 0.15625
- key_weight: bfloat16 [2, 1536, 512], P('section', None, 'tensor'), may hold values from -0.15625 to 0.15625
- value_weight: bfloat16 [2, 1536, 512], P('section', None, 'tensor'), may hold values from -0.15625 to 0.15625
- out_weight: bfloat16 [2, 1536, 1536], P('section', 'tensor'), may hold values from -0.625 to 0.625
- ffn_gain: float32 [2, 1536], P('section'), may hold values from 0.5 to 1.5
- router_weight: bfloat16 [2, 1536, 32], P('section'), may hold values from -0.078125 to 0.078125
- gate_weight: bfloat16 [2, 32, 1536, 512], P('section', ('expert', 'tensor')), may hold values from -0.15625 to 0.15625
- up_weight: bfloat16 [2, 32, 1536, 512], P('section', ('expert', 'tensor')), may hold values from -0.15625 to 0.15625
- down_weight: bfloat16 [2, 32, 512, 1536], P('section', ('expert', 'tensor')), may hold values from -0.75 to 0.75
Outputs:
- ends_out: bfloat16 [2, 2, 4096, 1536], P('section', None, ('dp', 'expert'))
- attn_gain_grad: float32 [2, 1536], P('section')
- query_grad: float32 [2, 1536, 1536], P('section', None, 'tensor')
- key_grad: float32 [2, 1536, 512], P('section', None, 'tensor')
- value_grad: float32 [2, 1536, 512], P('section', None, 'tensor')
- out_grad: float32 [2, 1536, 1536], P('section', 'tensor')
- ffn_gain_grad: float32 [2, 1536], P('section')
- router_grad: float32 [2, 1536, 32], P('section')
- gate_grad: float32 [2, 32, 1536, 512], P('section', ('expert', 'tensor'))
- up_grad: float32 [2, 32, 1536, 512], P('section', ('expert', 'tensor'))
- down_grad: float32 [2, 32, 512, 1536], P('section', ('expert', 'tensor'))
Inputs may be any that keep to these rules, and one draw needn't show every extreme that they name: `expert_ids`: in each aligned block of 256 rows (one device's tokens of one layer and micro-batch), no expert is named by more than 96 rows, a bound that some block reaches; the 8 experts of a row differ. `segments`: document numbers never fall along a row; a document holds 1 to 800 positions, some exactly 800.
All inputs are finite; a program needn't handle non-finite values.
Results may differ from a plain program's by a relative error of at most 0.03.
Values may be sent and summed in bfloat16 or wider, within the bound.
A program may use at most 448 MiB of HBM per device.

v0:
```python
import jax
import jax.numpy as jnp
from jax import lax
from jax.sharding import PartitionSpec as P

HD = 64
TOPK = 8
EXPERTS = 32
LEN = 256


EPS = 1e-06
THETA = 10000.0
NEG_BIG = -1e30


def shifted(block, axis, distance):
    devices = range(lax.axis_size(axis))
    route = [(i - distance, i) for i in devices if i - distance in devices]
    return lax.ppermute(block, axis, route)


def rms_scale(values):
    return lax.rsqrt(jnp.mean(values * values, axis=-1, keepdims=True) + EPS)


def norm_back(grad_out, values, scale_col, gain_vec):
    weighted = grad_out * gain_vec
    inner_mean = jnp.mean(weighted * values, axis=-1, keepdims=True)
    grad_values = scale_col * weighted - values * (scale_col * scale_col * scale_col) * inner_mean
    grad_gain = jnp.sum(grad_out * values * scale_col, axis=0)
    return (grad_values, grad_gain)


def rope_tables(row_count, head_width, length):
    position = (jnp.arange(row_count) % length).astype(jnp.float32)
    frequency = THETA ** (-2.0 * jnp.arange(head_width // 2).astype(jnp.float32) / head_width)
    angles = position[:, None] * frequency[None, :]
    return (jnp.cos(angles), jnp.sin(angles))


def rotate(matrix, cosine_table, sine_table, head_width, direction):
    row_count = matrix.shape[0]
    by_head = matrix.reshape(row_count, -1, head_width)
    half_width = head_width // 2
    first_half = by_head[..., :half_width]
    second_half = by_head[..., half_width:]
    cosine = cosine_table[:, None, :]
    sine_val = sine_table[:, None, :] * direction
    turned = jnp.concatenate(
        [
            first_half * cosine - second_half * sine_val,
            second_half * cosine + first_half * sine_val,
        ],
        axis=-1,
    )
    return turned.reshape(row_count, -1)


def slot_count(share_rows):
    return share_rows * 3 // 8


def score_block(query_blk, key_blk, seg_row):
    length = query_blk.shape[0]
    kv_heads = key_blk.shape[1] // HD
    query_heads = query_blk.reshape(length, kv_heads, -1, HD)
    key_heads = key_blk.reshape(length, kv_heads, HD)
    scores = jnp.einsum(
        "qkgd,skd->kgqs", query_heads, key_heads, preferred_element_type=jnp.float32
    ) * HD ** (-0.5)
    position = jnp.arange(length)
    allowed = (position[:, None] >= position[None, :]) & (seg_row[:, None] == seg_row[None, :])
    return (jnp.where(allowed, scores, NEG_BIG), query_heads, key_heads)


def attend_forward(bundle):
    query_blk, key_blk, value_blk, seg_row = bundle
    length = query_blk.shape[0]
    scores, query_heads, key_heads = score_block(query_blk, key_blk, seg_row)
    top_score = jnp.max(scores, axis=-1, keepdims=True)
    exponent = jnp.exp(scores - top_score)
    row_total = jnp.sum(exponent, axis=-1, keepdims=True)
    probability = (exponent / row_total).astype(jnp.bfloat16)
    value_heads = value_blk.reshape(length, key_heads.shape[1], HD)
    mixture = jnp.einsum(
        "kgqs,skd->qkgd", probability, value_heads, preferred_element_type=jnp.float32
    )
    return (mixture.astype(jnp.bfloat16).reshape(length, -1), top_score + jnp.log(row_total))


def attend_backward(bundle):
    query_blk, key_blk, value_blk, seg_row, log_total, grad_mix = bundle
    length = query_blk.shape[0]
    scores, query_heads, key_heads = score_block(query_blk, key_blk, seg_row)
    kv_heads = key_heads.shape[1]
    probability = jnp.exp(scores - log_total)
    prob_low = probability.astype(jnp.bfloat16)
    grad_heads = grad_mix.reshape(length, kv_heads, -1, HD)
    value_heads = value_blk.reshape(length, kv_heads, HD)
    grad_value = jnp.einsum(
        "kgqs,qkgd->skd", prob_low, grad_heads, preferred_element_type=jnp.float32
    )
    grad_prob = jnp.einsum(
        "qkgd,skd->kgqs", grad_heads, value_heads, preferred_element_type=jnp.float32
    )
    centre = jnp.sum(probability * grad_prob, axis=-1, keepdims=True)
    grad_scores = (probability * (grad_prob - centre)).astype(jnp.bfloat16)
    grad_query = jnp.einsum(
        "kgqs,skd->qkgd", grad_scores, key_heads, preferred_element_type=jnp.float32
    ) * HD ** (-0.5)
    grad_key = jnp.einsum(
        "kgqs,qkgd->skd", grad_scores, query_heads, preferred_element_type=jnp.float32
    ) * HD ** (-0.5)
    return (
        grad_query.reshape(length, -1),
        grad_key.reshape(length, -1),
        grad_value.reshape(length, -1),
    )


def attention_forward(hidden_in, seg_rows, params):
    attn_gain, query_weight, key_weight, value_weight = params[:4]
    row_count = hidden_in.shape[0]
    scale_one = rms_scale(hidden_in)
    normed = (hidden_in * scale_one * attn_gain).astype(jnp.bfloat16)
    query_proj = jnp.dot(normed, query_weight, preferred_element_type=jnp.float32)
    key_proj = jnp.dot(normed, key_weight, preferred_element_type=jnp.float32)
    value_rot = jnp.dot(normed, value_weight, preferred_element_type=jnp.float32).astype(
        jnp.bfloat16
    )
    cosine_table, sine_table = rope_tables(row_count, HD, LEN)
    query_rot = rotate(query_proj, cosine_table, sine_table, HD, 1.0).astype(jnp.bfloat16)
    key_rot = rotate(key_proj, cosine_table, sine_table, HD, 1.0).astype(jnp.bfloat16)
    seq_count = row_count // LEN
    mixed, log_total = lax.map(
        attend_forward,
        (
            query_rot.reshape(seq_count, LEN, -1),
            key_rot.reshape(seq_count, LEN, -1),
            value_rot.reshape(seq_count, LEN, -1),
            seg_rows.reshape(seq_count, LEN),
        ),
    )
    attended = mixed.reshape(row_count, -1)
    return (
        scale_one,
        normed,
        query_rot,
        key_rot,
        value_rot,
        attended,
        log_total,
        cosine_table,
        sine_table,
    )


def expert_plan(route_rows, capacity):
    pair_ids = route_rows.reshape(-1)
    onehot = (pair_ids[:, None] == jnp.arange(EXPERTS, dtype=jnp.int32)[None, :]).astype(jnp.int32)
    earlier = jnp.cumsum(onehot, axis=0) - onehot
    slot_pos = jnp.sum(earlier * onehot, axis=1)
    target = pair_ids * capacity + slot_pos
    source = (
        jnp.zeros((EXPERTS * capacity,), jnp.int32)
        .at[target]
        .set(jnp.arange(pair_ids.shape[0], dtype=jnp.int32) + 1)
    )
    return (target.reshape(route_rows.shape), source)


def send_out(buffer):
    return lax.all_to_all(buffer, ("expert", "tensor"), split_axis=0, concat_axis=1, tiled=True)


def send_home(produced):
    return lax.all_to_all(produced, ("expert", "tensor"), split_axis=1, concat_axis=0, tiled=True)


def moe_forward(middle_share, route_rows, params, outward, homeward):
    ffn_gain, router_weight, gate_weight, up_weight, down_weight = params[5:]
    share_rows = middle_share.shape[0]
    capacity = slot_count(share_rows)
    scale_two = rms_scale(middle_share)
    normed_two = (middle_share * scale_two * ffn_gain).astype(jnp.bfloat16)
    logits = jnp.dot(normed_two, router_weight, preferred_element_type=jnp.float32)
    member = route_rows[:, :, None] == jnp.arange(EXPERTS, dtype=jnp.int32)[None, None, :]
    chosen = jnp.sum(jnp.where(member, logits[:, None, :], 0.0), axis=2)
    exponent = jnp.exp(chosen - jnp.max(chosen, axis=1, keepdims=True))
    gates = exponent / jnp.sum(exponent, axis=1, keepdims=True)
    target, source = expert_plan(route_rows, capacity)
    filled = (source > 0)[:, None]
    gathered = normed_two[jnp.maximum(source - 1, 0) // TOPK]
    buffer = jnp.where(filled, gathered, jnp.zeros_like(gathered)).reshape(EXPERTS, capacity, -1)
    received = outward(buffer)
    gate_pre = jnp.einsum("erd,edf->erf", received, gate_weight, preferred_element_type=jnp.float32)
    up_pre = jnp.einsum("erd,edf->erf", received, up_weight, preferred_element_type=jnp.float32)
    hidden = (jax.nn.silu(gate_pre) * up_pre).astype(jnp.bfloat16)
    produced = jnp.einsum(
        "erf,efd->erd", hidden, down_weight, preferred_element_type=jnp.float32
    ).astype(jnp.bfloat16)
    returned = homeward(produced)
    picked = returned.reshape(EXPERTS * capacity, -1)[target]
    addition = jnp.einsum("tk,tkd->td", gates, picked, preferred_element_type=jnp.float32)
    return (
        scale_two,
        normed_two,
        member,
        gates,
        target,
        source,
        received,
        gate_pre,
        up_pre,
        hidden,
        picked,
        addition,
    )


def section_forward(layer_in, seg_rows, route_rows, params, share_start, share_rows):
    hidden_in = layer_in.astype(jnp.float32)
    attn_parts = attention_forward(hidden_in, seg_rows, params)
    partial_sum = jnp.dot(attn_parts[5], params[4], preferred_element_type=jnp.float32)
    own_share = lax.dynamic_slice_in_dim(hidden_in, share_start, share_rows, 0)
    summed = lax.psum(partial_sum.astype(jnp.bfloat16), "tensor").astype(jnp.float32)
    branch = lax.dynamic_slice_in_dim(summed, share_start, share_rows, 0)
    middle_share = own_share + branch
    moe_parts = moe_forward(middle_share, route_rows, params, send_out, send_home)
    block_share = middle_share + moe_parts[-1]
    block_full = lax.all_gather(
        block_share.astype(jnp.bfloat16), "tensor", axis=0, tiled=True
    ).astype(block_share.dtype)
    return (block_full, middle_share, moe_parts)


def section_backward(layer_in, middle_share, grad_top, seg_rows, params, share_start, kept_parts):
    (
        attn_gain,
        query_weight,
        key_weight,
        value_weight,
        out_weight,
        ffn_gain,
        router_weight,
        gate_weight,
        up_weight,
        down_weight,
    ) = params
    hidden_in = layer_in.astype(jnp.float32)
    row_count = hidden_in.shape[0]
    share_rows = middle_share.shape[0]
    capacity = slot_count(share_rows)
    (
        scale_one,
        normed,
        query_rot,
        key_rot,
        value_rot,
        attended,
        log_total,
        cosine_table,
        sine_table,
    ) = attention_forward(hidden_in, seg_rows, params)
    (
        scale_two,
        normed_two,
        member,
        gates,
        target,
        source,
        received,
        gate_pre,
        up_pre,
        hidden,
        picked,
        addition,
    ) = kept_parts
    grad_share = lax.dynamic_slice_in_dim(grad_top, share_start, share_rows, 0)
    grad_picked = (gates[:, :, None] * grad_share[:, None, :]).astype(jnp.bfloat16)
    grad_gates = jnp.einsum("td,tkd->tk", grad_share, picked, preferred_element_type=jnp.float32)
    grad_chosen = gates * (grad_gates - jnp.sum(gates * grad_gates, axis=1, keepdims=True))
    grad_logits = jnp.sum(jnp.where(member, grad_chosen[:, :, None], 0.0), axis=1).astype(
        jnp.bfloat16
    )
    router_grad = jnp.einsum(
        "td,te->de", normed_two, grad_logits, preferred_element_type=jnp.float32
    )
    grad_normed = jnp.einsum(
        "te,de->td", grad_logits, router_weight, preferred_element_type=jnp.float32
    )
    filled = (source > 0)[:, None]
    flat_grad = grad_picked.reshape(share_rows * TOPK, -1)
    gathered = flat_grad[jnp.maximum(source - 1, 0)]
    grad_buffer = jnp.where(filled, gathered, jnp.zeros_like(gathered)).reshape(
        EXPERTS, capacity, -1
    )
    sent = lax.all_to_all(
        grad_buffer, ("expert", "tensor"), split_axis=0, concat_axis=1, tiled=True
    )
    grad_hidden = jnp.einsum("erd,efd->erf", sent, down_weight, preferred_element_type=jnp.float32)
    sigmoid_gate = jax.nn.sigmoid(gate_pre)
    grad_gate = (
        grad_hidden * up_pre * sigmoid_gate * (1.0 + gate_pre * (1.0 - sigmoid_gate))
    ).astype(jnp.bfloat16)
    grad_up = (grad_hidden * gate_pre * sigmoid_gate).astype(jnp.bfloat16)
    down_grad = jnp.einsum("erf,erd->efd", hidden, sent, preferred_element_type=jnp.float32)
    gate_grad = jnp.einsum("erd,erf->edf", received, grad_gate, preferred_element_type=jnp.float32)
    up_grad = jnp.einsum("erd,erf->edf", received, grad_up, preferred_element_type=jnp.float32)
    grad_rows = jnp.einsum(
        "erf,edf->erd", grad_gate, gate_weight, preferred_element_type=jnp.float32
    )
    grad_rows = (
        grad_rows
        + jnp.einsum("erf,edf->erd", grad_up, up_weight, preferred_element_type=jnp.float32)
    ).astype(jnp.bfloat16)
    back_rows = lax.all_to_all(
        grad_rows, ("expert", "tensor"), split_axis=1, concat_axis=0, tiled=True
    )
    grad_normed = grad_normed + jnp.sum(
        back_rows.reshape(EXPERTS * capacity, -1)[target].astype(jnp.float32), axis=1
    )
    grad_middle, ffn_gain_grad = norm_back(grad_normed, middle_share, scale_two, ffn_gain)
    grad_middle = grad_middle + grad_share
    grad_mid_full = lax.all_gather(
        grad_middle.astype(jnp.bfloat16), "tensor", axis=0, tiled=True
    ).astype(grad_middle.dtype)
    grad_mid_low = grad_mid_full.astype(jnp.bfloat16)
    out_grad = jnp.einsum("rh,rd->hd", attended, grad_mid_low, preferred_element_type=jnp.float32)
    grad_attended = jnp.einsum(
        "rd,hd->rh", grad_mid_low, out_weight, preferred_element_type=jnp.float32
    ).astype(jnp.bfloat16)
    seq_count = row_count // LEN
    grad_query, grad_key, grad_value = lax.map(
        attend_backward,
        (
            query_rot.reshape(seq_count, LEN, -1),
            key_rot.reshape(seq_count, LEN, -1),
            value_rot.reshape(seq_count, LEN, -1),
            seg_rows.reshape(seq_count, LEN),
            log_total,
            grad_attended.reshape(seq_count, LEN, -1),
        ),
    )
    grad_query = rotate(
        grad_query.reshape(row_count, -1), cosine_table, sine_table, HD, -1.0
    ).astype(jnp.bfloat16)
    grad_key = rotate(grad_key.reshape(row_count, -1), cosine_table, sine_table, HD, -1.0).astype(
        jnp.bfloat16
    )
    grad_value = grad_value.reshape(row_count, -1).astype(jnp.bfloat16)
    query_grad = jnp.einsum("rd,rh->dh", normed, grad_query, preferred_element_type=jnp.float32)
    key_grad = jnp.einsum("rd,rh->dh", normed, grad_key, preferred_element_type=jnp.float32)
    value_grad = jnp.einsum("rd,rh->dh", normed, grad_value, preferred_element_type=jnp.float32)
    grad_normed_one = jnp.einsum(
        "rh,dh->rd", grad_query, query_weight, preferred_element_type=jnp.float32
    )
    grad_normed_one = grad_normed_one + jnp.einsum(
        "rh,dh->rd", grad_key, key_weight, preferred_element_type=jnp.float32
    )
    grad_normed_one = grad_normed_one + jnp.einsum(
        "rh,dh->rd", grad_value, value_weight, preferred_element_type=jnp.float32
    )
    grad_normed_one = lax.psum(grad_normed_one.astype(jnp.bfloat16), "tensor").astype(jnp.float32)
    grad_input, attn_gain_grad = norm_back(grad_normed_one, hidden_in, scale_one, attn_gain)
    grad_input = grad_input + grad_mid_full
    return (
        grad_input,
        (
            attn_gain_grad,
            query_grad,
            key_grad,
            value_grad,
            out_grad,
            ffn_gain_grad,
            router_grad,
            gate_grad,
            up_grad,
            down_grad,
        ),
    )


def stack_zeros(piece_arr, count):
    return jnp.zeros((count,) + piece_arr.shape, piece_arr.dtype)


def on_device(
    boundary,
    segments,
    expert_ids,
    attn_gain,
    query_weight,
    key_weight,
    value_weight,
    out_weight,
    ffn_gain,
    router_weight,
    gate_weight,
    up_weight,
    down_weight,
):
    params = tuple(
        (
            array_in[0]
            for array_in in (
                attn_gain,
                query_weight,
                key_weight,
                value_weight,
                out_weight,
                ffn_gain,
                router_weight,
                gate_weight,
                up_weight,
                down_weight,
            )
        )
    )
    section_index = lax.axis_index("section")
    tensor_index = lax.axis_index("tensor")
    own_rows = boundary[0]
    micro_count = own_rows.shape[0]
    row_count = own_rows.shape[1]
    model_width = own_rows.shape[2]
    share_rows = expert_ids.shape[2]
    share_start = tensor_index * share_rows
    routes = expert_ids[0]
    kept_inputs = jnp.zeros((micro_count, row_count, model_width), jnp.bfloat16)
    kept_middle = jnp.zeros((micro_count, share_rows, model_width), jnp.float32)
    block_outputs = jnp.zeros((micro_count, row_count, model_width), jnp.bfloat16)
    arrived = jnp.zeros((row_count, model_width), jnp.bfloat16)
    kept_moe = None
    for tick_idx in range(micro_count + 1):
        micro_idx = tick_idx - section_index
        is_valid = (micro_idx >= 0) & (micro_idx < micro_count)
        slot_idx = jnp.clip(micro_idx, 0, micro_count - 1)
        layer_in = jnp.where(section_index == 0, own_rows[min(tick_idx, micro_count - 1)], arrived)
        seg_rows = lax.dynamic_index_in_dim(segments, slot_idx, 0, keepdims=False)
        route_rows = lax.dynamic_index_in_dim(routes, slot_idx, 0, keepdims=False)
        block_full, middle_share, moe_parts = section_forward(
            layer_in, seg_rows, route_rows, params, share_start, share_rows
        )
        block_low = block_full.astype(jnp.bfloat16)
        kept_inputs = jnp.where(
            is_valid,
            lax.dynamic_update_index_in_dim(kept_inputs, layer_in, slot_idx, 0),
            kept_inputs,
        )
        kept_middle = jnp.where(
            is_valid,
            lax.dynamic_update_index_in_dim(kept_middle, middle_share, slot_idx, 0),
            kept_middle,
        )
        block_outputs = jnp.where(
            is_valid,
            lax.dynamic_update_index_in_dim(block_outputs, block_low, slot_idx, 0),
            block_outputs,
        )
        if kept_moe is None:
            kept_moe = tuple((stack_zeros(piece_arr, micro_count) for piece_arr in moe_parts))
        kept_moe = tuple(
            (
                jnp.where(
                    is_valid,
                    lax.dynamic_update_index_in_dim(stack_arr, piece_arr, slot_idx, 0),
                    stack_arr,
                )
                for stack_arr, piece_arr in zip(kept_moe, moe_parts)
            )
        )
        arrived = shifted(block_low, "section", 1)
    grads = tuple((jnp.zeros(param_arr.shape, jnp.float32) for param_arr in params))
    input_grads = jnp.zeros((micro_count, row_count, model_width), jnp.bfloat16)
    grad_arrived = jnp.zeros((row_count, model_width), jnp.bfloat16)
    for tick_idx in range(micro_count + 1):
        micro_idx = tick_idx - (1 - section_index)
        is_valid = (micro_idx >= 0) & (micro_idx < micro_count)
        slot_idx = jnp.clip(micro_idx, 0, micro_count - 1)
        grad_top = jnp.where(
            section_index == 1, own_rows[min(tick_idx, micro_count - 1)], grad_arrived
        ).astype(jnp.float32)
        layer_in = lax.dynamic_index_in_dim(kept_inputs, slot_idx, 0, keepdims=False)
        middle_share = lax.dynamic_index_in_dim(kept_middle, slot_idx, 0, keepdims=False)
        seg_rows = lax.dynamic_index_in_dim(segments, slot_idx, 0, keepdims=False)
        route_rows = lax.dynamic_index_in_dim(routes, slot_idx, 0, keepdims=False)
        tick_moe = tuple(
            (
                lax.dynamic_index_in_dim(stack_arr, slot_idx, 0, keepdims=False)
                for stack_arr in kept_moe
            )
        )
        grad_input, tick_grads = section_backward(
            layer_in, middle_share, grad_top, seg_rows, params, share_start, tick_moe
        )
        valid_weight = is_valid.astype(jnp.float32)
        grads = tuple(
            (
                total_grad + valid_weight * tick_part
                for total_grad, tick_part in zip(grads, tick_grads)
            )
        )
        grad_low = grad_input.astype(jnp.bfloat16)
        input_grads = jnp.where(
            is_valid,
            lax.dynamic_update_index_in_dim(input_grads, grad_low, slot_idx, 0),
            input_grads,
        )
        grad_arrived = shifted(grad_low, "section", -1)
    dense = (
        lax.psum(grads[0].astype(jnp.bfloat16), ("dp", "expert")).astype(jnp.float32),
        lax.psum(grads[1].astype(jnp.bfloat16), ("dp", "expert")).astype(jnp.float32),
        lax.psum(grads[2].astype(jnp.bfloat16), ("dp", "expert")).astype(jnp.float32),
        lax.psum(grads[3].astype(jnp.bfloat16), ("dp", "expert")).astype(jnp.float32),
        lax.psum(grads[4].astype(jnp.bfloat16), ("dp", "expert")).astype(jnp.float32),
    )
    shared = lax.psum((grads[5], grads[6]), ("dp", "expert", "tensor"))
    expert_sums = (
        lax.psum(grads[7].astype(jnp.bfloat16), "dp").astype(jnp.float32),
        lax.psum(grads[8].astype(jnp.bfloat16), "dp").astype(jnp.float32),
        lax.psum(grads[9].astype(jnp.bfloat16), "dp").astype(jnp.float32),
    )
    ends_out = jnp.where(section_index == 0, input_grads, block_outputs)[None]
    return (
        ends_out,
        dense[0][None],
        dense[1][None],
        dense[2][None],
        dense[3][None],
        dense[4][None],
        shared[0][None],
        shared[1][None],
        expert_sums[0][None],
        expert_sums[1][None],
        expert_sums[2][None],
    )


def solution(mesh):
    placed = (
        P("section", None, ("dp", "expert"), None),
        P(None, ("dp", "expert")),
        P("section", None, ("dp", "expert", "tensor"), None),
        P("section", None),
        P("section", None, "tensor"),
        P("section", None, "tensor"),
        P("section", None, "tensor"),
        P("section", "tensor", None),
        P("section", None),
        P("section", None, None),
        P("section", ("expert", "tensor"), None, None),
        P("section", ("expert", "tensor"), None, None),
        P("section", ("expert", "tensor"), None, None),
    )
    return jax.shard_map(
        on_device,
        mesh=mesh,
        in_specs=placed,
        out_specs=(
            P("section", None, ("dp", "expert"), None),
            P("section", None),
            P("section", None, "tensor"),
            P("section", None, "tensor"),
            P("section", None, "tensor"),
            P("section", "tensor", None),
            P("section", None),
            P("section", None, None),
            P("section", ("expert", "tensor"), None, None),
            P("section", ("expert", "tensor"), None, None),
            P("section", ("expert", "tensor"), None, None),
        ),
        check_vma=False,
    )
```

profile of v0, /device:TPU:25, one launch (start us, length us, event | category | flops | bytes accessed | tf_op | source)
XLA Modules:
  0.0 4893.6 jit_solution(6031390460724693021)
XLA Ops:
  30.5 17.7 while.108
  75.9 28.7 all-reduce.12.cloned.1.call-done
  110.0 14.5 gather_fusion
  132.7 209.8 %all_to_all.198 = bf16[32,96,1536]{2,1,0:T(8,128)(2,1)} all-to-all(bf16[32,96,1536]{2,1,0:T(8,128)(2,1)} %broadcast_select_fusion.6), channel_id=1, replica_groups=mesh['section'=2,'dp'=2,'expert'=4,'tensor'=2] {'expert','tensor'}, dimensions={0} | all-to-all | bytes 18874368 | tf_op jit(solution)/shard_map/all_to_all | solution.py:174
  395.0 32.7 copy.507
  436.8 15.9 reduce-window.24
  458.5 180.5 %all-to-all-done.1 = bf16[4,768,1536]{2,0,1:T(4,128)(2,1)} async-done(((bf16[4,768,1536]{2,0,1:T(4,128)(2,1)}), bf16[4,768,1536]{2,0,1:T(4,128)(2,1)}, u32[]{:S(2)}, u32[]{:S(2)}) %all-to-all-start.1) | async-done | bytes 9437216 | tf_op jit(solution)/shard_map/all_to_all | solution.py:178
  648.9 18.2 gather_fusion.1
  673.1 27.2 all-gather.7.cloned.1.call-done
  704.8 32.0 collective-permute-done
  752.3 17.7 while.109
  793.5 34.2 all-reduce.14.cloned.1.call-done
  832.9 14.5 gather_fusion.2
  855.6 209.7 %all_to_all.199 = bf16[32,96,1536]{2,1,0:T(8,128)(2,1)} all-to-all(bf16[32,96,1536]{2,1,0:T(8,128)(2,1)} %broadcast_select_fusion.5), channel_id=1, replica_groups=mesh['section'=2,'dp'=2,'expert'=4,'tensor'=2] {'expert','tensor'}, dimensions={0} | all-to-all | bytes 18874368 | tf_op jit(solution)/shard_map/all_to_all | solution.py:174
  1109.5 32.7 copy.521
  1150.9 202.7 %all-to-all-done.3 = bf16[4,768,1536]{2,0,1:T(4,128)(2,1)} async-done(((bf16[4,768,1536]{2,0,1:T(4,128)(2,1)}), bf16[4,768,1536]{2,0,1:T(4,128)(2,1)}, u32[]{:S(2)}, u32[]{:S(2)}) %all-to-all-start.3) | async-done | bytes 9437216 | tf_op jit(solution)/shard_map/all_to_all | solution.py:178
  1363.5 18.2 gather_fusion.3
  1387.8 27.4 all-gather.9.cloned.1.call-done
  1422.6 29.1 collective-permute-done.1
  1473.3 17.7 while.111
  1503.0 46.6 all-reduce.16.cloned.1.call-done
  1554.8 14.5 gather_fusion.4
  1577.4 209.7 %all_to_all.200 = bf16[32,96,1536]{2,1,0:T(8,128)(2,1)} all-to-all(bf16[32,96,1536]{2,1,0:T(8,128)(2,1)} %broadcast_select_fusion.4), channel_id=1, replica_groups=mesh['section'=2,'dp'=2,'expert'=4,'tensor'=2] {'expert','tensor'}, dimensions={0} | all-to-all | bytes 18874368 | tf_op jit(solution)/shard_map/all_to_all | solution.py:174
  1831.2 32.7 copy.538
  1904.5 170.8 %all-to-all-done.5 = bf16[4,768,1536]{2,0,1:T(4,128)(2,1)} async-done(((bf16[4,768,1536]{2,0,1:T(4,128)(2,1)}), bf16[4,768,1536]{2,0,1:T(4,128)(2,1)}, u32[]{:S(2)}, u32[]{:S(2)}) %all-to-all-start.5) | async-done | bytes 9437216 | tf_op jit(solution)/shard_map/all_to_all | solution.py:178
  2085.3 18.4 gather_fusion.5
  2124.7 22.8 gather_fusion.6
  2188.0 177.6 %all-to-all-done.6 = bf16[32,96,1536]{2,1,0:T(8,128)(2,1)} async-done(((bf16[32,96,1536]{2,1,0:T(8,128)(2,1)}), bf16[32,96,1536]{2,1,0:T(8,128)(2,1)}, u32[]{:S(2)}, u32[]{:S(2)}) %all-to-all-start.6) | async-done | bytes 9437216 | tf_op jit(solution)/shard_map/all_to_all | solution.py:299
  2373.9 15.1 fusion.140
  2458.8 179.8 %all-to-all-done.7 = bf16[4,768,1536]{2,0,1:T(4,128)(2,1)} async-done(((bf16[4,768,1536]{2,0,1:T(4,128)(2,1)}), bf16[4,768,1536]{2,0,1:T(4,128)(2,1)}, u32[]{:S(2)}, u32[]{:S(2)}) %all-to-all-start.7) | async-done | bytes 9437216 | tf_op jit(solution)/shard_map/all_to_all | solution.py:318
  2648.2 18.4 gather_fusion.7
  2681.0 16.8 while.110
  2713.5 83.8 %while.112 = (s32[]{:T(128)}, f32[2,256,768]{1,0,2:T(2,128)}, f32[2,256,256]{1,0,2:T(2,128)}, bf16[2,256,256]{2,1,0:T(8,128)(2,1)}, bf16[2,256,256]{1,2,0:T(8,12...) while((s32[]{:T(128)}, f32[2,256,768]{1,0,2:T(2,128)}, ...), condition=%wide.region_53.54_spmd, body=%wide.region_51.53_spmd.sunk | while | flops 510850048 | bytes 59800872 | solution.py:335
  2724.7 16.6 dynamic_update_slice.151
  2766.6 16.6 dynamic_update_slice.151
  2814.0 51.6 %all-reduce.18.cloned.1.call-done = bf16[512,1536]{1,0:T(8,128)(2,1)} async-done(((bf16[512,1536]{1,0:T(8,128)(2,1)}), bf16[512,1536]{1,0:T(8,128)(2,1)}) %all-reduce.18.cloned.1.call-update) | async-done | bytes 1572880 | tf_op jit(solution)/shard_map/psum | solution.py:365
  2878.4 36.1 collective-permute-done.2
  2931.4 22.9 gather_fusion.8
  2962.3 209.2 %all_to_all.201 = bf16[32,96,1536]{2,1,0:T(8,128)(2,1)} all-to-all(bf16[32,96,1536]{2,1,0:T(8,128)(2,1)} %broadcast_select_fusion.2), channel_id=1, replica_groups=mesh['section'=2,'dp'=2,'expert'=4,'tensor'=2] {'expert','tensor'}, dimensions={0} | all-to-all | bytes 18874368 | tf_op jit(solution)/shard_map/all_to_all | solution.py:299
  3179.7 15.1 fusion.129
  3261.6 184.6 %all-to-all-done.9 = bf16[4,768,1536]{2,0,1:T(4,128)(2,1)} async-done(((bf16[4,768,1536]{2,0,1:T(4,128)(2,1)}), bf16[4,768,1536]{2,0,1:T(4,128)(2,1)}, u32[]{:S(2)}, u32[]{:S(2)}) %all-to-all-start.9) | async-done | bytes 9437216 | tf_op jit(solution)/shard_map/all_to_all | solution.py:318
  3455.8 18.2 gather_fusion.9
  3488.3 16.7 while.113
  3520.0 83.7 %while.114 = (s32[]{:T(128)}, f32[2,256,768]{1,0,2:T(2,128)}, f32[2,256,256]{1,0,2:T(2,128)}, bf16[2,256,256]{2,1,0:T(8,128)(2,1)}, bf16[2,256,256]{1,2,0:T(8,12...) while((s32[]{:T(128)}, f32[2,256,768]{1,0,2:T(2,128)}, ...), condition=%wide.region_67.68_spmd, body=%wide.region_65.67_spmd.sunk | while | flops 510850048 | bytes 59800872 | solution.py:335
  3531.2 16.6 dynamic_update_slice.156
  3573.0 16.6 dynamic_update_slice.156
  3620.4 51.6 %all-reduce.20.cloned.1.call-done = bf16[512,1536]{1,0:T(8,128)(2,1)} async-done(((bf16[512,1536]{1,0:T(8,128)(2,1)}), bf16[512,1536]{1,0:T(8,128)(2,1)}) %all-reduce.20.cloned.1.call-update) | async-done | bytes 1572880 | tf_op jit(solution)/shard_map/psum | solution.py:365
  3682.7 36.1 collective-permute-done.3
  3734.7 22.8 gather_fusion.10
  3765.7 209.4 %all_to_all.202 = bf16[32,96,1536]{2,1,0:T(8,128)(2,1)} all-to-all(bf16[32,96,1536]{2,1,0:T(8,128)(2,1)} %broadcast_select_fusion.1), channel_id=1, replica_groups=mesh['section'=2,'dp'=2,'expert'=4,'tensor'=2] {'expert','tensor'}, dimensions={0} | all-to-all | bytes 18874368 | tf_op jit(solution)/shard_map/all_to_all | solution.py:299
  3983.5 15.4 fusion.118
  4089.3 160.7 %all-to-all-done.11 = bf16[4,768,1536]{2,0,1:T(4,128)(2,1)} async-done(((bf16[4,768,1536]{2,0,1:T(4,128)(2,1)}), bf16[4,768,1536]{2,0,1:T(4,128)(2,1)}, u32[]{:S(2)}, u32[]{:S(2)}) %all-to-all-start.11) | async-done | bytes 9437216 | tf_op jit(solution)/shard_map/all_to_all | solution.py:318
  4259.8 18.1 gather_fusion.11
  4386.2 18.1 fusion.187
  4404.3 17.7 fusion.190
  4421.9 16.5 fusion.193
  4463.8 16.7 while.115
  4502.5 84.0 %while.116 = (s32[]{:T(128)}, f32[2,256,768]{1,0,2:T(2,128)}, f32[2,256,256]{1,0,2:T(2,128)}, bf16[2,256,256]{2,1,0:T(8,128)(2,1)}, bf16[2,256,256]{1,2,0:T(8,12...) while((s32[]{:T(128)}, f32[2,256,768]{1,0,2:T(2,128)}, ...), condition=%wide.region_81.82_spmd, body=%wide.region_79.81_spmd.sunk | while | flops 510850048 | bytes 59800872 | solution.py:335
  4514.0 16.6 dynamic_update_slice.161
  4555.8 16.6 dynamic_update_slice.161
  4627.4 29.1 psum.123
  4691.3 19.7 psum.118
  4711.6 81.7 %all-reduce.26.cloned.1.call-done = (bf16[1,1536,768]{2,1,0:T(8,128)(2,1)}, bf16[1,1536,256]{2,1,0:T(8,128)(2,1)}, bf16[1,1536,256]{2,1,0:T(8,128)(2,1)}, bf16[1,768,1536]{2,1,0:T(8,128)(2,1)}) async-done(((bf16[1,1536,768]{2,1,0:T(8,128)(2,1)}, bf16[1,1536,256]{2,1,0:T(8,128)(2,1)}, bf16[1,1536,256]{2,1,0:T(8,128)(2,1)}, bf16[1,768,1536]{2,1,0:T(8,128)(2,1)}), (bf16[1,1536,768]{2,1,0:T(8,128)(2,1)}, ...) | async-done | bytes 6291472 | tf_op jit(solution)/shard_map/psum | solution.py:513
  4803.0 82.3 %all-reduce.24.cloned.1.call-done = f32[1,1536,32]{1,2,0:T(8,128)} async-done(((f32[1,1536,32]{1,2,0:T(8,128)}), f32[1,1536,32]{1,2,0:T(8,128)}) %all-reduce.24.cloned.1.call-update) | async-done | bytes 196624 | tf_op jit(solution)/shard_map/psum | solution.py:518
  (1259 shorter events, 1423.5 us)
Async XLA Ops:
  7.2 41.0 copy-start
  7.2 97.3 %all-reduce.12.cloned.1.call-start = ((), (), s32[]{:S(2)}) async-start(), calls=%async_computation.12 | async-start | bytes 3145728 | tf_op jit(solution)/shard_map/psum | solution.py:227
  52.6 404.4 %copy-start.146 = (s32[1,1,256,8]{2,3,1,0:T(8,128)}, s32[1,1,256,8]{2,3,1,0:T(8,128)S(1)}, u32[]{:S(2)}) copy-start(s32[1,1,256,8]{2,3,1,0:T(8,128)S(1)} %get-tuple-element.1043) | copy-start | bytes 24580
  52.6 405.6 %copy-start.143 = (s32[1,1,256,8]{2,3,1,0:T(8,128)}, s32[1,1,256,8]{2,3,1,0:T(8,128)S(1)}, u32[]{:S(2)}) copy-start(s32[1,1,256,8]{2,3,1,0:T(8,128)S(1)} %get-tuple-element.1041) | copy-start | bytes 24580
  62.9 372.4 %copy-start.166 = (s32[2048]{0:T(1024)}, s32[2048]{0:T(1024)S(1)}, u32[]{:S(2)}) copy-start(s32[2048]{0:T(1024)S(1)} %fusion.410) | copy-start | bytes 24580
  62.9 44.4 copy-start.109
  350.9 22.2 slice-start
  357.3 15.8 slice-start.1
  427.7 211.3 %all-to-all-start.1 = ((bf16[4,768,1536]{2,0,1:T(4,128)(2,1)}), bf16[4,768,1536]{2,0,1:T(4,128)(2,1)}, u32[]{:S(2)}, u32[]{:S(2)}) async-start(bf16[4,768,1536]{2,0,1:T(4,128)(2,1)} %copy.507), calls=%async_computation.1 | async-start | bytes 18874368 | tf_op jit(solution)/shard_map/all_to_all | solution.py:178
  434.1 23.7 copy-start.70
  434.1 266.2 %all-gather.7.cloned.1.call-start = ((), (), s32[]{:S(2)}) async-start(), calls=%async_computation.13 | async-start | bytes 2359296 | tf_op jit(solution)/shard_map/all_gather | solution.py:232
  455.8 328.7 %copy-start.168 = (s32[2048]{0:T(1024)}, s32[2048]{0:T(1024)S(1)}, u32[]{:S(2)}) copy-start(s32[2048]{0:T(1024)S(1)} %fusion.407) | copy-start | bytes 24580
  458.3 190.6 %copy-start.153 = (f32[256,8]{0,1:T(8,128)}, f32[256,8]{0,1:T(8,128)S(1)}, u32[]{:S(2)}) copy-start(f32[256,8]{0,1:T(8,128)S(1)} %select_reduce_fusion.5) | copy-start | bytes 24580
  458.3 190.6 %copy-start.205 = (f32[256]{0:T(256)}, f32[256]{0:T(256)S(1)}, u32[]{:S(2)}) copy-start(f32[256]{0:T(256)S(1)} %reduce_max.81) | copy-start | bytes 3076
  458.3 190.6 %copy-start.219 = (f32[256]{0:T(256)}, f32[256]{0:T(256)S(1)}, u32[]{:S(2)}) copy-start(f32[256]{0:T(256)S(1)} %fusion.477) | copy-start | bytes 3076
  671.8 33.0 copy-start.228
  673.1 154.6 %all-reduce.14.cloned.1.call-start = ((), (), s32[]{:S(2)}) async-start(), calls=%async_computation.14 | async-start | bytes 3145728 | tf_op jit(solution)/shard_map/psum | solution.py:227
  700.3 36.5 collective-permute-start
  704.8 35.8 copy-start.47
  704.8 35.8 copy-start.127
  773.7 56.0 %copy-start.110 = (f32[1536]{0:T(1024)S(1)}, f32[1536]{0:T(1024)}, u32[]{:S(2)}) copy-start(f32[1536]{0:T(1024)} %copy-done.109) | copy-start | bytes 18436
  784.5 48.4 copy-start.170
  793.4 36.3 copy-start.158
  1142.2 211.4 %all-to-all-start.3 = ((bf16[4,768,1536]{2,0,1:T(4,128)(2,1)}), bf16[4,768,1536]{2,0,1:T(4,128)(2,1)}, u32[]{:S(2)}, u32[]{:S(2)}) async-start(bf16[4,768,1536]{2,0,1:T(4,128)(2,1)} %copy.521), calls=%async_computation.3 | async-start | bytes 18874368 | tf_op jit(solution)/shard_map/all_to_all | solution.py:178
  1148.8 266.5 %all-gather.9.cloned.1.call-start = ((), (), s32[]{:S(2)}) async-start(), calls=%async_computation.15 | async-start | bytes 2359296 | tf_op jit(solution)/shard_map/all_gather | solution.py:232
  1149.6 213.9 %copy-start.151 = (f32[256,8]{0,1:T(8,128)}, f32[256,8]{0,1:T(8,128)S(1)}, u32[]{:S(2)}) copy-start(f32[256,8]{0,1:T(8,128)S(1)} %select_reduce_fusion.4) | copy-start | bytes 24580
  1386.4 33.2 copy-start.227
  1387.7 161.8 %all-reduce.16.cloned.1.call-start = ((), (), s32[]{:S(2)}) async-start(), calls=%async_computation.16 | async-start | bytes 3145728 | tf_op jit(solution)/shard_map/psum | solution.py:227
  1415.2 36.5 collective-permute-start.1
  1422.6 31.5 copy-start.48
  1422.6 31.5 copy-start.128
  1494.6 56.9 %copy-start.111 = (f32[1536]{0:T(1024)S(1)}, f32[1536]{0:T(1024)}, u32[]{:S(2)}) copy-start(f32[1536]{0:T(1024)} %copy-done.109) | copy-start | bytes 18436
  1502.8 48.7 copy-start.159
  1863.9 211.4 %all-to-all-start.5 = ((bf16[4,768,1536]{2,0,1:T(4,128)(2,1)}), bf16[4,768,1536]{2,0,1:T(4,128)(2,1)}, u32[]{:S(2)}, u32[]{:S(2)}) async-start(bf16[4,768,1536]{2,0,1:T(4,128)(2,1)} %copy.538), calls=%async_computation.5 | async-start | bytes 18874368 | tf_op jit(solution)/shard_map/all_to_all | solution.py:178
  1904.4 180.8 %copy-start.149 = (f32[256,8]{0,1:T(8,128)}, f32[256,8]{0,1:T(8,128)S(1)}, u32[]{:S(2)}) copy-start(f32[256,8]{0,1:T(8,128)S(1)} %select_reduce_fusion.3) | copy-start | bytes 24580
  1904.5 180.8 %copy-start.201 = (f32[256]{0:T(256)}, f32[256]{0:T(256)S(1)}, u32[]{:S(2)}) copy-start(f32[256]{0:T(256)S(1)} %reduce_max.83) | copy-start | bytes 3076
  1904.5 180.8 %copy-start.215 = (f32[256]{0:T(256)}, f32[256]{0:T(256)S(1)}, u32[]{:S(2)}) copy-start(f32[256]{0:T(256)S(1)} %fusion.479) | copy-start | bytes 3076
  1904.5 214.4 %copy-start.155 = (f32[2,256,8]{1,2,0:T(8,128)}, f32[2,256,8]{1,2,0:T(8,128)S(1)}, u32[]{:S(2)}) copy-start(f32[2,256,8]{1,2,0:T(8,128)S(1)} %constant_dynamic-update-slice_fusion.12) | copy-start | bytes 49156
  2155.5 210.1 %all-to-all-start.6 = ((bf16[32,96,1536]{2,1,0:T(8,128)(2,1)}), bf16[32,96,1536]{2,1,0:T(8,128)(2,1)}, u32[]{:S(2)}, u32[]{:S(2)}) async-start(bf16[32,96,1536]{2,1,0:T(8,128)(2,1)} %broadcast_select_fusion.3), calls=%async_computation.6 | async-start | bytes 18874368 | tf_op jit(solution)/shard_map/all_to_all | solution.py:299
  2167.3 13.7 slice-start.10
  2428.7 209.9 %all-to-all-start.7 = ((bf16[4,768,1536]{2,0,1:T(4,128)(2,1)}), bf16[4,768,1536]{2,0,1:T(4,128)(2,1)}, u32[]{:S(2)}, u32[]{:S(2)}) async-start(bf16[4,768,1536]{2,0,1:T(4,128)(2,1)} %copy.544), calls=%async_computation.7 | async-start | bytes 18874368 | tf_op jit(solution)/shard_map/all_to_all | solution.py:318
  2433.8 272.8 %all-gather.11.cloned.1.call-start = ((), (), s32[]{:S(2)}) async-start(), calls=%async_computation.17 | async-start | bytes 2359296 | tf_op jit(solution)/shard_map/all_gather | solution.py:326
  2458.8 214.9 %copy-start.160 = (bf16[256,32]{0,1:T(8,128)(2,1)}, bf16[256,32]{0,1:T(8,128)(2,1)S(1)}, u32[]{:S(2)}) copy-start(bf16[256,32]{0,1:T(8,128)(2,1)S(1)} %select_reduce_fusion.2) | copy-start | bytes 49156
  2679.4 186.2 %all-reduce.18.cloned.1.call-start = ((), (), s32[]{:S(2)}) async-start(), calls=%async_computation.18 | async-start | bytes 3145728 | tf_op jit(solution)/shard_map/psum | solution.py:365
  2812.2 53.4 %copy-start.130 = (f32[1536]{0:T(1024)S(1)}, f32[1536]{0:T(1024)}, u32[]{:S(2)}) copy-start(f32[1536]{0:T(1024)} %copy-done.126) | copy-start | bytes 18436
  2812.2 53.4 %copy-start.199 = (f32[512]{0:T(512)S(1)}, f32[512]{0:T(512)}, u32[]{:S(2)}) copy-start(f32[512]{0:T(512)} %copy-done.198) | copy-start | bytes 6148
  2877.0 37.5 collective-permute-start.2
  3234.3 211.9 %all-to-all-start.9 = ((bf16[4,768,1536]{2,0,1:T(4,128)(2,1)}), bf16[4,768,1536]{2,0,1:T(4,128)(2,1)}, u32[]{:S(2)}, u32[]{:S(2)}) async-start(bf16[4,768,1536]{2,0,1:T(4,128)(2,1)} %copy.562), calls=%async_computation.9 | async-start | bytes 18874368 | tf_op jit(solution)/shard_map/all_to_all | solution.py:318
  3241.3 271.8 %all-gather.13.cloned.1.call-start = ((), (), s32[]{:S(2)}) async-start(), calls=%async_computation.19 | async-start | bytes 2359296 | tf_op jit(solution)/shard_map/all_gather | solution.py:326
  3261.6 219.5 %copy-start.162 = (bf16[256,32]{0,1:T(8,128)(2,1)}, bf16[256,32]{0,1:T(8,128)(2,1)S(1)}, u32[]{:S(2)}) copy-start(bf16[256,32]{0,1:T(8,128)(2,1)S(1)} %select_reduce_fusion.1) | copy-start | bytes 49156
  3486.8 185.3 %all-reduce.20.cloned.1.call-start = ((), (), s32[]{:S(2)}) async-start(), calls=%async_computation.20 | async-start | bytes 3145728 | tf_op jit(solution)/shard_map/psum | solution.py:365
  3618.6 53.4 %copy-start.131 = (f32[1536]{0:T(1024)S(1)}, f32[1536]{0:T(1024)}, u32[]{:S(2)}) copy-start(f32[1536]{0:T(1024)} %copy-done.126) | copy-start | bytes 18436
  3618.6 53.4 %copy-start.182 = (f32[512]{0:T(512)S(1)}, f32[512]{0:T(512)}, u32[]{:S(2)}) copy-start(f32[512]{0:T(512)} %copy-done.181) | copy-start | bytes 6148
  3620.4 55.5 %copy-start.223 = (f32[512]{0:T(512)S(1)}, f32[512]{0:T(512)}, u32[]{:S(2)}) copy-start(f32[512]{0:T(512)} %get-tuple-element.1054) | copy-start | bytes 6148
  3681.3 37.5 collective-permute-start.3
  4038.2 211.7 %all-to-all-start.11 = ((bf16[4,768,1536]{2,0,1:T(4,128)(2,1)}), bf16[4,768,1536]{2,0,1:T(4,128)(2,1)}, u32[]{:S(2)}, u32[]{:S(2)}) async-start(bf16[4,768,1536]{2,0,1:T(4,128)(2,1)} %copy.577), calls=%async_computation.11 | async-start | bytes 18874368 | tf_op jit(solution)/shard_map/all_to_all | solution.py:318
  4045.1 450.2 %all-gather.15.cloned.1.call-start = ((), (), s32[]{:S(2)}) async-start(), calls=%async_computation.21 | async-start | bytes 2359296 | tf_op jit(solution)/shard_map/all_gather | solution.py:326
  4089.3 195.7 %copy-start.164 = (bf16[256,32]{0,1:T(8,128)(2,1)}, bf16[256,32]{0,1:T(8,128)(2,1)S(1)}, u32[]{:S(2)}) copy-start(bf16[256,32]{0,1:T(8,128)(2,1)S(1)} %select_reduce_fusion) | copy-start | bytes 49156
  4290.8 331.8 %all-gather.17.cloned.1.call-start = ((), (), s32[]{:S(2)}) async-start(), calls=%async_computation.23 | async-start | bytes 2359296 | tf_op jit(solution)/shard_map/all_gather | solution.py:232
  4307.1 349.5 %all-reduce.28.cloned.1.call-start = ((), (), s32[]{:S(2)}) async-start(), calls=%async_computation.26 | async-start | bytes 37748736 | tf_op jit(solution)/shard_map/psum | solution.py:520
  4438.5 240.6 %all-reduce.22.cloned.1.call-start = ((), (), s32[]{:S(2)}) async-start(), calls=%async_computation.22 | async-start | bytes 3145728 | tf_op jit(solution)/shard_map/psum | solution.py:365
  4599.4 193.9 %all-reduce.26.cloned.1.call-start = ((), (), s32[]{:S(2)}) async-start(), calls=%async_computation.25 | async-start | bytes 12582912 | tf_op jit(solution)/shard_map/psum | solution.py:513
  4615.7 269.6 %all-reduce.24.cloned.1.call-start = ((), (), s32[]{:S(2)}) async-start(), calls=%async_computation.24 | async-start | bytes 393216 | tf_op jit(solution)/shard_map/psum | solution.py:518
  4656.5 16.1 slice-start.8
  (229 other events, 1096.8 us)
Sparse Core Ops, SparseCore 0:
  52.0 52.4 all-reduce.11
  673.2 27.0 all-gather.6
  773.8 53.8 all-reduce.13
  1387.8 27.3 all-gather.8
  1494.7 54.7 all-reduce.15
  2679.5 27.0 all-gather.10
  2814.1 51.4 all-reduce.17
  3486.9 26.1 all-gather.12
  3620.5 51.4 all-reduce.19
  4290.9 26.1 all-gather.14
  4318.7 27.1 all-gather.16
  4438.6 64.1 all-reduce.27
  4599.6 52.7 all-reduce.21
  4655.6 137.6 all-reduce.25
  4797.5 87.6 all-reduce.23
where the time goes:
time: 4920 us; the launch traced here: 4890 us
  waiting for transfers between devices  1840 us (37%)
  blocking collectives  1100 us (22%)
  local copies, waits for them, and re-layouts  885 us (18%)
  matrix products  619 us (13%)
  other arithmetic  379 us (8%)
  starting transfers between devices  56.9 us (1%)
    all_to_all x3, blocking collectives, send_out(): lax.all_to_all(buffer, ('expert', 'tensor'), split_axis=0, concat_axis=1,...  629 us
    all_to_all x3, waiting for transfers between devices, send_home(): lax.all_to_all(produced, ('expert', 'tensor'), split_axis=1, concat_axis=...  554 us
    all_to_all x3, waiting for transfers between devices, section_backward(): lax.all_to_all(grad_rows, ('expert', 'tensor'), split_axis=1, concat_axis...  525 us
    all_to_all x2, blocking collectives, section_backward(): lax.all_to_all(grad_buffer, ('expert', 'tensor'), split_axis=0, concat_ax...  419 us
    all_to_all x1, waiting for transfers between devices, section_backward(): lax.all_to_all(grad_buffer, ('expert', 'tensor'), split_axis=0, concat_ax...  178 us
    dynamic_update_slice x36, local copies, waits for them, and re-layouts, section_backward(): lax.map(attend_backward, (query_rot.reshape(seq_count, LEN, -1), key_rot....  163 us
    ppermute x4, waiting for transfers between devices, shifted(): return lax.ppermute(block, axis, route)  133 us
    psum x3, waiting for transfers between devices, section_forward(): lax.psum(partial_sum.astype(jnp.bfloat16), 'tensor').astype(jnp.float32)  109 us
  transfers between devices with their start and end apart: 26, of which 22 were waited for; matrix products, arithmetic and copies ran while one was open for 13% of the time, Pallas kernels for 0%

commit v1 on v0

--- a/solution.py
+++ b/solution.py
@@ -1,8 +1,13 @@
+import functools
+
 import jax
 import jax.numpy as jnp
 from jax import lax
+from jax.experimental import pallas as pl
+from jax.experimental.pallas import tpu as pltpu
 from jax.sharding import PartitionSpec as P
 
+SECTION, DP, EXPERT, TENSOR = "section", "dp", "expert", "tensor"
 HD = 64
 TOPK = 8
 EXPERTS = 32
@@ -171,11 +176,11 @@
 
 
 def send_out(buffer):
-    return lax.all_to_all(buffer, ("expert", "tensor"), split_axis=0, concat_axis=1, tiled=True)
+    return lax.all_to_all(buffer, (EXPERT, TENSOR), split_axis=0, concat_axis=1, tiled=True)
 
 
 def send_home(produced):
-    return lax.all_to_all(produced, ("expert", "tensor"), split_axis=1, concat_axis=0, tiled=True)
+    return lax.all_to_all(produced, (EXPERT, TENSOR), split_axis=1, concat_axis=0, tiled=True)
 
 
 def moe_forward(middle_share, route_rows, params, outward, homeward):
@@ -224,13 +229,13 @@
     attn_parts = attention_forward(hidden_in, seg_rows, params)
     partial_sum = jnp.dot(attn_parts[5], params[4], preferred_element_type=jnp.float32)
     own_share = lax.dynamic_slice_in_dim(hidden_in, share_start, share_rows, 0)
-    summed = lax.psum(partial_sum.astype(jnp.bfloat16), "tensor").astype(jnp.float32)
+    summed = lax.psum(partial_sum.astype(jnp.bfloat16), TENSOR).astype(jnp.float32)
     branch = lax.dynamic_slice_in_dim(summed, share_start, share_rows, 0)
     middle_share = own_share + branch
     moe_parts = moe_forward(middle_share, route_rows, params, send_out, send_home)
     block_share = middle_share + moe_parts[-1]
     block_full = lax.all_gather(
-        block_share.astype(jnp.bfloat16), "tensor", axis=0, tiled=True
+        block_share.astype(jnp.bfloat16), TENSOR, axis=0, tiled=True
     ).astype(block_share.dtype)
     return (block_full, middle_share, moe_parts)
 
@@ -297,7 +302,7 @@
         EXPERTS, capacity, -1
     )
     sent = lax.all_to_all(
-        grad_buffer, ("expert", "tensor"), split_axis=0, concat_axis=1, tiled=True
+        grad_buffer, (EXPERT, TENSOR), split_axis=0, concat_axis=1, tiled=True
     )
     grad_hidden = jnp.einsum("erd,efd->erf", sent, down_weight, preferred_element_type=jnp.float32)
     sigmoid_gate = jax.nn.sigmoid(gate_pre)
@@ -316,7 +321,7 @@
         + jnp.einsum("erf,edf->erd", grad_up, up_weight, preferred_element_type=jnp.float32)
     ).astype(jnp.bfloat16)
     back_rows = lax.all_to_all(
-        grad_rows, ("expert", "tensor"), split_axis=1, concat_axis=0, tiled=True
+        grad_rows, (EXPERT, TENSOR), split_axis=1, concat_axis=0, tiled=True
     )
     grad_normed = grad_normed + jnp.sum(
         back_rows.reshape(EXPERTS * capacity, -1)[target].astype(jnp.float32), axis=1
@@ -324,7 +329,7 @@
     grad_middle, ffn_gain_grad = norm_back(grad_normed, middle_share, scale_two, ffn_gain)
     grad_middle = grad_middle + grad_share
     grad_mid_full = lax.all_gather(
-        grad_middle.astype(jnp.bfloat16), "tensor", axis=0, tiled=True
+        grad_middle.astype(jnp.bfloat16), TENSOR, axis=0, tiled=True
     ).astype(grad_middle.dtype)
     grad_mid_low = grad_mid_full.astype(jnp.bfloat16)
     out_grad = jnp.einsum("rh,rd->hd", attended, grad_mid_low, preferred_element_type=jnp.float32)
@@ -362,7 +367,7 @@
     grad_normed_one = grad_normed_one + jnp.einsum(
         "rh,dh->rd", grad_value, value_weight, preferred_element_type=jnp.float32
     )
-    grad_normed_one = lax.psum(grad_normed_one.astype(jnp.bfloat16), "tensor").astype(jnp.float32)
+    grad_normed_one = lax.psum(grad_normed_one.astype(jnp.bfloat16), TENSOR).astype(jnp.float32)
     grad_input, attn_gain_grad = norm_back(grad_normed_one, hidden_in, scale_one, attn_gain)
     grad_input = grad_input + grad_mid_full
     return (
@@ -418,8 +423,8 @@
             )
         )
     )
-    section_index = lax.axis_index("section")
-    tensor_index = lax.axis_index("tensor")
+    section_index = lax.axis_index(SECTION)
+    tensor_index = lax.axis_index(TENSOR)
     own_rows = boundary[0]
     micro_count = own_rows.shape[0]
     row_count = own_rows.shape[1]
@@ -470,7 +475,7 @@
                 for stack_arr, piece_arr in zip(kept_moe, moe_parts)
             )
         )
-        arrived = shifted(block_low, "section", 1)
+        arrived = shifted(block_low, SECTION, 1)
     grads = tuple((jnp.zeros(param_arr.shape, jnp.float32) for param_arr in params))
     input_grads = jnp.zeros((micro_count, row_count, model_width), jnp.bfloat16)
     grad_arrived = jnp.zeros((row_count, model_width), jnp.bfloat16)
@@ -507,19 +512,19 @@
             lax.dynamic_update_index_in_dim(input_grads, grad_low, slot_idx, 0),
             input_grads,
         )
-        grad_arrived = shifted(grad_low, "section", -1)
+        grad_arrived = shifted(grad_low, SECTION, -1)
     dense = (
-        lax.psum(grads[0].astype(jnp.bfloat16), ("dp", "expert")).astype(jnp.float32),
-        lax.psum(grads[1].astype(jnp.bfloat16), ("dp", "expert")).astype(jnp.float32),
-        lax.psum(grads[2].astype(jnp.bfloat16), ("dp", "expert")).astype(jnp.float32),
-        lax.psum(grads[3].astype(jnp.bfloat16), ("dp", "expert")).astype(jnp.float32),
-        lax.psum(grads[4].astype(jnp.bfloat16), ("dp", "expert")).astype(jnp.float32),
-    )
-    shared = lax.psum((grads[5], grads[6]), ("dp", "expert", "tensor"))
+        lax.psum(grads[0].astype(jnp.bfloat16), (DP, EXPERT)).astype(jnp.float32),
+        lax.psum(grads[1].astype(jnp.bfloat16), (DP, EXPERT)).astype(jnp.float32),
+        lax.psum(grads[2].astype(jnp.bfloat16), (DP, EXPERT)).astype(jnp.float32),
+        lax.psum(grads[3].astype(jnp.bfloat16), (DP, EXPERT)).astype(jnp.float32),
+        lax.psum(grads[4].astype(jnp.bfloat16), (DP, EXPERT)).astype(jnp.float32),
+    )
+    shared = lax.psum((grads[5], grads[6]), (DP, EXPERT, TENSOR))
     expert_sums = (
-        lax.psum(grads[7].astype(jnp.bfloat16), "dp").astype(jnp.float32),
-        lax.psum(grads[8].astype(jnp.bfloat16), "dp").astype(jnp.float32),
-        lax.psum(grads[9].astype(jnp.bfloat16), "dp").astype(jnp.float32),
+        lax.psum(grads[7].astype(jnp.bfloat16), DP).astype(jnp.float32),
+        lax.psum(grads[8].astype(jnp.bfloat16), DP).astype(jnp.float32),
+        lax.psum(grads[9].astype(jnp.bfloat16), DP).astype(jnp.float32),
     )
     ends_out = jnp.where(section_index == 0, input_grads, block_outputs)[None]
     return (
@@ -537,38 +542,2829 @@
     )
 
 
+MIB = 1024 * 1024
+NT = (((1,), (1,)), ((), ()))
+TN = (((0,), (0,)), ((), ()))
+
+
+def dot(left, right, dims=None):
+    if dims is None:
+        return jnp.dot(left, right, preferred_element_type=jnp.float32)
+    return lax.dot_general(left, right, dims, preferred_element_type=jnp.float32)
+
+
+def lane_grid(rows):
+    return lax.broadcasted_iota(jnp.int32, (rows, 2 * HD), 1)
+
+
+def turn_pair(slab, cosine, sine):
+    low_half = (lane_grid(slab.shape[0]) % HD) < HD // 2
+    partner = jnp.where(
+        low_half, pltpu.roll(slab, 2 * HD - HD // 2, 1), pltpu.roll(slab, HD // 2, 1)
+    )
+    return slab * cosine + partner * sine
+
+
+def pair_tables(length):
+    cosine, sine = rope_tables(length, HD, length)
+    return (
+        jnp.concatenate([cosine] * 4, axis=1),
+        jnp.concatenate([-sine, sine, -sine, sine], axis=1),
+    )
+
+
+def aligned_head(slabs, head, side, scale):
+    slab = slabs[head // 2]
+    if head % 2 != side:
+        slab = pltpu.roll(slab, HD, 1)
+    keep = (lane_grid(slab.shape[0]) // HD) == side
+    return jnp.where(keep, slab * scale, 0.0).astype(jnp.bfloat16)
+
+
+def one_side(slab, side):
+    return jnp.where((lane_grid(slab.shape[0]) // HD) == side, slab, jnp.zeros_like(slab))
+
+
+def slabs_of(matrix, start, count):
+    return [matrix[:, start + 2 * HD * i : start + 2 * HD * (i + 1)] for i in range(count)]
+
+
+def attend_part(group, rows, weights, tables, allowed):
+    width = weights.shape[1]
+    query_width = width * group // (group + 2)
+    key_width = (width - query_width) // 2
+    cosine, sine = tables
+    projected = dot(rows, weights)
+    query = [
+        turn_pair(slab, cosine, sine) for slab in slabs_of(projected, 0, query_width // (2 * HD))
+    ]
+    key = [
+        turn_pair(slab, cosine, sine).astype(jnp.bfloat16)
+        for slab in slabs_of(projected, query_width, key_width // (2 * HD))
+    ]
+    value = [
+        slab.astype(jnp.bfloat16)
+        for slab in slabs_of(projected, query_width + key_width, key_width // (2 * HD))
+    ]
+    turned = jnp.concatenate([slab.astype(jnp.bfloat16) for slab in query] + key + value, axis=1)
+    query = [slab.astype(jnp.bfloat16).astype(jnp.float32) for slab in query]
+    mixed = [None] * len(query)
+    for kv_head in range(key_width // HD):
+        side = kv_head % 2
+        key_slab = key[kv_head // 2]
+        value_side = one_side(value[kv_head // 2], side)
+        for head in range(group * kv_head, group * (kv_head + 1)):
+            scores = dot(aligned_head(query, head, side, HD**-0.5), key_slab, NT)
+            scores = jnp.where(allowed, scores, NEG_BIG)
+            exponent = jnp.exp(scores - jnp.max(scores, axis=1, keepdims=True))
+            probability = exponent / jnp.sum(exponent, axis=1, keepdims=True)
+            part = dot(probability.astype(jnp.bfloat16), value_side)
+            if head % 2 != side:
+                part = pltpu.roll(part, HD, 1)
+            mixed[head // 2] = part if head % 2 == 0 else mixed[head // 2] + part
+    return turned, jnp.concatenate([part.astype(jnp.bfloat16) for part in mixed], axis=1)
+
+
+def allowed_pairs(seg_col, seg_row):
+    length = seg_row.shape[1]
+    row = lax.broadcasted_iota(jnp.int32, (length, length), 0)
+    column = lax.broadcasted_iota(jnp.int32, (length, length), 1)
+    return (row >= column) & (seg_col == seg_row)
+
+
+def of_section(first, second):
+    return jnp.where(lax.axis_index(SECTION) == 0, first[...], second[...])
+
+
+def start_of_section(first, second, to, sem):
+    @pl.when(lax.axis_index(SECTION) == 0)
+    def _():
+        pltpu.make_async_copy(first, to, sem).start()
+
+    @pl.when(lax.axis_index(SECTION) != 0)
+    def _():
+        pltpu.make_async_copy(second, to, sem).start()
+
+
+def attn_forward_kernel(
+    group,
+    x_first,
+    x_second,
+    gain_one_ref,
+    wqkv_hbm,
+    wo_hbm,
+    cos_ref,
+    sin_ref,
+    seg_col_ref,
+    seg_row_ref,
+    gain_two_ref,
+    h1_ref,
+    xn1_ref,
+    qkv_ref,
+    att_ref,
+    xn2_ref,
+    x_ref,
+    wqkv_ref,
+    wo_ref,
+    x_sem,
+    weight_sem,
+):
+    parts = wqkv_ref.shape[0]
+
+    def weight_copies(half):
+        return [
+            pltpu.make_async_copy(hbm.at[half], ref.at[half], weight_sem.at[i, half])
+            for i, (hbm, ref) in enumerate(((wqkv_hbm, wqkv_ref), (wo_hbm, wo_ref)))
+        ]
+
+    start_of_section(x_first, x_second, x_ref, x_sem)
+    for copy in weight_copies(0):
+        copy.start()
+    pltpu.make_async_copy(x_first, x_ref, x_sem).wait()
+    rows = x_ref[...].astype(jnp.float32)
+    xn1_ref[...] = (rows * rms_scale(rows) * gain_one_ref[...]).astype(jnp.bfloat16)
+    h1_ref[...] = rows
+
+    def one(half, carry):
+        for copy in weight_copies(half):
+            copy.wait()
+
+        @pl.when(half + 1 < parts)
+        def _():
+            for copy in weight_copies(half + 1):
+                copy.start()
+
+        turned, attended = attend_part(
+            group,
+            xn1_ref[...],
+            wqkv_ref[half],
+            (cos_ref[...], sin_ref[...]),
+            allowed_pairs(seg_col_ref[...], seg_row_ref[...]),
+        )
+        qkv_ref[half] = turned
+        att_ref[half] = attended
+        h1_ref[...] += dot(attended, wo_ref[half])
+        return carry
+
+    lax.fori_loop(0, parts, one, 0)
+    middle = h1_ref[...]
+    xn2_ref[...] = (middle * rms_scale(middle) * gain_two_ref[...]).astype(jnp.bfloat16)
+
+
+def attn_forward(first, second, seg, gains, wqkv, wo, tables, group):
+    length, width = first.shape
+    parts, _, qkv_width = wqkv.shape
+    att_width = wo.shape[1]
+    vmem = pl.BlockSpec(memory_space=pltpu.VMEM)
+    anywhere = pl.BlockSpec(memory_space=pl.ANY)
+    return pl.pallas_call(
+        functools.partial(attn_forward_kernel, group),
+        in_specs=[anywhere] * 2 + [vmem] + [anywhere] * 2 + [vmem] * 5,
+        out_specs=[vmem] * 5,
+        out_shape=[
+            jax.ShapeDtypeStruct((length, width), jnp.float32),
+            jax.ShapeDtypeStruct((length, width), jnp.bfloat16),
+            jax.ShapeDtypeStruct((parts, length, qkv_width), jnp.bfloat16),
+            jax.ShapeDtypeStruct((parts, length, att_width), jnp.bfloat16),
+            jax.ShapeDtypeStruct((length, width), jnp.bfloat16),
+        ],
+        scratch_shapes=[
+            pltpu.VMEM((length, width), jnp.bfloat16),
+            pltpu.VMEM(wqkv.shape, wqkv.dtype),
+            pltpu.VMEM(wo.shape, wo.dtype),
+            pltpu.SemaphoreType.DMA,
+            pltpu.SemaphoreType.DMA((2, parts)),
+        ],
+        compiler_params=pltpu.CompilerParams(vmem_limit_bytes=62 * MIB),
+        cost_estimate=pl.CostEstimate(
+            flops=4 * 10**9, bytes_accessed=20 * 10**6, transcendentals=2 * 10**6
+        ),
+        name="attn_forward",
+    )(first, second, gains[0], wqkv, wo, *tables, seg[:, None], seg[None, :], gains[1])
+
+
+def attn_again_kernel(
+    group,
+    x_ref,
+    gain_ref,
+    wqkv_hbm,
+    cos_ref,
+    sin_ref,
+    seg_col_ref,
+    seg_row_ref,
+    xn1_ref,
+    qkv_ref,
+    att_ref,
+    wqkv_ref,
+    sem,
+):
+    @pl.when(lax.axis_index(SECTION) == 0)
+    def _():
+        parts = wqkv_ref.shape[0]
+
+        def copy(half):
+            return pltpu.make_async_copy(wqkv_hbm.at[half], wqkv_ref.at[half], sem.at[half])
+
+        for half in range(parts):
+            copy(half).start()
+        rows = x_ref[...].astype(jnp.float32)
+        xn1_ref[...] = (rows * rms_scale(rows) * gain_ref[...]).astype(jnp.bfloat16)
+
+        def one(half, carry):
+            copy(half).wait()
+            qkv_ref[half], att_ref[half] = attend_part(
+                group,
+                xn1_ref[...],
+                wqkv_ref[half],
+                (cos_ref[...], sin_ref[...]),
+                allowed_pairs(seg_col_ref[...], seg_row_ref[...]),
+            )
+            return carry
+
+        lax.fori_loop(0, parts, one, 0)
+
+
+def attn_again(layer_in, seg, gain, wqkv, tables, group):
+    length, width = layer_in.shape
+    parts, _, qkv_width = wqkv.shape
+    vmem = pl.BlockSpec(memory_space=pltpu.VMEM)
+    return pl.pallas_call(
+        functools.partial(attn_again_kernel, group),
+        in_specs=[vmem] * 2 + [pl.BlockSpec(memory_space=pl.ANY)] + [vmem] * 4,
+        out_specs=[vmem] * 3,
+        out_shape=[
+            jax.ShapeDtypeStruct((length, width), jnp.bfloat16),
+            jax.ShapeDtypeStruct((parts, length, qkv_width), jnp.bfloat16),
+            jax.ShapeDtypeStruct((parts, length, width // parts), jnp.bfloat16),
+        ],
+        scratch_shapes=[
+            pltpu.VMEM(wqkv.shape, wqkv.dtype),
+            pltpu.SemaphoreType.DMA((parts,)),
+        ],
+        compiler_params=pltpu.CompilerParams(vmem_limit_bytes=62 * MIB),
+        cost_estimate=pl.CostEstimate(
+            flops=3 * 10**9, bytes_accessed=12 * 10**6, transcendentals=2 * 10**6
+        ),
+        name="attn_again",
+    )(layer_in, gain, wqkv, tables[0], tables[1], seg[:, None], seg[None, :])
+
+
+def attn_split_kernel(
+    group,
+    x_ref,
+    gain_one_ref,
+    wqkv_ref,
+    wo_ref,
+    cos_ref,
+    sin_ref,
+    seg_col_ref,
+    seg_row_ref,
+    gain_two_ref,
+    h1_ref,
+    xn2_ref,
+    part,
+    arrived,
+    send_sem,
+    recv_sem,
+):
+    x = lax.axis_index(TENSOR)
+    aside = {TENSOR: 1 - x}
+
+    @pl.when(lax.axis_index(SECTION) == 0)
+    def _():
+        barrier = pltpu.get_barrier_semaphore()
+        pl.semaphore_signal(barrier, inc=1, device_id=aside, device_id_type=pl.DeviceIdType.MESH)
+
+        def one(i, carry):
+            at = jnp.where(i == 0, 1 - x, x)
+            rows = x_ref[at].astype(jnp.float32)
+            normed = (rows * rms_scale(rows) * gain_one_ref[...]).astype(jnp.bfloat16)
+            _, attended = attend_part(
+                group,
+                normed,
+                wqkv_ref[...],
+                (cos_ref[...], sin_ref[...]),
+                allowed_pairs(seg_col_ref[at], seg_row_ref[at]),
+            )
+            branch = dot(attended, wo_ref[...])
+
+            @pl.when(i == 0)
+            def _():
+                part[...] = branch.astype(jnp.bfloat16)
+                pl.semaphore_wait(barrier, 1)
+                copy().start()
+
+            @pl.when(i == 1)
+            def _():
+                h1_ref[...] = rows + branch
+
+            return carry
+
+        def copy():
+            return pltpu.make_async_remote_copy(
+                src_ref=part,
+                dst_ref=arrived,
+                send_sem=send_sem,
+                recv_sem=recv_sem,
+                device_id=aside,
+                device_id_type=pl.DeviceIdType.MESH,
+            )
+
+        lax.fori_loop(0, 2, one, 0)
+        copy().wait()
+        middle = h1_ref[...] + arrived[...].astype(jnp.float32)
+        h1_ref[...] = middle
+        xn2_ref[...] = (middle * rms_scale(middle) * gain_two_ref[...]).astype(jnp.bfloat16)
+
+
+def attn_split(rows, seg, gains, wqkv, wo, tables, group):
+    _, length, width = rows.shape
+    vmem = pl.BlockSpec(memory_space=pltpu.VMEM)
+    return pl.pallas_call(
+        functools.partial(attn_split_kernel, group),
+        in_specs=[vmem] * 9,
+        out_specs=[vmem] * 2,
+        out_shape=[
+            jax.ShapeDtypeStruct((length, width), jnp.float32),
+            jax.ShapeDtypeStruct((length, width), jnp.bfloat16),
+        ],
+        scratch_shapes=[
+            pltpu.VMEM((length, width), jnp.bfloat16),
+            pltpu.VMEM((length, width), jnp.bfloat16),
+            pltpu.SemaphoreType.DMA,
+            pltpu.SemaphoreType.DMA,
+        ],
+        compiler_params=pltpu.CompilerParams(
+            collective_id=8, has_side_effects=True, vmem_limit_bytes=48 * MIB
+        ),
+        cost_estimate=pl.CostEstimate(
+            flops=4 * 10**9, bytes_accessed=20 * 10**6, transcendentals=2 * 10**6
+        ),
+        name="attn_split",
+    )(
+        rows,
+        gains[0],
+        wqkv,
+        wo,
+        tables[0],
+        tables[1],
+        seg[:, :, None],
+        seg[:, None, :],
+        gains[1],
+    )
+
+
+def both_halves_kernel(
+    chunks,
+    wqkv,
+    wo,
+    after,
+    wqkv_before,
+    wo_before,
+    wqkv_all,
+    wo_all,
+    wqkv_held,
+    wo_held,
+    own_sem,
+    out_sem,
+    x_send,
+    x_recv,
+    core_send,
+    core_recv,
+):
+    del after, wqkv_before, wo_before
+    x = lax.axis_index(TENSOR)
+    core = lax.axis_index(DP)
+    aside, partner = {TENSOR: 1 - x}, {DP: 1 - core}
+    pairs = ((wqkv, wqkv_held, wqkv_all), (wo, wo_held, wo_all))
+
+    def span(i, of_core, chunk):
+        rows = pairs[i][0].shape[0] // (2 * chunks)
+        return pl.ds((of_core * chunks + chunk) * rows, rows)
+
+    def own_copy(i, of_core, chunk):
+        shard, held, _ = pairs[i]
+        at = span(i, of_core, chunk)
+        return pltpu.make_async_copy(shard.at[at], held.at[x, at], own_sem.at[i, of_core, chunk])
+
+    def out_copy(i, half):
+        _, held, out = pairs[i]
+        return pltpu.make_async_copy(held.at[half], out.at[half], out_sem.at[i, half])
+
+    def x_copy(i, chunk, half):
+        _, held, _ = pairs[i]
+        at = held.at[half, span(i, core, chunk)]
+        return pltpu.make_async_remote_copy(
+            src_ref=at,
+            dst_ref=at,
+            send_sem=x_send.at[i, chunk],
+            recv_sem=x_recv.at[i, chunk],
+            device_id=aside,
+            device_id_type=pl.DeviceIdType.MESH,
+        )
+
+    def core_copy(i, chunk, of_core):
+        _, held, _ = pairs[i]
+        at = held.at[1 - x, span(i, of_core, chunk)]
+        return pltpu.make_async_remote_copy(
+            src_ref=at,
+            dst_ref=at,
+            send_sem=core_send.at[i, chunk],
+            recv_sem=core_recv.at[i, chunk],
+            device_id=partner,
+            device_id_type=pl.DeviceIdType.MESH,
+        )
+
+    steps = [(i, chunk) for i in range(2) for chunk in range(chunks)]
+
+    @pl.when(lax.axis_index(SECTION) == 0)
+    def _():
+        for of_core in (core, 1 - core):
+            for i, chunk in steps:
+                own_copy(i, of_core, chunk).start()
+        barrier = pltpu.get_barrier_semaphore()
+        for other in (aside, partner):
+            pl.semaphore_signal(barrier, inc=1, device_id=other, device_id_type=pl.DeviceIdType.MESH)
+        pl.semaphore_wait(barrier, 2)
+        for i, chunk in steps:
+            own_copy(i, core, chunk).wait()
+            x_copy(i, chunk, x).start()
+        for i, chunk in steps:
+            own_copy(i, 1 - core, chunk).wait()
+        for i in range(2):
+            out_copy(i, x).start()
+        for i, chunk in steps:
+            x_copy(i, chunk, 1 - x).wait_recv()
+            core_copy(i, chunk, core).start()
+        for i in range(2):
+            for chunk in range(chunks):
+                core_copy(i, chunk, 1 - core).wait_recv()
+            out_copy(i, 1 - x).start()
+        for i, chunk in steps:
+            x_copy(i, chunk, x).wait_send()
+            core_copy(i, chunk, core).wait_send()
+        for i in range(2):
+            for half in range(2):
+                out_copy(i, half).wait()
+
+
+def both_halves(wqkv, wo, after, before, chunks=4):
+    anywhere = pl.BlockSpec(memory_space=pl.ANY)
+    dma = pltpu.SemaphoreType.DMA
+    return pl.pallas_call(
+        functools.partial(both_halves_kernel, chunks),
+        in_specs=[anywhere] * 5,
+        out_specs=[anywhere] * 2,
+        input_output_aliases={3: 0, 4: 1},
+        out_shape=[
+            jax.ShapeDtypeStruct((2,) + wqkv.shape, wqkv.dtype),
+            jax.ShapeDtypeStruct((2,) + wo.shape, wo.dtype),
+        ],
+        scratch_shapes=[
+            pltpu.VMEM((2,) + wqkv.shape, wqkv.dtype),
+            pltpu.VMEM((2,) + wo.shape, wo.dtype),
+            dma((2, 2, chunks)),
+            dma((2, 2)),
+        ]
+        + [dma((2, chunks))] * 4,
+        compiler_params=pltpu.CompilerParams(
+            collective_id=9, has_side_effects=True, vmem_limit_bytes=62 * MIB
+        ),
+        cost_estimate=pl.CostEstimate(flops=0, bytes_accessed=30 * 10**6, transcendentals=0),
+        name="both_halves",
+    )(wqkv, wo, after, *before)
+
+
+def attn_backward_kernel(group, *refs):
+    pairs = [refs[2 * i : 2 * i + 2] for i in range(6)]
+    (
+        wqkv_hbm,
+        wo_hbm,
+        rows_ref,
+        grad_gates_ref,
+        router_ref,
+        gain_one_ref,
+        gain_two_ref,
+        cos_ref,
+        sin_ref,
+        seg_col_ref,
+        seg_row_ref,
+        grad_in_ref,
+        mid_ref,
+        dqkv_ref,
+        small_ref,
+        x_ref,
+        h1_ref,
+        xn2_ref,
+        gates_ref,
+        qkv_ref,
+        top_ref,
+        wqkv_ref,
+        wo_ref,
+        middle_acc,
+        normed_acc,
+        taken_sem,
+        weight_sem,
+    ) = refs[12:]
+    taken = (x_ref, h1_ref, xn2_ref, gates_ref, qkv_ref, top_ref)
+    experts = grad_gates_ref.shape[0]
+    parts = wqkv_ref.shape[0]
+
+    def weight_copies(half):
+        return [
+            pltpu.make_async_copy(hbm.at[half], ref.at[half], weight_sem.at[i, half])
+            for i, (hbm, ref) in enumerate(((wqkv_hbm, wqkv_ref), (wo_hbm, wo_ref)))
+        ]
+
+    for i in (3, 2, 1, 5, 4, 0):
+        start_of_section(*pairs[i], taken[i], taken_sem.at[i])
+
+    def arrived(i):
+        pltpu.make_async_copy(pairs[i][0], taken[i], taken_sem.at[i]).wait()
+        return taken[i]
+
+    gates = arrived(3)[...]
+    grad_gates = grad_gates_ref[...]
+    chosen = gates * (grad_gates - jnp.sum(gates * grad_gates, axis=0, keepdims=True))
+    logits = chosen.astype(jnp.bfloat16)
+    small_ref[0:experts, :] = dot(logits, arrived(2)[...])
+    for copy in weight_copies(0):
+        copy.start()
+    grad_normed = dot(logits, router_ref[...], TN) + rows_ref[...].astype(jnp.float32)
+    middle = arrived(1)[...]
+    grad_middle, gain_grad = norm_back(grad_normed, middle, rms_scale(middle), gain_two_ref[...])
+    small_ref[experts : experts + 1, :] = gain_grad[None, :]
+    grad_middle = grad_middle + arrived(5)[...].astype(jnp.float32)
+    middle_acc[...] = grad_middle
+    mid_ref[...] = grad_middle.astype(jnp.bfloat16)
+    normed_acc[...] = jnp.zeros_like(normed_acc)
+    arrived(4)
+
+    def one(half, carry):
+        for copy in weight_copies(half):
+            copy.wait()
+
+        @pl.when(half + 1 < parts)
+        def _():
+            for copy in weight_copies(half + 1):
+                copy.start()
+
+        attn_backward_part(
+            group,
+            half,
+            mid_ref,
+            wqkv_ref,
+            wo_ref,
+            (cos_ref[...], -sin_ref[...]),
+            (seg_col_ref[...], seg_row_ref[...]),
+            qkv_ref,
+            dqkv_ref,
+            normed_acc,
+        )
+        return carry
+
+    lax.fori_loop(0, parts, one, 0)
+    rows = arrived(0)[...].astype(jnp.float32)
+    grad_rows, gain_grad = norm_back(normed_acc[...], rows, rms_scale(rows), gain_one_ref[...])
+    grad_in_ref[...] = (grad_rows + middle_acc[...]).astype(jnp.bfloat16)
+    small_ref[experts + 1 : experts + 2, :] = gain_grad[None, :]
+    small_ref[experts + 2 :, :] = jnp.zeros_like(small_ref[experts + 2 :, :])
+
+
+def attn_backward_part(
+    group, part, mid_ref, wqkv_ref, wo_ref, tables, segs, qkv_ref, dqkv_ref, normed_acc
+):
+    length = mid_ref.shape[0]
+    width = wqkv_ref.shape[2]
+    query_width = width * group // (group + 2)
+    key_width = (width - query_width) // 2
+    cosine, sine = tables
+    seg_col, seg_row = segs
+    grad_att = dot(mid_ref[...], wo_ref[part], NT).astype(jnp.bfloat16).astype(jnp.float32)
+    grad_out = slabs_of(grad_att, 0, query_width // (2 * HD))
+    kept = qkv_ref[part]
+    query = [slab.astype(jnp.float32) for slab in slabs_of(kept, 0, query_width // (2 * HD))]
+    key = slabs_of(kept, query_width, key_width // (2 * HD))
+    value = slabs_of(kept, query_width + key_width, key_width // (2 * HD))
+    key_at = lax.broadcasted_iota(jnp.int32, (length, length), 0)
+    query_at = lax.broadcasted_iota(jnp.int32, (length, length), 1)
+    allowed = (query_at >= key_at) & (seg_col == seg_row)
+    grad_query = [None] * len(query)
+    grad_key = [None] * len(key)
+    grad_value = [None] * len(value)
+    for kv_head in range(key_width // HD):
+        side = kv_head % 2
+        slab_at = kv_head // 2
+        key_slab = key[slab_at]
+        key_side = one_side(key_slab, side)
+        value_slab = value[slab_at]
+        for head in range(group * kv_head, group * (kv_head + 1)):
+            query_head = aligned_head(query, head, side, HD**-0.5)
+            out_head = aligned_head(grad_out, head, side, 1.0)
+            scores = dot(key_slab, query_head, NT)
+            scores = jnp.where(allowed, scores, NEG_BIG)
+            exponent = jnp.exp(scores - jnp.max(scores, axis=0, keepdims=True))
+            probability = exponent / jnp.sum(exponent, axis=0, keepdims=True)
+            grad_prob = dot(value_slab, out_head, NT)
+            value_part = dot(probability.astype(jnp.bfloat16), out_head)
+            centre = jnp.sum(probability * grad_prob, axis=0, keepdims=True)
+            grad_scores = (probability * (grad_prob - centre)).astype(jnp.bfloat16)
+            key_part = dot(grad_scores, query_head)
+            query_part = dot(grad_scores, key_side, TN) * HD**-0.5
+            if head % 2 != side:
+                query_part = pltpu.roll(query_part, HD, 1)
+            at = head // 2
+            grad_query[at] = query_part if head % 2 == 0 else grad_query[at] + query_part
+            first = head == 2 * group * slab_at
+            grad_key[slab_at] = key_part if first else grad_key[slab_at] + key_part
+            grad_value[slab_at] = value_part if first else grad_value[slab_at] + value_part
+    turned = [turn_pair(slab, cosine, sine).astype(jnp.bfloat16) for slab in grad_query + grad_key]
+    dqkv = jnp.concatenate(turned + [slab.astype(jnp.bfloat16) for slab in grad_value], axis=1)
+    dqkv_ref[part] = dqkv
+    normed_acc[...] += dot(dqkv, wqkv_ref[part], NT)
+
+
+def attn_backward(kept, rows, grad_gates, seg, gains, router, wqkv, wo, tables, group):
+    length, width = rows.shape
+    parts, _, qkv_width = wqkv.shape
+    experts = router.shape[0]
+    vmem = pl.BlockSpec(memory_space=pltpu.VMEM)
+    anywhere = pl.BlockSpec(memory_space=pl.ANY)
+    dma = pltpu.SemaphoreType.DMA
+    return pl.pallas_call(
+        functools.partial(attn_backward_kernel, group),
+        in_specs=[anywhere] * 14 + [vmem] * 9,
+        out_specs=[vmem] * 4,
+        out_shape=[
+            jax.ShapeDtypeStruct((length, width), jnp.bfloat16),
+            jax.ShapeDtypeStruct((length, width), jnp.bfloat16),
+            jax.ShapeDtypeStruct((parts, length, qkv_width), jnp.bfloat16),
+            jax.ShapeDtypeStruct((experts + 8, width), jnp.float32),
+        ],
+        scratch_shapes=[pltpu.VMEM(one.shape, one.dtype) for one, _ in kept]
+        + [
+            pltpu.VMEM(wqkv.shape, wqkv.dtype),
+            pltpu.VMEM(wo.shape, wo.dtype),
+            pltpu.VMEM((length, width), jnp.float32),
+            pltpu.VMEM((length, width), jnp.float32),
+            dma((len(kept),)),
+            dma((2, parts)),
+        ],
+        compiler_params=pltpu.CompilerParams(vmem_limit_bytes=62 * MIB),
+        cost_estimate=pl.CostEstimate(
+            flops=8 * 10**9, bytes_accessed=20 * 10**6, transcendentals=2 * 10**6
+        ),
+        name="attn_backward",
+    )(
+        *[one for pair in kept for one in pair],
+        wqkv,
+        wo,
+        rows,
+        grad_gates,
+        router,
+        gains[0],
+        gains[1],
+        tables[0],
+        tables[1],
+        seg[:, None],
+        seg[None, :],
+    )
+
+
+def attn_weights_kernel(*refs):
+    groups, out_ref = [refs[3 * i : 3 * i + 3] for i in range(4)], refs[12]
+    width = out_ref.shape[1]
+
+    def kept(group):
+        one, both, three = group
+        return jnp.concatenate([of_section(one, three), both[...]], axis=-2)
+
+    def found(group):
+        one, both, three = group
+        return jnp.concatenate([both[...], of_section(three, one)], axis=-2)
+
+    xn1, att = kept(groups[0]), kept(groups[1])[0]
+    mid, dqkv = found(groups[2]), found(groups[3])[0]
+    qkv_width = dqkv.shape[1]
+    out_ref[0, :, :qkv_width] = dot(xn1, dqkv, TN).astype(jnp.bfloat16)
+    half = width // 2
+    for i in range(2):
+        out_ref[0, i * half : (i + 1) * half, qkv_width:] = dot(
+            att, mid[:, i * half : (i + 1) * half], TN
+        ).astype(jnp.bfloat16)
+
+
+def attn_weights(xn1, att, mid, dqkv):
+    rows, width = xn1[0].shape
+    parts, _, att_width = att[0].shape
+    qkv_width = dqkv[0].shape[2]
+
+    def whole(*shape):
+        return pl.BlockSpec(shape, lambda i: (0,) * len(shape))
+
+    def part(*shape):
+        return pl.BlockSpec((1,) + shape, lambda i: (i, 0, 0))
+
+    return pl.pallas_call(
+        attn_weights_kernel,
+        grid=(parts,),
+        in_specs=[whole(rows, width)] * 3
+        + [part(rows, att_width)] * 3
+        + [whole(rows, width)] * 3
+        + [part(rows, qkv_width)] * 3,
+        out_specs=part(width, qkv_width + width // 2),
+        out_shape=jax.ShapeDtypeStruct((parts, width, qkv_width + width // 2), jnp.bfloat16),
+        compiler_params=pltpu.CompilerParams(vmem_limit_bytes=56 * MIB),
+        cost_estimate=pl.CostEstimate(
+            flops=7 * 10**9, bytes_accessed=20 * 10**6, transcendentals=0
+        ),
+        name="attn_weights",
+    )(*xn1, *att, *mid, *dqkv)
+
+
+def looked_up(place, values):
+    found = values[0]
+    for i, value in enumerate(values[1:]):
+        found = jnp.where(place == i + 1, value, found)
+    return found
+
+
+def nearest_first(place, reach):
+    table = []
+    for at in range(reach):
+        table.append(sorted(range(reach), key=lambda other: (abs(other - at), other)))
+    return [looked_up(place, [table[at][k] for at in range(reach)]) for k in range(reach)]
+
+
+MESH_ID = pl.DeviceIdType.MESH
+
+
+class Chain:
+    def __init__(self, reach):
+        self.reach = reach
+        self.z = lax.axis_index(EXPERT)
+        self.x = lax.axis_index(TENSOR)
+        self.me = 2 * self.z + self.x
+        self.aside = {TENSOR: 1 - self.x}
+        self.above = {EXPERT: self.z + 1}
+        self.below = {EXPERT: self.z - 1}
+        self.has_above = self.z < reach - 1
+        self.has_below = self.z > 0
+        self.order = nearest_first(self.z, reach)
+
+    def near(self, k):
+        return self.order[k] if isinstance(k, int) else looked_up(k, self.order)
+
+    def greet_group(self, partner=None):
+        barrier = pltpu.get_barrier_semaphore()
+        if partner is not None:
+            pl.semaphore_signal(barrier, inc=1, device_id=partner, device_id_type=MESH_ID)
+        for other in range(2 * self.reach):
+
+            @pl.when(other != self.me)
+            def _():
+                pl.semaphore_signal(
+                    barrier,
+                    inc=1,
+                    device_id={EXPERT: other // 2, TENSOR: other % 2},
+                    device_id_type=MESH_ID,
+                )
+
+        pl.semaphore_wait(barrier, 2 * self.reach - (1 if partner is None else 0))
+
+
+def is_end(chain, source):
+    return jnp.logical_or(source == 0, source == chain.reach - 1)
+
+
+class Gather:
+    def __init__(self, chain, blocks, send_sem, recv_sem, paired=False):
+        self.chain, self.blocks, self.send_sem, self.recv_sem = chain, blocks, send_sem, recv_sem
+        self.paired = paired
+
+    def copy(self, source, column, piece, way, target):
+        at = 2 * source + column
+        return pltpu.make_async_remote_copy(
+            src_ref=self.blocks.at[at, piece],
+            dst_ref=self.blocks.at[at, piece],
+            send_sem=self.send_sem.at[way, source, piece],
+            recv_sem=self.recv_sem.at[at, piece],
+            device_id=target,
+            device_id_type=MESH_ID,
+        )
+
+    def over_x(self, source, piece, act):
+        c = self.chain
+        crosses = jnp.logical_and(is_end(c, source), source != c.z)
+        if piece == 0:
+            act(self.copy(source, c.x, 0, 0, c.aside))
+        else:
+
+            @pl.when(jnp.logical_not(crosses))
+            def _():
+                act(self.copy(source, c.x, piece, 0, c.aside))
+
+    def each_way(self, source, piece, up, down, act):
+        c = self.chain
+        if up:
+
+            @pl.when(c.has_above)
+            def _():
+                act(self.copy(source, c.x, piece, 1, c.above))
+
+        if down:
+
+            @pl.when(c.has_below)
+            def _():
+                act(self.copy(source, c.x, piece, 2, c.below))
+
+        if not (self.paired and up and down):
+            self.over_x(source, piece, act)
+
+    def start(self):
+        for piece in range(PIECES):
+            self.each_way(self.chain.z, piece, True, True, lambda copy: copy.start())
+        if self.paired:
+            self.cross_out()
+
+    def relay(self, distance):
+        c = self.chain
+        for piece in range(PIECES):
+
+            @pl.when(c.z - distance >= 0)
+            def _():
+                self.copy(c.z - distance, c.x, piece, 1, c.below).wait_recv()
+                self.each_way(c.z - distance, piece, True, False, lambda copy: copy.start())
+
+            @pl.when(c.z + distance <= c.reach - 1)
+            def _():
+                self.copy(c.z + distance, c.x, piece, 2, c.above).wait_recv()
+                self.each_way(c.z + distance, piece, False, True, lambda copy: copy.start())
+
+    def cross_copy(self, end):
+        c = self.chain
+        return self.copy(end, 1 - c.x, PIECES - 1, 3, c.below if end else c.above)
+
+    def cross_out(self):
+        c = self.chain
+        for end in (0, c.reach - 1):
+
+            @pl.when(c.z == end)
+            def _():
+                self.cross_copy(end).start()
+
+    def cross_relay(self, distance):
+        c = self.chain
+        for end in (0, c.reach - 1):
+            last = c.reach - 1 - end
+
+            @pl.when(jnp.where(c.z > end, c.z - end, end - c.z) == distance)
+            def _():
+                self.cross_copy(end).wait_recv()
+
+                @pl.when(c.z != last)
+                def _():
+                    self.cross_copy(end).start()
+
+    def wait_aside(self, source):
+        c = self.chain
+        self.copy(source, 1 - c.x, 0, 0, c.aside).wait_recv()
+
+        @pl.when(jnp.logical_not(jnp.logical_and(is_end(c, source), source != c.z)))
+        def _():
+            self.copy(source, 1 - c.x, PIECES - 1, 0, c.aside).wait_recv()
+
+    def drain(self):
+        c = self.chain
+        for piece in range(PIECES):
+            self.each_way(c.z, piece, True, True, lambda copy: copy.wait_send())
+            for distance in range(1, c.reach):
+
+                @pl.when(c.z - distance >= 0)
+                def _():
+                    self.each_way(
+                        c.z - distance, piece, True, False, lambda copy: copy.wait_send()
+                    )
+
+                @pl.when(c.z + distance <= c.reach - 1)
+                def _():
+                    self.each_way(
+                        c.z + distance, piece, False, True, lambda copy: copy.wait_send()
+                    )
+
+        for end in (0, c.reach - 1):
+
+            @pl.when(c.z != c.reach - 1 - end)
+            def _():
+                self.cross_copy(end).wait_send()
+
+
+PIECES = 2
+TAIL_PIECES = 4
+
+
+class Reduce:
+    def __init__(self, chain, part_at, from_x, from_z, sems, pieces=PIECES, cross=None):
+        self.chain, self.part_at, self.from_x, self.from_z = chain, part_at, from_x, from_z
+        self.pieces = pieces
+        self.cross = cross
+        self.x_send, self.x_recv, self.z_send, self.z_recv = sems
+
+    def part_copy(self, home, piece):
+        c = self.chain
+        return pltpu.make_async_remote_copy(
+            src_ref=self.part_at(home, 1 - c.x, piece),
+            dst_ref=self.from_x.at[home, piece],
+            send_sem=self.x_send.at[home, piece],
+            recv_sem=self.x_recv.at[home, piece],
+            device_id=c.aside,
+            device_id_type=MESH_ID,
+        )
+
+    def sum_copy(self, home, piece, slot, target):
+        return pltpu.make_async_remote_copy(
+            src_ref=self.part_at(home, self.chain.x, piece),
+            dst_ref=self.from_z.at[slot, piece],
+            send_sem=self.z_send.at[home, piece],
+            recv_sem=self.z_recv.at[slot, piece],
+            device_id=target,
+            device_id_type=MESH_ID,
+        )
+
+    def over_x(self, home, piece, act):
+        c = self.chain
+        if self.cross is None:
+            act()
+        else:
+            crosses = jnp.logical_and(is_end(c, home), home != c.z)
+
+            @pl.when(jnp.logical_not(jnp.logical_and(crosses, piece == self.pieces - 1)))
+            def _():
+                act()
+
+    def start(self, k, piece):
+        home = self.chain.near(k)
+        self.over_x(home, piece, lambda: self.part_copy(home, piece).start())
+
+    def arrive(self, k, piece):
+        home = self.chain.near(k)
+        self.over_x(home, piece, lambda: self.part_copy(home, piece).wait_recv())
+
+    def own(self, home, piece):
+        c = self.chain
+        mine = self.part_at(home, c.x, piece)[...].astype(jnp.float32)
+        came = self.from_x[home, piece].astype(jnp.float32)
+        if self.cross is not None:
+            crosses = jnp.logical_and(is_end(c, home), home != c.z)
+            came = jnp.where(jnp.logical_and(crosses, piece == self.pieces - 1), 0.0, came)
+        return mine + came
+
+    def cross_copy(self, end):
+        c = self.chain
+        from_cross, send_sem, recv_sem = self.cross
+        at = 1 if end else 0
+        return pltpu.make_async_remote_copy(
+            src_ref=self.part_at(end, 1 - c.x, self.pieces - 1),
+            dst_ref=from_cross.at[at],
+            send_sem=send_sem.at[at],
+            recv_sem=recv_sem.at[at],
+            device_id=c.above if end else c.below,
+            device_id_type=MESH_ID,
+        )
+
+    def cross_step(self, distance):
+        c = self.chain
+        for end in (0, c.reach - 1):
+
+            @pl.when(jnp.where(c.z > end, c.z - end, end - c.z) == distance)
+            def _():
+                @pl.when(c.z != c.reach - 1 - end)
+                def _():
+                    self.cross_copy(end).wait_recv()
+                    mine = self.part_at(end, 1 - c.x, self.pieces - 1)
+                    mine[...] = (
+                        mine[...].astype(jnp.float32)
+                        + self.cross[0][1 if end else 0].astype(jnp.float32)
+                    ).astype(mine.dtype)
+
+                @pl.when(c.z != end)
+                def _():
+                    self.cross_copy(end).start()
+
+    def pass_on(self, k, piece):
+        c = self.chain
+        home = c.near(k)
+        up = home > c.z
+        comes = jnp.logical_or(
+            jnp.logical_and(up, c.has_below), jnp.logical_and(home < c.z, c.has_above)
+        )
+        mine = self.part_at(home, c.x, piece)
+
+        @pl.when(comes)
+        def _():
+            self.sum_copy(home, piece, home, c.above).wait_recv()
+            mine[...] = (
+                self.own(home, piece) + self.from_z[home, piece].astype(jnp.float32)
+            ).astype(mine.dtype)
+
+        @pl.when(jnp.logical_not(comes))
+        def _():
+            mine[...] = self.own(home, piece).astype(mine.dtype)
+
+        @pl.when(up)
+        def _():
+            self.sum_copy(home, piece, home, c.above).start()
+
+        @pl.when(home < c.z)
+        def _():
+            slot = jnp.where(home == c.z - 1, c.reach, home)
+            self.sum_copy(home, piece, slot, c.below).start()
+
+    def finish(self, piece, act):
+        c = self.chain
+        home = c.z
+
+        @pl.when(c.has_below)
+        def _():
+            self.sum_copy(home, piece, home, c.below).wait_recv()
+
+        @pl.when(c.has_above)
+        def _():
+            self.sum_copy(home, piece, c.reach, c.above).wait_recv()
+
+        @pl.when(c.has_below & c.has_above)
+        def _():
+            act(
+                piece,
+                self.own(home, piece)
+                + self.from_z[home, piece].astype(jnp.float32)
+                + self.from_z[c.reach, piece].astype(jnp.float32),
+            )
+
+        @pl.when(jnp.logical_not(c.has_above))
+        def _():
+            act(piece, self.own(home, piece) + self.from_z[home, piece].astype(jnp.float32))
+
+        @pl.when(jnp.logical_not(c.has_below))
+        def _():
+            act(piece, self.own(home, piece) + self.from_z[c.reach, piece].astype(jnp.float32))
+
+    def drain(self):
+        c = self.chain
+
+        def one(home, carry):
+            for piece in range(self.pieces):
+                self.over_x(home, piece, lambda: self.part_copy(home, piece).wait_send())
+
+                @pl.when(home != c.z)
+                def _():
+                    self.sum_copy(home, piece, home, c.above).wait_send()
+
+            return carry
+
+        lax.fori_loop(0, c.reach, one, 0)
+        if self.cross is not None:
+            for end in (0, c.reach - 1):
+
+                @pl.when(c.z != end)
+                def _():
+                    self.cross_copy(end).wait_send()
+
+
+def masked_softmax(logits, kept):
+    top = jnp.max(jnp.where(kept, logits, NEG_BIG), axis=0, keepdims=True)
+    exponent = jnp.where(kept, jnp.exp(jnp.where(kept, logits - top, 0.0)), 0.0)
+    return exponent / jnp.sum(exponent, axis=0, keepdims=True)
+
+
+def slot_gates(picks, gate_row):
+    return jnp.sum(picks.astype(jnp.float32) * gate_row, axis=1, keepdims=True)
+
+
+def one_hot_slots(slot_row, cap):
+    length = slot_row.shape[1]
+    at = lax.broadcasted_iota(jnp.int32, (cap, length), 0).astype(jnp.float32)
+    return jnp.where(at == slot_row, 1.0, 0.0).astype(jnp.bfloat16)
+
+
+def finish_pieces(summed, act):
+    def one(piece, carry):
+        summed.arrive(0, piece)
+        summed.finish(piece, act)
+        return carry
+
+    lax.fori_loop(0, PIECES, one, 0)
+
+
+def reduced_in_order(reach, summed, act):
+    count = PIECES * (reach - 1)
+    ahead = 3
+
+    def place(i):
+        return reach - 1 - i // PIECES, i % PIECES
+
+    summed.cross_step(reach - 1)
+    for i in range(ahead):
+        summed.start(*place(i))
+
+    def step(i, carry):
+        summed.arrive(*place(i))
+
+        @pl.when(i + ahead < count)
+        def _():
+            summed.start(*place(i + ahead))
+
+        summed.pass_on(*place(i))
+
+        @pl.when(jnp.logical_and(i % PIECES == 1, i < count - 1))
+        def _():
+            summed.cross_step(reach - 2 - i // PIECES)
+
+        return carry
+
+    lax.fori_loop(0, count, step, 0)
+    summed.cross_step(0)
+    summed.start(0, PIECES - 1)
+    finish_pieces(summed, act)
+
+
+def gathered_steps(reach, chain, rows, summed, compute):
+    rows.start()
+
+    def step(k, carry):
+        @pl.when(k + 1 < reach)
+        def _():
+            rows.relay(k + 1)
+
+        source = chain.near(k)
+        rows.wait_aside(source)
+
+        @pl.when(k == 0)
+        def _():
+            rows.cross_out()
+
+        @pl.when(k > 0)
+        def _():
+            rows.cross_relay(k)
+
+        @pl.when(k + 1 == reach)
+        def _():
+            summed.start(0, 0)
+
+        compute(k, source)
+        return carry
+
+    lax.fori_loop(0, reach, step, 0)
+
+
+def whole_rows(block):
+    return block.reshape(-1, block.shape[-1])
+
+
+def moe_forward_kernel(
+    reach,
+    tick,
+    last,
+    own_ref,
+    h1_ref,
+    ids_ref,
+    router_ref,
+    wg_hbm,
+    wu_hbm,
+    wd_hbm,
+    *refs,
+):
+    refs = list(refs)
+    if tick == 0:
+        tops_ref, *shards = refs[:3]
+        refs = refs[3:]
+    out_ref, gates_ref, slots_ref, own_gates_ref, picked_hbm, g_hbm, u_hbm = refs[:7]
+    refs = refs[7:]
+    if tick == 0:
+        tops_hbm, *halves = refs[:3]
+        refs = refs[3:]
+    (
+        blocks,
+        parts,
+        from_x,
+        from_z,
+        from_cross,
+        wg_ref,
+        wu_ref,
+        wd_ref,
+        rows_in,
+        rows_out,
+        g_slots,
+        u_slots,
+        picks_of,
+        ids_all,
+        gather_send,
+        gather_recv,
+        x_send,
+        x_recv,
+        z_send,
+        z_recv,
+        cross_send,
+        cross_recv,
+        weight_sem,
+        keep_sem,
+        id_send,
+        id_recv,
+    ) = refs[:26]
+    local = wg_ref.shape[0]
+    cap = rows_in.shape[2] // 2
+    experts = router_ref.shape[0]
+    length = own_ref.shape[0]
+    section = lax.axis_index(SECTION)
+    chain = Chain(reach)
+
+    def weight_copies():
+        return [
+            pltpu.make_async_copy(hbm, vmem, weight_sem.at[i])
+            for i, (hbm, vmem) in enumerate(
+                ((wg_hbm, wg_ref), (wu_hbm, wu_ref), (wd_hbm, wd_ref))
+            )
+        ]
+
+    def keep_copies(k):
+        source = chain.near(k)
+        slot = k % 2 if isinstance(k, int) else lax.rem(k, 2)
+        return [
+            pltpu.make_async_copy(rows_in.at[slot], picked_hbm.at[source], keep_sem.at[0, k]),
+            pltpu.make_async_copy(g_slots.at[slot], g_hbm.at[source], keep_sem.at[1, k]),
+            pltpu.make_async_copy(u_slots.at[slot], u_hbm.at[source], keep_sem.at[2, k]),
+        ]
+
+    def id_copy(target, at):
+        return pltpu.make_async_remote_copy(
+            src_ref=ids_ref,
+            dst_ref=ids_all.at[at],
+            send_sem=id_send.at[target],
+            recv_sem=id_recv.at[at],
+            device_id={EXPERT: target // 2, TENSOR: target % 2},
+            device_id_type=MESH_ID,
+        )
+
+    def compute(k, source):
+        slot = lax.rem(k, 2)
+
+        @pl.when(k == 0)
+        def _():
+            for copy in weight_copies():
+                copy.wait()
+
+        @pl.when(k >= 2)
+        def _():
+            for copy in keep_copies(k - 2):
+                copy.wait()
+
+        gate_of = {}
+        ahead = lax.broadcasted_iota(jnp.int32, (length, length), 0)
+        behind = lax.broadcasted_iota(jnp.int32, (length, length), 1)
+        before = jnp.where(ahead < behind, 1.0, 0.0).astype(jnp.bfloat16)
+        named = lax.rem(
+            lax.broadcasted_iota(jnp.int32, (experts, length), 0) + chain.me * local, experts
+        )
+        for i in range(2):
+            at = 2 * source + i
+
+            @pl.when(at != chain.me)
+            def _():
+                id_copy(at, at).wait_recv()
+
+            ids = ids_all[at]
+            member = ids[0:1, :] == named
+            for pick in range(1, TOPK):
+                member = jnp.logical_or(member, ids[pick : pick + 1, :] == named)
+            rows = whole_rows(blocks[at])
+            gates = masked_softmax(dot(router_ref[...], rows, NT), member)
+            gates_ref[at] = gates
+
+            @pl.when(at == chain.me)
+            def _():
+                own_gates_ref[...] = gates
+
+            mine = jnp.where(member[:8], 1.0, 0.0).astype(jnp.bfloat16)
+            taken = jnp.where(member[:8], dot(mine, before), -1.0)
+            slots_ref[at] = taken
+            for e in range(local):
+                picks = one_hot_slots(taken[e : e + 1, :], cap)
+                picks_of[i, e * cap : (e + 1) * cap, :] = picks
+                gate_of[i, e] = slot_gates(picks, gates[e : e + 1, :])
+            gathered = dot(picks_of[i], rows).astype(jnp.bfloat16)
+            for e in range(local):
+                rows_in[slot, e, i * cap : (i + 1) * cap, :] = gathered[e * cap : (e + 1) * cap, :]
+        for e in range(local):
+            rows = rows_in[slot, e]
+            gate_pre = dot(rows, wg_ref[e])
+            up_pre = dot(rows, wu_ref[e])
+            g_slots[slot, e] = gate_pre.astype(jnp.bfloat16)
+            u_slots[slot, e] = up_pre.astype(jnp.bfloat16)
+            hidden = (gate_pre * jax.nn.sigmoid(gate_pre) * up_pre).astype(jnp.bfloat16)
+            produced = dot(hidden, wd_ref[e])
+            for i in range(2):
+                rows_out[i, e * cap : (e + 1) * cap, :] = (
+                    produced[i * cap : (i + 1) * cap, :] * gate_of[i, e]
+                ).astype(jnp.bfloat16)
+        for i in range(2):
+            share = dot(picks_of[i], rows_out[i], TN).astype(jnp.bfloat16)
+            parts[2 * source + i] = share.reshape(parts.shape[1:])
+        for copy in keep_copies(k):
+            copy.start()
+
+    def finish(piece, total):
+        at = pl.ds(pl.multiple_of(piece * total.shape[0], total.shape[0]), total.shape[0])
+        out_ref[at, :] = (h1_ref[at, :] + total).astype(jnp.bfloat16)
+
+    def run():
+        for copy in weight_copies():
+            copy.start()
+        blocks[chain.me] = own_ref[...].reshape(blocks.shape[1:])
+        ids_all[chain.me] = ids_ref[...]
+        chain.greet_group()
+        for target in range(2 * reach):
+
+            @pl.when(target != chain.me)
+            def _():
+                id_copy(target, chain.me).start()
+
+        rows = Gather(chain, blocks, gather_send, gather_recv)
+        summed = Reduce(
+            chain,
+            lambda home, column, piece: parts.at[2 * home + column, piece],
+            from_x,
+            from_z,
+            (x_send, x_recv, z_send, z_recv),
+            cross=(from_cross, cross_send, cross_recv),
+        )
+        gathered_steps(reach, chain, rows, summed, compute)
+        reduced_in_order(reach, summed, finish)
+        rows.drain()
+        summed.drain()
+        for target in range(2 * reach):
+
+            @pl.when(target != chain.me)
+            def _():
+                id_copy(target, chain.me).wait_send()
+
+        for k in (reach - 2, reach - 1):
+            for copy in keep_copies(k):
+                copy.wait()
+
+    if tick == 0:
+        second_send, second_recv, tops_sem, *refs = refs[26:]
+        landed, (stage_sem, own_sem, half_sem, wx_send, wx_recv, core_send, core_recv) = (
+            refs[:2],
+            refs[2:],
+        )
+        core = lax.axis_index(DP)
+        partner = {DP: 1 - core}
+        chunks = local
+        pieces = [(i, chunk) for i in range(2) for chunk in range(chunks)]
+
+        def span(i, of_core, chunk):
+            rows = shards[i].shape[0] // (2 * chunks)
+            return pl.ds((of_core * chunks + chunk) * rows, rows)
+
+        def stage(i, chunk, mine):
+            rows, columns = shards[i].shape[0] // (2 * chunks), shards[i].shape[1]
+            if mine:
+                return rows_in.at[i, chunk, pl.ds(0, rows), pl.ds(0, columns)]
+            if i == 0:
+                return rows_out.at[chunk // 2, pl.ds(chunk % 2 * rows, rows), pl.ds(0, columns)]
+            return from_x.at[chunk, 0, pl.ds(0, rows)]
+
+        def stage_copy(i, chunk, mine):
+            at = span(i, core if mine else 1 - core, chunk)
+            return pltpu.make_async_copy(
+                shards[i].at[at], stage(i, chunk, mine), stage_sem.at[i, chunk, 1 - mine]
+            )
+
+        def own_copy(i, chunk, mine):
+            at = span(i, core if mine else 1 - core, chunk)
+            return pltpu.make_async_copy(
+                stage(i, chunk, mine), halves[i].at[chain.x, at], own_sem.at[i, chunk, 1 - mine]
+            )
+
+        def half_copy(i):
+            return pltpu.make_async_copy(landed[i], halves[i].at[1 - chain.x], half_sem.at[i])
+
+        def weight_x_copy(i, chunk):
+            return pltpu.make_async_remote_copy(
+                src_ref=stage(i, chunk, 1),
+                dst_ref=landed[i].at[span(i, core, chunk)],
+                send_sem=wx_send.at[i, chunk],
+                recv_sem=wx_recv.at[i, chunk],
+                device_id=chain.aside,
+                device_id_type=MESH_ID,
+            )
+
+        def weight_core_copy(i, chunk, of_core):
+            at = landed[i].at[span(i, of_core, chunk)]
+            return pltpu.make_async_remote_copy(
+                src_ref=at,
+                dst_ref=at,
+                send_sem=core_send.at[i, chunk],
+                recv_sem=core_recv.at[i, chunk],
+                device_id=partner,
+                device_id_type=MESH_ID,
+            )
+
+        @pl.when(section == 0)
+        def _():
+            run()
+
+        @pl.when(section != 0)
+        def _():
+            for mine in (1, 0):
+                for i, chunk in pieces:
+                    stage_copy(i, chunk, mine).start()
+            own_tops = [
+                pltpu.make_async_copy(
+                    tops_ref.at[micro], buffer.at[pl.ds(2 * chain.z, 2)], tops_sem.at[micro]
+                )
+                for micro, buffer in enumerate((blocks, parts))
+            ]
+            for copy in own_tops:
+                copy.start()
+            chain.greet_group(partner)
+            for copy in own_tops:
+                copy.wait()
+            both = (
+                Gather(chain, blocks, gather_send, gather_recv, True),
+                Gather(chain, parts, second_send, second_recv, True),
+            )
+            copies = [
+                pltpu.make_async_copy(blocks, tops_hbm.at[0], tops_sem.at[0]),
+                pltpu.make_async_copy(parts, tops_hbm.at[1], tops_sem.at[1]),
+            ]
+            both[0].start()
+            both[1].start()
+            for i, chunk in pieces:
+                stage_copy(i, chunk, 1).wait()
+                weight_x_copy(i, chunk).start()
+                own_copy(i, chunk, 1).start()
+            for i, chunk in pieces:
+                stage_copy(i, chunk, 0).wait()
+                own_copy(i, chunk, 0).start()
+            for rows in both:
+                for distance in range(1, reach):
+                    rows.relay(distance)
+                    rows.cross_relay(distance)
+            for i, chunk in pieces:
+                weight_x_copy(i, chunk).wait_recv()
+                weight_core_copy(i, chunk, core).start()
+            for i in range(2):
+                for chunk in range(chunks):
+                    weight_core_copy(i, chunk, 1 - core).wait_recv()
+                half_copy(i).start()
+            for rows, copy in zip(both, copies):
+                for k in range(1, reach):
+                    rows.wait_aside(chain.near(k))
+                copy.start()
+            for rows in both:
+                rows.drain()
+            for i, chunk in pieces:
+                weight_x_copy(i, chunk).wait_send()
+                weight_core_copy(i, chunk, core).wait_send()
+                for mine in (1, 0):
+                    own_copy(i, chunk, mine).wait()
+            for i in range(2):
+                half_copy(i).wait()
+            for copy in copies:
+                copy.wait()
+
+    elif tick == last:
+
+        @pl.when(section != 0)
+        def _():
+            run()
+
+    else:
+        run()
+
+
+def exchange_scratch(reach, length, width):
+    piece = (PIECES, length // PIECES, width)
+    return [
+        pltpu.VMEM((2 * reach,) + piece, jnp.bfloat16),
+        pltpu.VMEM((2 * reach,) + piece, jnp.bfloat16),
+        pltpu.VMEM((reach,) + piece, jnp.bfloat16),
+        pltpu.VMEM((reach + 1,) + piece, jnp.bfloat16),
+        pltpu.VMEM((2,) + piece[1:], jnp.bfloat16),
+    ]
+
+
+def exchange_sems(reach):
+    dma = pltpu.SemaphoreType.DMA
+    return [
+        dma((4, reach, PIECES)),
+        dma((2 * reach, PIECES)),
+        dma((reach, PIECES)),
+        dma((reach, PIECES)),
+        dma((reach, PIECES)),
+        dma((reach + 1, PIECES)),
+        dma((2,)),
+        dma((2,)),
+    ]
+
+
+def moe_forward_call(reach, tick, last, own, h1, ids, router, wg, wu, wd, firsts):
+    length, width = own.shape
+    local, _, hidden = wg.shape
+    cap = slot_count(length)
+    experts = router.shape[0]
+    vmem = pl.BlockSpec(memory_space=pltpu.VMEM)
+    anywhere = pl.BlockSpec(memory_space=pl.ANY)
+    slots = (reach, local, 2 * cap, hidden)
+    first = tick == 0
+    all_rows = (2 * reach, PIECES, length // PIECES, width)
+    return pl.pallas_call(
+        functools.partial(moe_forward_kernel, reach, tick, last),
+        in_specs=[vmem] * 4 + [anywhere] * 3 + [anywhere] * 3 * first,
+        out_specs=[vmem] * 4 + [anywhere] * 3 + [anywhere] * 3 * first,
+        out_shape=[
+            jax.ShapeDtypeStruct((length, width), jnp.bfloat16),
+            jax.ShapeDtypeStruct((2 * reach, experts, length), jnp.float32),
+            jax.ShapeDtypeStruct((2 * reach, 8, length), jnp.float32),
+            jax.ShapeDtypeStruct((experts, length), jnp.float32),
+            jax.ShapeDtypeStruct(slots[:3] + (width,), jnp.bfloat16),
+            jax.ShapeDtypeStruct(slots, jnp.bfloat16),
+            jax.ShapeDtypeStruct(slots, jnp.bfloat16),
+        ]
+        + (
+            [jax.ShapeDtypeStruct((2,) + all_rows, jnp.bfloat16)]
+            + [jax.ShapeDtypeStruct((2,) + shard.shape, shard.dtype) for shard in firsts[1:]]
+        )
+        * first,
+        scratch_shapes=exchange_scratch(reach, length, width)
+        + [
+            pltpu.VMEM(wg.shape, jnp.bfloat16),
+            pltpu.VMEM(wu.shape, jnp.bfloat16),
+            pltpu.VMEM(wd.shape, jnp.bfloat16),
+            pltpu.VMEM((2, local, 2 * cap, width), jnp.bfloat16),
+            pltpu.VMEM((2, local * cap, width), jnp.bfloat16),
+            pltpu.VMEM((2,) + slots[1:], jnp.bfloat16),
+            pltpu.VMEM((2,) + slots[1:], jnp.bfloat16),
+            pltpu.VMEM((2, local * cap, length), jnp.bfloat16),
+            pltpu.VMEM((2 * reach, TOPK, length), jnp.int32),
+        ]
+        + exchange_sems(reach)
+        + [
+            pltpu.SemaphoreType.DMA((3,)),
+            pltpu.SemaphoreType.DMA((3, reach)),
+            pltpu.SemaphoreType.DMA((2 * reach,)),
+            pltpu.SemaphoreType.DMA((2 * reach,)),
+        ]
+        + (
+            exchange_sems(reach)[:2]
+            + [pltpu.SemaphoreType.DMA((2,))]
+            + [pltpu.VMEM(shard.shape, shard.dtype) for shard in firsts[1:]]
+            + [
+                pltpu.SemaphoreType.DMA((2, local, 2)),
+                pltpu.SemaphoreType.DMA((2, local, 2)),
+                pltpu.SemaphoreType.DMA((2,)),
+            ]
+            + [pltpu.SemaphoreType.DMA((2, local))] * 4
+        )
+        * first,
+        compiler_params=pltpu.CompilerParams(
+            collective_id=1 + tick, has_side_effects=True, vmem_limit_bytes=62 * MIB
+        ),
+        cost_estimate=pl.CostEstimate(
+            flops=20 * 10**9, bytes_accessed=45 * 10**6, transcendentals=2 * 10**6
+        ),
+        name="moe_forward",
+    )(own, h1, ids, router, wg, wu, wd, *(firsts * first))
+
+
+def moe_backward_kernel(
+    reach,
+    tick,
+    last,
+    own_ref,
+    slots_first,
+    slots_second,
+    gates_first,
+    gates_second,
+    g_first,
+    g_second,
+    u_first,
+    u_second,
+    wg_hbm,
+    wu_hbm,
+    wd_hbm,
+    tops_hbm,
+    after,
+    out_ref,
+    home_gates_ref,
+    picked_hbm,
+    gg_hbm,
+    gu_hbm,
+    hg_hbm,
+    blocks,
+    parts,
+    from_x,
+    from_z,
+    from_cross,
+    wg_ref,
+    wu_ref,
+    wd_ref,
+    rows_in,
+    rows_out,
+    g_slots,
+    u_slots,
+    gg_slots,
+    gu_slots,
+    hg_slots,
+    picks_of,
+    gate_parts,
+    gate_from,
+    gather_send,
+    gather_recv,
+    x_send,
+    x_recv,
+    z_send,
+    z_recv,
+    cross_send,
+    cross_recv,
+    weight_sem,
+    keep_sem,
+    load_sem,
+    gate_send,
+    gate_recv,
+    tops_sem,
+):
+    del after
+    local = wg_ref.shape[0]
+    cap = rows_in.shape[2] // 2
+    section = lax.axis_index(SECTION)
+    chain = Chain(reach)
+    me = chain.me
+
+    def weight_copies():
+        return [
+            pltpu.make_async_copy(hbm, vmem, weight_sem.at[i])
+            for i, (hbm, vmem) in enumerate(
+                ((wd_hbm, wd_ref), (wg_hbm, wg_ref), (wu_hbm, wu_ref))
+            )
+        ]
+
+    def load_copies(step, source, first):
+        slot = step % 2 if isinstance(step, int) else lax.rem(step, 2)
+        return [
+            pltpu.make_async_copy(
+                (g_first if first else g_second).at[source], g_slots.at[slot], load_sem.at[0, step]
+            ),
+            pltpu.make_async_copy(
+                (u_first if first else u_second).at[source], u_slots.at[slot], load_sem.at[1, step]
+            ),
+        ]
+
+    def keep_copies(step, source):
+        slot = step % 2 if isinstance(step, int) else lax.rem(step, 2)
+        return [
+            pltpu.make_async_copy(rows_in.at[slot], picked_hbm.at[source], keep_sem.at[0, step]),
+            pltpu.make_async_copy(gg_slots.at[slot], gg_hbm.at[source], keep_sem.at[1, step]),
+            pltpu.make_async_copy(gu_slots.at[slot], gu_hbm.at[source], keep_sem.at[2, step]),
+            pltpu.make_async_copy(hg_slots.at[slot], hg_hbm.at[source], keep_sem.at[3, step]),
+        ]
+
+    def gate_copy(target, at):
+        return pltpu.make_async_remote_copy(
+            src_ref=gate_parts.at[target],
+            dst_ref=gate_from.at[at],
+            send_sem=gate_send.at[target],
+            recv_sem=gate_recv.at[at],
+            device_id={EXPERT: target // 2, TENSOR: target % 2},
+            device_id_type=MESH_ID,
+        )
+
+    def compute(step, source_of, first):
+        source = source_of(step)
+        slot = lax.rem(step, 2)
+
+        @pl.when(step == 0)
+        def _():
+            for copy in weight_copies():
+                copy.wait()
+
+        @pl.when(step >= 2)
+        def _():
+            for copy in keep_copies(step - 2, source_of(step - 2)):
+                copy.wait()
+
+        for copy in load_copies(step, source, first):
+            copy.wait()
+        slots_ref = slots_first if first else slots_second
+        gates_ref = gates_first if first else gates_second
+        gate_of = {}
+        for i in range(2):
+            at = 2 * source + i
+            for e in range(local):
+                picks = one_hot_slots(slots_ref[at, e : e + 1, :], cap)
+                picks_of[i, e * cap : (e + 1) * cap, :] = picks
+                gate_of[i, e] = slot_gates(picks, gates_ref[at, e : e + 1, :])
+            gathered = dot(picks_of[i], whole_rows(blocks[at])).astype(jnp.bfloat16)
+            for e in range(local):
+                rows_in[slot, e, i * cap : (i + 1) * cap, :] = gathered[e * cap : (e + 1) * cap, :]
+        for e in range(local):
+            plain = dot(rows_in[slot, e], wd_ref[e], NT)
+            gate_pre = g_slots[slot, e].astype(jnp.float32)
+            up_pre = u_slots[slot, e].astype(jnp.float32)
+            sg = jax.nn.sigmoid(gate_pre)
+            hidden = gate_pre * sg * up_pre
+            gate_col = jnp.concatenate([gate_of[i, e] for i in range(2)], axis=0)
+            grad_gate_col = jnp.sum(hidden * plain, axis=1, keepdims=True)
+            grad_hidden = plain * gate_col
+            grad_gate = (grad_hidden * up_pre * sg * (1.0 + gate_pre * (1.0 - sg))).astype(
+                jnp.bfloat16
+            )
+            grad_up = (grad_hidden * gate_pre * sg).astype(jnp.bfloat16)
+            gg_slots[slot, e] = grad_gate
+            gu_slots[slot, e] = grad_up
+            hg_slots[slot, e] = (hidden * gate_col).astype(jnp.bfloat16)
+            grad_rows = dot(grad_gate, wg_ref[e], NT) + dot(grad_up, wu_ref[e], NT)
+            for i in range(2):
+                at = 2 * source + i
+                rows = slice(i * cap, (i + 1) * cap)
+                rows_out[i, e * cap : (e + 1) * cap, :] = grad_rows[rows, :].astype(jnp.bfloat16)
+                picks = picks_of[i, e * cap : (e + 1) * cap, :].astype(jnp.float32)
+                gate_parts[at, e : e + 1, :] = jnp.sum(
+                    picks * grad_gate_col[rows, :], axis=0, keepdims=True
+                )
+        for i in range(2):
+            share = dot(picks_of[i], rows_out[i], TN).astype(jnp.bfloat16)
+            parts[2 * source + i] = share.reshape(parts.shape[1:])
+        for copy in keep_copies(step, source):
+            copy.start()
+
+        @pl.when(step + 2 < reach)
+        def _():
+            for copy in load_copies(step + 2, source_of(step + 2), first):
+                copy.start()
+
+        for i in range(2):
+            at = 2 * source + i
+
+            @pl.when(at != me)
+            def _():
+                gate_copy(at, me).start()
+
+    def finish(piece, total):
+        at = pl.ds(pl.multiple_of(piece * total.shape[0], total.shape[0]), total.shape[0])
+        out_ref[at, :] = total
+
+    def run(gathered):
+        first = gathered
+
+        def source_of(step):
+            if isinstance(step, int):
+                return chain.near(step if gathered else reach - 1 - step)
+            return chain.near(step if gathered else reach - 1 - step)
+
+        def top_copy(step):
+            pair = pl.ds(2 * source_of(step), 2)
+            return pltpu.make_async_copy(
+                tops_hbm.at[min(tick, 1), pair], blocks.at[pair], tops_sem.at[step]
+            )
+
+        for step in range(2):
+            for copy in load_copies(step, source_of(step), first):
+                copy.start()
+        if not gathered:
+            for step in range(reach):
+                top_copy(step).start()
+        for copy in weight_copies():
+            copy.start()
+        chain.greet_group()
+        summed = Reduce(
+            chain,
+            lambda home, column, piece: parts.at[2 * home + column, piece],
+            from_x,
+            from_z,
+            (x_send, x_recv, z_send, z_recv),
+            cross=(from_cross, cross_send, cross_recv),
+        )
+        if gathered:
+            blocks[me] = own_ref[...].reshape(blocks.shape[1:])
+            rows = Gather(chain, blocks, gather_send, gather_recv)
+            gathered_steps(
+                reach, chain, rows, summed, lambda step, source: compute(step, source_of, first)
+            )
+            reduced_in_order(reach, summed, finish)
+            rows.drain()
+        else:
+
+            def step_back(step, carry):
+                k = reach - 1 - step
+                top_copy(step).wait()
+                compute(step, source_of, first)
+                summed.start(k, 0)
+
+                @pl.when(k > 0)
+                def _():
+                    summed.start(k, PIECES - 1)
+                    summed.cross_step(k)
+
+                @pl.when(step >= 1)
+                def _():
+                    for piece in range(PIECES):
+                        summed.arrive(k + 1, piece)
+                        summed.pass_on(k + 1, piece)
+
+                return carry
+
+            lax.fori_loop(0, reach, step_back, 0)
+            summed.cross_step(0)
+            summed.start(0, PIECES - 1)
+            finish_pieces(summed, finish)
+        summed.drain()
+        home_gates_ref[0] = gate_parts[me, :local]
+        for at in range(2 * reach):
+
+            @pl.when(at != me)
+            def _():
+                gate_copy(at, me).wait_send()
+                gate_copy(at, at).wait_recv()
+                home_gates_ref[lax.rem(at - me + 2 * reach, 2 * reach)] = gate_from[at, :local]
+
+        for step in (reach - 2, reach - 1):
+            for copy in keep_copies(step, source_of(step)):
+                copy.wait()
+
+    if tick > 0:
+
+        @pl.when(section == 0)
+        def _():
+            run(True)
+
+    if tick < last:
+
+        @pl.when(section != 0)
+        def _():
+            run(False)
+
+
+def moe_backward_call(
+    reach, tick, last, own, slots_two, gates_two, g_two, u_two, wg, wu, wd, tops, after
+):
+    length, width = own.shape
+    local, _, hidden = wg.shape
+    cap = slot_count(length)
+    vmem = pl.BlockSpec(memory_space=pltpu.VMEM)
+    anywhere = pl.BlockSpec(memory_space=pl.ANY)
+    slot_rows = (reach, local, 2 * cap, hidden)
+    kept = jax.ShapeDtypeStruct(slot_rows, jnp.bfloat16)
+    return pl.pallas_call(
+        functools.partial(moe_backward_kernel, reach, tick, last),
+        in_specs=[vmem] * 5 + [anywhere] * 9,
+        out_specs=[vmem, vmem] + [anywhere] * 4,
+        out_shape=[
+            jax.ShapeDtypeStruct((length, width), jnp.float32),
+            jax.ShapeDtypeStruct((2 * reach, local, length), jnp.float32),
+            jax.ShapeDtypeStruct(slot_rows[:3] + (width,), jnp.bfloat16),
+            kept,
+            kept,
+            kept,
+        ],
+        scratch_shapes=exchange_scratch(reach, length, width)
+        + [
+            pltpu.VMEM(wg.shape, jnp.bfloat16),
+            pltpu.VMEM(wu.shape, jnp.bfloat16),
+            pltpu.VMEM(wd.shape, jnp.bfloat16),
+            pltpu.VMEM((2, local, 2 * cap, width), jnp.bfloat16),
+            pltpu.VMEM((2, local * cap, width), jnp.bfloat16),
+        ]
+        + [pltpu.VMEM((2,) + slot_rows[1:], jnp.bfloat16)] * 5
+        + [
+            pltpu.VMEM((2, local * cap, length), jnp.bfloat16),
+            pltpu.VMEM((2 * reach, 8, length), jnp.float32),
+            pltpu.VMEM((2 * reach, 8, length), jnp.float32),
+        ]
+        + exchange_sems(reach)
+        + [
+            pltpu.SemaphoreType.DMA((3,)),
+            pltpu.SemaphoreType.DMA((4, reach)),
+            pltpu.SemaphoreType.DMA((2, reach)),
+            pltpu.SemaphoreType.DMA((2 * reach,)),
+            pltpu.SemaphoreType.DMA((2 * reach,)),
+            pltpu.SemaphoreType.DMA((reach,)),
+        ],
+        compiler_params=pltpu.CompilerParams(
+            collective_id=4 + tick, has_side_effects=True, vmem_limit_bytes=62 * MIB
+        ),
+        cost_estimate=pl.CostEstimate(
+            flops=20 * 10**9, bytes_accessed=55 * 10**6, transcendentals=2 * 10**6
+        ),
+        name="moe_backward",
+    )(own, *slots_two, *gates_two, *g_two, *u_two, wg, wu, wd, tops, after)
+
+
+def middle_weights_kernel(
+    x_first, x_second, dh_ref, gg_ref, gu_ref, hg_ref, after, wg_ref, wu_ref, wd_ref
+):
+    del after
+    hidden = gg_ref.shape[3]
+    wide = dh_ref.shape[3]
+    rows = of_section(x_first, x_second).reshape(-1, wide)
+    wg_ref[0] = dot(rows, gg_ref[...].reshape(-1, hidden), TN).astype(jnp.bfloat16)
+    wu_ref[0] = dot(rows, gu_ref[...].reshape(-1, hidden), TN).astype(jnp.bfloat16)
+    wd_ref[0] = dot(
+        hg_ref[...].reshape(-1, hidden), dh_ref[...].reshape(-1, wide), TN
+    ).astype(jnp.bfloat16)
+
+
+def middle_weights(x_two, dh, gg, gu, hg, after):
+    groups, local, rows, width = dh.shape
+    hidden = gg.shape[3]
+    tiles = width // hidden
+    wide = width // tiles
+    tiled = pl.BlockSpec((groups, 1, rows, wide), lambda e, t: (0, e, 0, t))
+    held = pl.BlockSpec((groups, 1, rows, hidden), lambda e, t: (0, e, 0, 0))
+    up = jax.ShapeDtypeStruct((local, width, hidden), jnp.bfloat16)
+    return pl.pallas_call(
+        middle_weights_kernel,
+        grid=(local, tiles),
+        in_specs=[tiled] * 3 + [held] * 3 + [pl.BlockSpec(memory_space=pl.ANY)],
+        out_specs=[
+            pl.BlockSpec((1, wide, hidden), lambda e, t: (e, t, 0)),
+            pl.BlockSpec((1, wide, hidden), lambda e, t: (e, t, 0)),
+            pl.BlockSpec((1, hidden, wide), lambda e, t: (e, 0, t)),
+        ],
+        out_shape=[up, up, jax.ShapeDtypeStruct((local, hidden, width), jnp.bfloat16)],
+        compiler_params=pltpu.CompilerParams(vmem_limit_bytes=62 * MIB),
+        cost_estimate=pl.CostEstimate(
+            flops=30 * 10**9, bytes_accessed=60 * 10**6, transcendentals=0
+        ),
+        name="middle_weights",
+    )(*x_two, dh, gg, gu, hg, after)
+
+
+def tail_kernel(
+    reach,
+    tiles,
+    dense_hbm,
+    x_hbm,
+    dh_first,
+    dh_last,
+    gg_first,
+    gg_last,
+    gu_first,
+    gu_last,
+    hg_first,
+    hg_last,
+    wg_before,
+    wu_before,
+    wd_before,
+    small_first,
+    small_both,
+    small_last,
+    ends_back_one,
+    ends_forward_one,
+    ends_back_two,
+    ends_forward_two,
+    query_out,
+    key_out,
+    value_out,
+    out_out,
+    wg_out,
+    wu_out,
+    wd_out,
+    small_out,
+    ends_out,
+    mine,
+    from_core,
+    from_x,
+    from_z,
+    whole,
+    x_rows,
+    dh_rows,
+    slots,
+    before,
+    wg_tile,
+    wu_tile,
+    wd_tile,
+    wg_from,
+    wu_from,
+    wd_from,
+    small_held,
+    small_came,
+    small_z,
+    ends_held,
+    ends_came,
+    mine_sem,
+    core_send,
+    core_recv,
+    x_send,
+    x_recv,
+    z_send,
+    z_recv,
+    ring_send,
+    ring_recv,
+    last_send,
+    last_recv,
+    out_sem,
+    row_sem,
+    slot_sem,
+    before_sem,
+    tile_sem,
+    tile_send,
+    tile_recv,
+    free_sem,
+    small_send,
+    small_recv,
+    ends_load,
+    ends_keep,
+    ends_send,
+    ends_recv,
+):
+    section = lax.axis_index(SECTION)
+    core = lax.axis_index(DP)
+    partner = {DP: 1 - core}
+    chain = Chain(reach)
+    x = chain.x
+    z = chain.z
+    quarter = mine.shape[3]
+    local = gg_first.shape[1]
+    width = x_hbm.shape[3]
+    hidden = gg_first.shape[3]
+    wide = width // tiles
+
+    def mine_copy(half):
+        return pltpu.make_async_copy(dense_hbm.at[half, core], mine.at[half], mine_sem.at[half])
+
+    def core_copy(half, piece):
+        return pltpu.make_async_remote_copy(
+            src_ref=dense_hbm.at[half, 1 - core, :, piece],
+            dst_ref=from_core.at[half, :, piece],
+            send_sem=core_send.at[half, piece],
+            recv_sem=core_recv.at[half, piece],
+            device_id=partner,
+            device_id_type=MESH_ID,
+        )
+
+    def add_core(half, k, piece):
+        home = chain.near(k)
+
+        @pl.when(k == reach - 1)
+        def _():
+            core_copy(half, piece).wait_recv()
+
+        mine[half, home, piece] = (
+            mine[half, home, piece].astype(jnp.float32)
+            + from_core[half, home, piece].astype(jnp.float32)
+        ).astype(jnp.bfloat16)
+
+    summed = Reduce(
+        chain,
+        lambda home, column, piece: mine.at[column, home, piece],
+        from_x,
+        from_z,
+        (x_send, x_recv, z_send, z_recv),
+        TAIL_PIECES,
+    )
+
+    def ring_copy(source, piece, way, target):
+        return pltpu.make_async_remote_copy(
+            src_ref=whole.at[core, source, piece],
+            dst_ref=whole.at[core, source, piece],
+            send_sem=ring_send.at[way, source, piece],
+            recv_sem=ring_recv.at[source, piece],
+            device_id=target,
+            device_id_type=MESH_ID,
+        )
+
+    def last_copy(source, piece, side):
+        return pltpu.make_async_remote_copy(
+            src_ref=whole.at[side, source, piece],
+            dst_ref=whole.at[side, source, piece],
+            send_sem=last_send.at[source, piece],
+            recv_sem=last_recv.at[source, piece],
+            device_id=partner,
+            device_id_type=MESH_ID,
+        )
+
+    def out_copies(side, source):
+        block = whole.at[side, source]
+        at = side * reach + source
+        first = query_out.shape[3]
+        second = first + key_out.shape[3]
+        third = second + value_out.shape[3]
+        half = block.shape[2] - third
+        columns = pl.ds(pl.multiple_of(side * half, half), half)
+        return [
+            pltpu.make_async_copy(block.at[:, :, found], to, out_sem.at[side, source, i])
+            for i, (found, to) in enumerate(
+                (
+                    (pl.ds(0, first), query_out.at[at]),
+                    (pl.ds(first, second - first), key_out.at[at]),
+                    (pl.ds(second, third - second), value_out.at[at]),
+                    (pl.ds(third, half), out_out.at[source, :, :, columns]),
+                )
+            )
+        ]
+
+    def spread_block(source, piece, up, down):
+        if up:
+
+            @pl.when(chain.has_above)
+            def _():
+                ring_copy(source, piece, 0, chain.above).start()
+
+        if down:
+
+            @pl.when(chain.has_below)
+            def _():
+                ring_copy(source, piece, 1, chain.below).start()
+
+        last_copy(source, piece, core).start()
+
+        @pl.when(piece == TAIL_PIECES - 1)
+        def _():
+            for copy in out_copies(core, source):
+                copy.start()
+
+    def relay(distance, piece):
+        @pl.when(z - distance >= 0)
+        def _():
+            ring_copy(z - distance, piece, 0, chain.below).wait_recv()
+            spread_block(z - distance, piece, True, False)
+
+        @pl.when(z + distance <= reach - 1)
+        def _():
+            ring_copy(z + distance, piece, 1, chain.above).wait_recv()
+            spread_block(z + distance, piece, False, True)
+
+    depth = wg_tile.shape[0]
+
+    def spot(index):
+        expert = index // tiles
+        return expert, pl.ds(pl.multiple_of(lax.rem(index, tiles) * wide, wide), wide)
+
+    def tile_loads(index, first):
+        expert, at = spot(index)
+        slot = lax.rem(index, 2)
+        back = dh_last if first else dh_first
+        return [
+            pltpu.make_async_copy(
+                x_hbm.at[:, expert, :, at], x_rows.at[slot], row_sem.at[slot, 0]
+            ),
+            pltpu.make_async_copy(
+                back.at[:, expert, :, at], dh_rows.at[slot], row_sem.at[slot, 1]
+            ),
+        ] + [
+            pltpu.make_async_copy(ref, before.at[slot, i], before_sem.at[slot, i])
+            for i, ref in enumerate(
+                (wg_before.at[expert, at], wu_before.at[expert, at], wd_before.at[expert, :, at])
+            )
+        ]
+
+    def slot_loads(expert, first):
+        slot = lax.rem(expert, 2)
+        return [
+            pltpu.make_async_copy(
+                (two if first else one).at[:, expert], slots.at[slot, i], slot_sem.at[slot, i]
+            )
+            for i, (one, two) in enumerate(
+                ((gg_first, gg_last), (gu_first, gu_last), (hg_first, hg_last))
+            )
+        ]
+
+    def start(copies):
+        @pl.when(section == 0)
+        def _():
+            for copy in copies(True):
+                copy.start()
+
+        @pl.when(section != 0)
+        def _():
+            for copy in copies(False):
+                copy.start()
+
+    held = ((wg_tile, wg_from), (wu_tile, wu_from), (wd_tile, wd_from))
+
+    def tile_sends(index):
+        slot = lax.rem(index, depth)
+        return [
+            pltpu.make_async_remote_copy(
+                src_ref=tile.at[slot],
+                dst_ref=came.at[slot],
+                send_sem=tile_send.at[slot, i],
+                recv_sem=tile_recv.at[slot, i],
+                device_id=partner,
+                device_id_type=MESH_ID,
+            )
+            for i, (tile, came) in enumerate(held)
+        ]
+
+    def tile_stores(index):
+        expert, at = spot(index)
+        slot = lax.rem(index, depth)
+        outs = (wg_out.at[expert, at], wu_out.at[expert, at], wd_out.at[expert, :, at])
+        return [
+            pltpu.make_async_copy(came.at[slot], out, tile_sem.at[slot, i])
+            for i, ((_, came), out) in enumerate(zip(held, outs))
+        ]
+
+    count = local * tiles
+
+    def sum_tile(index):
+        slot = lax.rem(index, depth)
+        for copy, (tile, came) in zip(tile_sends(index), held):
+            copy.wait_recv()
+            came[slot] = (
+                tile[slot].astype(jnp.float32) + came[slot].astype(jnp.float32)
+            ).astype(jnp.bfloat16)
+        for copy in tile_stores(index):
+            copy.start()
+
+    def one_tile(index):
+        slot = lax.rem(index, 2)
+        expert = index // tiles
+        taken = lax.rem(expert, 2)
+
+        @pl.when(index + 1 < count)
+        def _():
+            start(functools.partial(tile_loads, index + 1))
+
+        @pl.when(jnp.logical_and(lax.rem(index, tiles) == 0, expert + 1 < local))
+        def _():
+            start(functools.partial(slot_loads, expert + 1))
+
+        @pl.when(lax.rem(index, tiles) == 0)
+        def _():
+            for copy in slot_loads(expert, True):
+                copy.wait()
+
+        for copy in tile_loads(index, True):
+            copy.wait()
+
+        @pl.when(index >= depth)
+        def _():
+            for copy in tile_sends(index - depth):
+                copy.wait_send()
+            for copy in tile_stores(index - depth):
+                copy.wait()
+            pl.semaphore_signal(free_sem, inc=1, device_id=partner, device_id_type=MESH_ID)
+            pl.semaphore_wait(free_sem, 1)
+
+        to = lax.rem(index, depth)
+        rows = x_rows[slot].reshape(-1, wide)
+        found = (
+            dot(rows, slots[taken, 0].reshape(-1, hidden), TN),
+            dot(rows, slots[taken, 1].reshape(-1, hidden), TN),
+            dot(slots[taken, 2].reshape(-1, hidden), dh_rows[slot].reshape(-1, wide), TN),
+        )
+        for i, (one, (tile, _)) in enumerate(zip(found, held)):
+            tile[to] = (one + before[slot, i].astype(jnp.float32)).astype(jnp.bfloat16)
+        for copy in tile_sends(index):
+            copy.start()
+
+        @pl.when(index >= 1)
+        def _():
+            sum_tile(index - 1)
+
+    def tile_run(low, high):
+        lax.fori_loop(low, high, lambda index, carry: (one_tile(index), carry)[1], 0)
+
+    def small_copy(to, i):
+        if i < 2:
+            return pltpu.make_async_remote_copy(
+                src_ref=small_held.at[i],
+                dst_ref=small_came.at[i],
+                send_sem=small_send.at[i],
+                recv_sem=small_recv.at[i],
+                device_id=to,
+                device_id_type=MESH_ID,
+            )
+        return pltpu.make_async_remote_copy(
+            src_ref=small_z.at[z],
+            dst_ref=small_z.at[z],
+            send_sem=small_send.at[2 + to],
+            recv_sem=small_recv.at[2 + z],
+            device_id={EXPERT: to},
+            device_id_type=MESH_ID,
+        )
+
+    def others(act):
+        for other in range(reach):
+
+            @pl.when(other != z)
+            def _():
+                act(other)
+
+    def small_step(stage):
+        if stage == 0:
+            total = small_both[...] + of_section(small_last, small_first)
+            experts = 2 * reach * local
+            small_held[0, :experts] = pltpu.roll(total[:experts], chain.me * local, 0)
+            small_held[0, experts:] = total[experts:]
+            small_copy(partner, 0).start()
+        elif stage == 1:
+            small_copy(partner, 0).wait_recv()
+            small_held[1] = small_held[0] + small_came[0]
+            small_copy(chain.aside, 1).start()
+        elif stage == 2:
+            small_copy(chain.aside, 1).wait_recv()
+            small_z[z] = small_held[1] + small_came[1]
+            others(lambda other: small_copy(other, 2).start())
+        else:
+
+            def wait(other):
+                pltpu.make_async_remote_copy(
+                    src_ref=small_z.at[other],
+                    dst_ref=small_z.at[other],
+                    send_sem=small_send.at[2 + other],
+                    recv_sem=small_recv.at[2 + other],
+                    device_id={EXPERT: other},
+                    device_id_type=MESH_ID,
+                ).wait_recv()
+
+            others(wait)
+            total = small_z[0]
+            for other in range(1, reach):
+                total = total + small_z[other]
+            small_out[...] = total
+
+    ends_of = ((ends_back_one, ends_forward_one), (ends_back_two, ends_forward_two))
+
+    def ends_copy(m):
+        return pltpu.make_async_remote_copy(
+            src_ref=ends_held.at[m],
+            dst_ref=ends_came.at[m],
+            send_sem=ends_send.at[m],
+            recv_sem=ends_recv.at[m],
+            device_id=chain.aside,
+            device_id_type=MESH_ID,
+        )
+
+    def ends_store(m, other):
+        found = ends_came if other else ends_held
+        at = 1 - x if other else x
+        return pltpu.make_async_copy(found.at[m], ends_out.at[m, at], ends_keep.at[m, int(other)])
+
+    for half in range(2):
+        mine_copy(half).start()
+    for m in range(2):
+        start_of_section(*ends_of[m], ends_held.at[m], ends_load.at[m])
+
+    barrier = pltpu.get_barrier_semaphore()
+    pl.semaphore_signal(barrier, inc=1, device_id=partner, device_id_type=MESH_ID)
+    pl.semaphore_signal(barrier, inc=1, device_id=chain.aside, device_id_type=MESH_ID)
+    others(
+        lambda other: pl.semaphore_signal(
+            barrier, inc=1, device_id={EXPERT: other}, device_id_type=MESH_ID
+        )
+    )
+    pl.semaphore_wait(barrier, 1 + reach)
+
+    def core_start(piece):
+        for half in (1 - x, x):
+            core_copy(half, piece).start()
+
+    for piece in range(2):
+        core_start(piece)
+    small_step(0)
+    start(functools.partial(slot_loads, 0))
+    start(functools.partial(tile_loads, 0))
+    for m in range(2):
+        pltpu.make_async_copy(ends_of[m][0], ends_held.at[m], ends_load.at[m]).wait()
+        ends_store(m, False).start()
+    ends_copy(0).start()
+    for half in range(2):
+        mine_copy(half).wait()
+
+    steps = TAIL_PIECES * reach
+    ahead = 3
+
+    def place(i):
+        return reach - 1 - i % reach, i // reach
+
+    def launch(i):
+        k, piece = place(i)
+        add_core(1 - x, k, piece)
+        summed.start(k, piece)
+
+    def finish(piece, total):
+        whole[core, z, piece] = total.astype(jnp.bfloat16)
+
+    def late(i):
+        def due(offset, act):
+            since = i - offset
+            if isinstance(i, int):
+                if since >= 0 and since % reach == 0 and since // reach < TAIL_PIECES:
+                    act(since // reach)
+            else:
+
+                @pl.when(jnp.logical_and(since >= 0, lax.rem(since, reach) == 0))
+                def _():
+                    act(since // reach)
+
+        def own(piece):
+            summed.finish(piece, finish)
+            spread_block(z, piece, True, True)
+
+        due(reach + 1, own)
+        for distance in range(1, reach):
+            due(reach + 1 + 2 * distance, functools.partial(relay, distance))
+
+    for i in range(ahead):
+        launch(i)
+    small_step(1)
+
+    def step(i, carry):
+        k, piece = place(i)
+
+        @pl.when(jnp.logical_and(k == reach - 1, piece + 2 < TAIL_PIECES))
+        def _():
+            core_start(piece + 2)
+
+        @pl.when(jnp.logical_and(k > 0, piece * (reach - 1) + reach - 1 - k < count))
+        def _():
+            one_tile(piece * (reach - 1) + reach - 1 - k)
+
+        @pl.when(i == reach)
+        def _():
+            small_step(2)
+
+        summed.arrive(k, piece)
+
+        @pl.when(i + ahead < steps)
+        def _():
+            launch(i + ahead)
+
+        add_core(x, k, piece)
+
+        @pl.when(k > 0)
+        def _():
+            summed.pass_on(k, piece)
+
+        late(i)
+        return carry
+
+    lax.fori_loop(0, steps, step, 0)
+    done = min(count, TAIL_PIECES * (reach - 1))
+    ends_copy(1).start()
+    small_step(3)
+    for i in range(steps, steps + 3 * reach):
+        late(i)
+    tile_run(done, count)
+    sum_tile(count - 1)
+
+    def settle_last(source, carry):
+        for piece in range(TAIL_PIECES):
+            last_copy(source, piece, 1 - core).wait_recv()
+        for copy in out_copies(1 - core, source):
+            copy.start()
+        return carry
+
+    lax.fori_loop(0, reach, settle_last, 0)
+    for m in range(2):
+        ends_copy(m).wait_recv()
+        ends_store(m, True).start()
+
+    summed.drain()
+
+    def settle_sends(source, carry):
+        for piece in range(TAIL_PIECES):
+            last_copy(source, piece, core).wait_send()
+
+            @pl.when(jnp.logical_and(chain.has_above, z >= source))
+            def _():
+                ring_copy(source, piece, 0, chain.above).wait_send()
+
+            @pl.when(jnp.logical_and(chain.has_below, z <= source))
+            def _():
+                ring_copy(source, piece, 1, chain.below).wait_send()
+
+        for side in range(2):
+            for copy in out_copies(side, source):
+                copy.wait()
+        return carry
+
+    lax.fori_loop(0, reach, settle_sends, 0)
+    for piece in range(TAIL_PIECES):
+        for half in range(2):
+            core_copy(half, piece).wait_send()
+    for m in range(2):
+        ends_copy(m).wait_send()
+        for other in (False, True):
+            ends_store(m, other).wait()
+    small_copy(partner, 0).wait_send()
+    small_copy(chain.aside, 1).wait_send()
+    others(lambda other: small_copy(other, 2).wait_send())
+    def settle_tiles(index, carry):
+        for copy in tile_sends(index):
+            copy.wait_send()
+        for copy in tile_stores(index):
+            copy.wait()
+        return carry
+
+    lax.fori_loop(count - depth, count, settle_tiles, 0)
+
+
+def tail_call(reach, widths, dense, x_rows, dh_two, gg_two, gu_two, hg_two, before, smalls, ends):
+    halves, cores, _, _, quarter, columns = dense.shape
+    groups, local, slot_rows, width = x_rows.shape
+    hidden = gg_two[0].shape[3]
+    tiles = width // hidden
+    wide = width // tiles
+    anywhere = pl.BlockSpec(memory_space=pl.ANY)
+    vmem = pl.BlockSpec(memory_space=pltpu.VMEM)
+    end = ends[0].shape
+    up = jax.ShapeDtypeStruct((local, width, hidden), jnp.bfloat16)
+    down = jax.ShapeDtypeStruct((local, hidden, width), jnp.bfloat16)
+    block = (TAIL_PIECES, quarter, columns)
+    dma = pltpu.SemaphoreType.DMA
+    return pl.pallas_call(
+        functools.partial(tail_kernel, reach, tiles),
+        in_specs=[anywhere] * 13 + [vmem] * 3 + [anywhere] * 4,
+        out_specs=[anywhere] * 7 + [vmem, anywhere],
+        out_shape=[
+            jax.ShapeDtypeStruct((cores * reach, TAIL_PIECES, quarter, one), jnp.bfloat16)
+            for one in widths
+        ]
+        + [
+            jax.ShapeDtypeStruct((reach, TAIL_PIECES, quarter, width), jnp.bfloat16),
+            up,
+            up,
+            down,
+            jax.ShapeDtypeStruct(smalls[0].shape, jnp.float32),
+            jax.ShapeDtypeStruct((2, 2) + end, jnp.bfloat16),
+        ],
+        scratch_shapes=[
+            pltpu.VMEM((halves, reach) + block, jnp.bfloat16),
+            pltpu.VMEM((halves, reach) + block, jnp.bfloat16),
+            pltpu.VMEM((reach,) + block, jnp.bfloat16),
+            pltpu.VMEM((reach + 1,) + block, jnp.bfloat16),
+            pltpu.VMEM((cores, reach) + block, jnp.bfloat16),
+            pltpu.VMEM((2, groups, slot_rows, wide), jnp.bfloat16),
+            pltpu.VMEM((2, groups, slot_rows, wide), jnp.bfloat16),
+            pltpu.VMEM((2, 3, groups, slot_rows, hidden), jnp.bfloat16),
+            pltpu.VMEM((2, 3, wide, hidden), jnp.bfloat16),
+        ]
+        + [pltpu.VMEM((3, wide, hidden), jnp.bfloat16)] * 6
+        + [pltpu.VMEM((count,) + smalls[0].shape, jnp.float32) for count in (2, 2, reach)]
+        + [pltpu.VMEM((2,) + end, jnp.bfloat16)] * 2
+        + [
+            dma((halves,)),
+            dma((halves, TAIL_PIECES)),
+            dma((halves, TAIL_PIECES)),
+            dma((reach, TAIL_PIECES)),
+            dma((reach, TAIL_PIECES)),
+            dma((reach, TAIL_PIECES)),
+            dma((reach + 1, TAIL_PIECES)),
+            dma((2, reach, TAIL_PIECES)),
+            dma((reach, TAIL_PIECES)),
+            dma((reach, TAIL_PIECES)),
+            dma((reach, TAIL_PIECES)),
+            dma((cores, reach, 4)),
+            dma((2, 2)),
+            dma((2, 3)),
+            dma((2, 3)),
+            dma((3, 3)),
+            dma((3, 3)),
+            dma((3, 3)),
+            pltpu.SemaphoreType.REGULAR,
+            dma((2 + reach,)),
+            dma((2 + reach,)),
+            dma((2,)),
+            dma((2, 2)),
+            dma((2,)),
+            dma((2,)),
+        ],
+        compiler_params=pltpu.CompilerParams(
+            collective_id=7, has_side_effects=True, vmem_limit_bytes=62 * MIB
+        ),
+        cost_estimate=pl.CostEstimate(
+            flops=60 * 10**9, bytes_accessed=120 * 10**6, transcendentals=0
+        ),
+        name="tail",
+    )(dense, x_rows, *dh_two, *gg_two, *gu_two, *hg_two, *before, *smalls, *ends)
+
+
+GROUP = (EXPERT, TENSOR)
+ROWS = (DP, EXPERT)
+
+
+def by_rows(
+    boundary,
+    segments,
+    expert_ids,
+    attn_gain,
+    query_weight,
+    key_weight,
+    value_weight,
+    out_weight,
+    ffn_gain,
+    router_weight,
+    gate_weight,
+    up_weight,
+    down_weight,
+):
+    args = (
+        boundary,
+        segments,
+        expert_ids,
+        attn_gain,
+        query_weight,
+        key_weight,
+        value_weight,
+        out_weight,
+        ffn_gain,
+        router_weight,
+        gate_weight,
+        up_weight,
+        down_weight,
+    )
+    share_rows = expert_ids.shape[2]
+    local = gate_weight.shape[1]
+    if (
+        share_rows != LEN
+        or lax.axis_size(TENSOR) != 2
+        or lax.axis_size(SECTION) != 2
+        or lax.axis_size(DP) != 2
+        or query_weight.shape[2] % (4 * HD)
+    ):
+        return on_device(*args)
+    section = lax.axis_index(SECTION)
+    tensor = lax.axis_index(TENSOR)
+    group_at = lax.axis_index(EXPERT) * lax.axis_size(TENSOR) + tensor
+    micro_count = boundary.shape[1]
+    reach = lax.axis_size(EXPERT)
+    group = query_weight.shape[2] // key_weight.shape[2]
+    own_rows = lax.dynamic_slice_in_dim(boundary[0], tensor * share_rows, share_rows, 1)
+    own_seg = lax.dynamic_slice_in_dim(segments, tensor * share_rows, share_rows, 1)
+    own_ids = jnp.swapaxes(expert_ids[0], 1, 2)
+    gains = (attn_gain, ffn_gain)
+    tables = pair_tables(LEN)
+
+    wqkv_part = jnp.concatenate([query_weight[0], key_weight[0], value_weight[0]], axis=1)
+    wo_part = out_weight[0]
+    wqkv = wo = None
+    router_local = jnp.roll(router_weight[0].T, -group_at * local, axis=0)
+    wg, wu, wd = gate_weight[0], up_weight[0], down_weight[0]
+
+    def pick(array, index):
+        return lax.dynamic_index_in_dim(array, index, 0, keepdims=False)
+
+    arrived = None
+    kept = []
+    wide = []
+    outputs = []
+    for tick in range(micro_count + 1):
+        micro = jnp.clip(tick - section, 0, micro_count - 1)
+        if tick == 0:
+            layer_in = own_rows[0]
+            h1, xn2 = attn_split(
+                boundary[0, 0].reshape(2, share_rows, -1),
+                segments[0].reshape(2, share_rows),
+                gains,
+                wqkv_part,
+                wo_part,
+                tables,
+                group,
+            )
+        else:
+            layer_in = arrived
+            h1, xn1, qkv, att, xn2 = attn_forward(
+                own_rows[tick] if tick < micro_count else arrived,
+                arrived,
+                pick(own_seg, micro),
+                gains,
+                wqkv,
+                wo,
+                tables,
+                group,
+            )
+        h2, gates, slots, own_gates, picked, gate_pre, up_pre, *firsts = moe_forward_call(
+            reach,
+            tick,
+            micro_count,
+            xn2,
+            h1,
+            pick(own_ids, micro),
+            router_local,
+            wg,
+            wu,
+            wd,
+            [
+                boundary[0].reshape(micro_count, 2, PIECES, share_rows // PIECES, -1),
+                wqkv_part,
+                wo_part,
+            ],
+        )
+        outputs.append(h2)
+        arrived = shifted(h2, SECTION, 1)
+        if tick == 0:
+            tops, *before = firsts
+            wqkv, wo = both_halves(wqkv_part, wo_part, h2, before)
+            xn1, qkv, att = attn_again(own_rows[0], own_seg[0], attn_gain, wqkv, tables, group)
+        kept.append((layer_in, h1, xn2, own_gates, qkv, slots, gates, xn1, att))
+        wide.append((picked, gate_pre, up_pre))
+
+    arrived = jnp.zeros(own_rows.shape[1:], jnp.bfloat16)
+    backs = []
+    slotted = []
+    for tick in range(micro_count + 1):
+        micro = jnp.clip(tick - (1 - section), 0, micro_count - 1)
+        ticks = {0: (1, 1), 1: (0, 2), 2: (1, 1)}[tick]
+        pairs = list(zip(*(kept[one] for one in ticks)))
+        sides = [wide[one] for one in ticks]
+        if tick == micro_count:
+            pairs[0] = (own_rows[1], own_rows[1])
+            pairs.insert(5, (arrived, arrived))
+        elif tick == 0:
+            pairs.insert(5, (own_rows[0], own_rows[0]))
+        else:
+            pairs.insert(5, (arrived, own_rows[1]))
+        rows, grad_gates, picked, gg, gu, hg = moe_backward_call(
+            reach,
+            tick,
+            micro_count,
+            arrived,
+            pairs[6],
+            pairs[7],
+            [side[1] for side in sides],
+            [side[2] for side in sides],
+            wg,
+            wu,
+            wd,
+            tops,
+            before[0] if tick == micro_count else tops,
+        )
+        grad_in, mid, dqkv, small = attn_backward(
+            pairs[:6],
+            rows,
+            grad_gates.reshape(EXPERTS, LEN),
+            pick(own_seg, micro),
+            gains,
+            router_local,
+            wqkv,
+            wo,
+            tables,
+            group,
+        )
+        arrived = shifted(grad_in, SECTION, -1)
+        backs.append((grad_in, mid, dqkv, small))
+        slotted.append((picked, gg, gu, hg))
+        if tick == 1:
+            before = middle_weights([side[0] for side in sides], picked, gg, gu, hg, grad_in)
+
+    grads_in, mids, dqkvs, smalls = zip(*backs)
+    dense = attn_weights([one[7] for one in kept], [one[8] for one in kept], mids, dqkvs)
+    width = dense.shape[1]
+    dense = dense.reshape(
+        2, 2, reach, TAIL_PIECES, width // (2 * reach * TAIL_PIECES), dense.shape[2]
+    )
+    widths = [one.shape[2] for one in (query_weight, key_weight, value_weight)]
+    ends = (grads_in[1], outputs[1], grads_in[2], outputs[2])
+    *dense, wg_sum, wu_sum, wd_sum, small, ends = tail_call(
+        reach, widths, dense, wide[1][0], *zip(slotted[0], slotted[2]), before, smalls, ends
+    )
+    return (
+        ends.reshape(1, micro_count, 2 * share_rows, -1),
+        small[EXPERTS + 1][None],
+        *[one.astype(jnp.float32).reshape(1, -1, one.shape[3]) for one in dense],
+        small[EXPERTS][None],
+        small[:EXPERTS].T[None],
+        *[one.astype(jnp.float32)[None] for one in (wg_sum, wu_sum, wd_sum)],
+    )
+
+
 def solution(mesh):
     placed = (
-        P("section", None, ("dp", "expert"), None),
-        P(None, ("dp", "expert")),
-        P("section", None, ("dp", "expert", "tensor"), None),
-        P("section", None),
-        P("section", None, "tensor"),
-        P("section", None, "tensor"),
-        P("section", None, "tensor"),
-        P("section", "tensor", None),
-        P("section", None),
-        P("section", None, None),
-        P("section", ("expert", "tensor"), None, None),
-        P("section", ("expert", "tensor"), None, None),
-        P("section", ("expert", "tensor"), None, None),
+        P(SECTION, None, (DP, EXPERT), None),
+        P(None, (DP, EXPERT)),
+        P(SECTION, None, (DP, EXPERT, TENSOR), None),
+        P(SECTION, None),
+        P(SECTION, None, TENSOR),
+        P(SECTION, None, TENSOR),
+        P(SECTION, None, TENSOR),
+        P(SECTION, TENSOR, None),
+        P(SECTION, None),
+        P(SECTION, None, None),
+        P(SECTION, (EXPERT, TENSOR), None, None),
+        P(SECTION, (EXPERT, TENSOR), None, None),
+        P(SECTION, (EXPERT, TENSOR), None, None),
     )
     return jax.shard_map(
-        on_device,
+        by_rows,
         mesh=mesh,
         in_specs=placed,
         out_specs=(
-            P("section", None, ("dp", "expert"), None),
-            P("section", None),
-            P("section", None, "tensor"),
-            P("section", None, "tensor"),
-            P("section", None, "tensor"),
-            P("section", "tensor", None),
-            P("section", None),
-            P("section", None, None),
-            P("section", ("expert", "tensor"), None, None),
-            P("section", ("expert", "tensor"), None, None),
-            P("section", ("expert", "tensor"), None, None),
+            P(SECTION, None, (DP, EXPERT), None),
+            P(SECTION, None),
+            P(SECTION, None, TENSOR),
+            P(SECTION, None, TENSOR),
+            P(SECTION, None, TENSOR),
+            P(SECTION, TENSOR, None),
+            P(SECTION, None),
+            P(SECTION, None, None),
+            P(SECTION, (EXPERT, TENSOR), None, None),
+            P(SECTION, (EXPERT, TENSOR), None, None),
+            P(SECTION, (EXPERT, TENSOR), None, None),
         ),
         check_vma=False,
     )

time: 4920 us -> 1120 us (0.23)
  waiting for transfers between devices: 1840 us -> 54.8 us
  blocking collectives: 1100 us -> 0 us
  Pallas kernels: 0 us -> 967 us
  local copies, waits for them, and re-layouts: 885 us -> 26.5 us
  matrix products: 619 us -> 0 us
  other arithmetic: 379 us -> 36.4 us
    all_to_all x7 -> x0, waiting for transfers between devices: 1260 us -> none  [the longest x3 554 us: send_home(): lax.all_to_all(produced, ('expert', 'tensor'), split_axis=1, concat_axis=...]
    all_to_all x5 -> x0, blocking collectives: 1050 us -> none  [the longest x3 629 us: send_out(): lax.all_to_all(buffer, ('expert', 'tensor'), split_axis=0, concat_axis=1,...]
    pallas_call x0 -> x17, Pallas kernels: none -> 967 us  [the longest x3 271 us: moe_forward_call(): pl.pallas_call(functools.partial(moe_forward_kernel, reach, tick, last),...]
    dot_general x135 -> x0, matrix products: 598 us -> none  [the longest x3 45.6 us: section_backward(): jnp.einsum('erd,efd->erf', sent, down_weight, preferred_element_type=jnp....]
    psum x9 -> x0, waiting for transfers between devices: 377 us -> none  [the longest x3 109 us: section_forward(): lax.psum(partial_sum.astype(jnp.bfloat16), 'tensor').astype(jnp.float32)]
    gather x12 -> x0, local copies, waits for them, and re-layouts: 222 us -> none  [the longest x3 68.6 us: section_backward(): gathered = flat_grad[jnp.maximum(source - 1, 0)]]
    dynamic_update_slice x60 -> x0, local copies, waits for them, and re-layouts: 181 us -> none  [the longest x36 163 us: section_backward(): lax.map(attend_backward, (query_rot.reshape(seq_count, LEN, -1), key_rot....]
    select_n x51 -> x0, other arithmetic: 176 us -> none  [the longest x27 89.7 us: on_device(): jnp.where(is_valid, lax.dynamic_update_index_in_dim(stack_arr, piece_arr,...]
  transfers between devices with their start and end apart: 26 -> 4, of which waited for: 22 -> 1; matrix products, arithmetic and copies ran while one was open for 13% -> 1% of each run, Pallas kernels for 0% -> 14%
where the time goes in v1:
time: 1120 us; the launch traced here: 1110 us
  Pallas kernels  967 us (86%)
  waiting for transfers between devices  54.8 us (5%)
  other arithmetic  36.4 us (3%)
  local copies, waits for them, and re-layouts  26.5 us (2%)
  starting transfers between devices  23.9 us (2%)
    pallas_call x3, Pallas kernels, moe_forward_call(): pl.pallas_call(functools.partial(moe_forward_kernel, reach, tick, last),...  271 us
    pallas_call x3, Pallas kernels, moe_backward_call(): pl.pallas_call(functools.partial(moe_backward_kernel, reach, tick, last),...  258 us
    pallas_call x1, Pallas kernels, tail_call(): pl.pallas_call(functools.partial(tail_kernel, reach, tiles), in_specs=[an...  193 us
    pallas_call x1, Pallas kernels, both_halves(): pl.pallas_call(functools.partial(both_halves_kernel, chunks), in_specs=[a...  73.8 us
    pallas_call x3, Pallas kernels, attn_backward(): pl.pallas_call(functools.partial(attn_backward_kernel, group), in_specs=[...  62.5 us
    ppermute x4, waiting for transfers between devices, shifted(): return lax.ppermute(block, axis, route)  54.8 us
    pallas_call x2, Pallas kernels, attn_forward(): pl.pallas_call(functools.partial(attn_forward_kernel, group), in_specs=[a...  30.7 us
    pallas_call x1, Pallas kernels, attn_split(): pl.pallas_call(functools.partial(attn_split_kernel, group), in_specs=[vme...  26.5 us
  transfers between devices with their start and end apart: 4, of which 1 were waited for; matrix products, arithmetic and copies ran while one was open for 1% of the time, Pallas kernels for 14%

profile of v1, /device:TPU:25, one launch (start us, length us, event | category | flops | bytes accessed | tf_op | source)
XLA Modules:
  0.0 1110.4 jit_solution(9285093440116805168)
XLA Ops:
  0.7 0.8 fusion.5
  1.5 0.2 broadcast_in_dim_reshape_squeeze.8.seg_col_ref
  1.8 1.5 slice.33
  3.3 1.7 fusion.router_ref.refs_16_
  5.0 0.5 fusion.1
  5.5 0.3 pad_maximum_fusion.1
  5.8 0.0 copy-start
  5.8 0.0 copy-start.13
  5.8 0.0 copy-start.2
  5.9 3.4 pad_maximum_fusion.wqkv_ref.refs_1_.wqkv
  9.3 0.6 dynamic-slice_bitcast_fusion.2
  9.9 26.5 %attn_split.1 = (f32[256,1536]{1,0:T(8,128)S(1)}, bf16[256,1536]{1,0:T(8,128)(2,1)S(1)}) custom-call(bf16[2,256,1536]{2,1,0:T(8,128)(2,1)S(1)} %bitcast.64, f32[1,1536]{1,0:T(1,128)S(1)} %copy-done.2, bf16[1536,1280]{1,0:T(8,128)(2,1)} %pad_maximum_fusion.wqkv_ref.refs_1_.wqkv, bf16[768,1536]{1,0:T(8,128)(2,1)} %bitcast.72, ...), custom_call_target="tpu_custom_call" | custom-call | flops 4000000000 | bytes 20000000 | tf_op jit(solution)/shard_map/attn_split/pallas_call | solution.py:883
  36.4 0.0 copy-start.4
  36.4 1.1 copy-done.4
  37.5 0.9 copy-done.5
  38.4 132.8 %moe_forward.3 = (bf16[256,1536]{1,0:T(8,128)(2,1)}, f32[8,32,256]{2,1,0:T(8,128)}, f32[8,8,256]{2,1,0:T(8,128)}, f32[32,256]{1,0:T(8,128)}, bf16[4,4,192,1536]{...) custom-call(bf16[256,1536]{1,0:T(8,128)(2,1)} %copy-done.5, ...), custom_call_target="tpu_custom_call" | custom-call | flops 20000000000 | bytes 45000000 | tf_op jit(solution)/shard_map/moe_forward/pallas_call | solution.py:2082
  171.2 19.8 %collective-permute-start = (bf16[256,1536]{1,0:T(8,128)(2,1)}, bf16[256,1536]{1,0:T(8,128)(2,1)S(1)}, u32[]{:S(2)}, u32[]{:S(2)}) collective-permute-start(bf16[256,1536]{1,0:T(8,128)(2,1)} %get-tuple-element.96.after), channel_id=1, source_target_pairs={{0,16},{1,17},{2,18},{3,19},{4,20},{5,21},{6,22},{7,23},{8,24},{9,... | collective-permute-start | bytes 2359304 | tf_op jit(solution)/shard_map/ppermute | solution.py:25
  191.1 0.1 fusion.4
  191.2 0.0 copy-start.20
  191.3 0.8 copy.36.seg_col_ref
  192.1 0.8 copy.37.seg_col_ref
  192.9 0.8 copy.38.refs_21_
  193.7 0.8 copy.35.seg_col_ref
  194.5 0.8 copy.39.refs_21_
  195.2 0.8 copy.40.refs_21_
  196.0 73.8 %both_halves.1 = (bf16[2,1536,1280]{2,1,0:T(8,128)(2,1)}, bf16[2,768,1536]{2,1,0:T(8,128)(2,1)}) custom-call(bf16[1536,1280]{1,0:T(8,128)(2,1)} %pad_maximum_fusion.wqkv_ref.refs_1_.wqkv, bf16[768,1536]{1,0:T(8,128)(2,1)} %bitcast.74, bf16[256,1536]{1,0:T(8,128)(2,1)} %get-tuple-element.96.after, ...), custom_call_target="tpu_custom_call", output_to_operand_aliasing={{0}: (3, {}), {1}: (4, {})} | custom-call | bytes 30000000 | tf_op jit(solution)/shard_map/both_halves/pallas_call | solution.py:1014
  269.9 2.6 dynamic-slice_bitcast_fusion
  272.5 13.0 %attn_again.1 = (bf16[256,1536]{1,0:T(8,128)(2,1)}, bf16[2,256,1280]{2,1,0:T(8,128)(2,1)}, bf16[2,256,768]{2,1,0:T(8,128)(2,1)}) custom-call(bf16[256,1536]{1,0:T(8,128)(2,1)} %get-tuple-element.178.x_ref.refs_10_.refs_11_.refs_0_, f32[1,1536]{1,0:T(1,128)} %refs_17_.5, bf16[2,1536,1280]{2,1,0:T(8,128)(2,1)} %get-tuple-element.99.wqkv_hbm.refs_12_, ...), custom_call_target="tpu_custom_call" | custom-call | flops 3000000000 | bytes 12000000 | tf_op jit(solution)/shard_map/attn_again/pallas_call | solution.py:791
  285.5 0.9 copy-done.21
  286.4 15.3 %attn_forward.2 = (f32[256,1536]{1,0:T(8,128)}, bf16[256,1536]{1,0:T(8,128)(2,1)}, bf16[2,256,1280]{2,1,0:T(8,128)(2,1)}, bf16[2,256,768]{2,1,0:T(8,128)(2,1)}, bf16[256,1536]{1,0:T(8,128)(2,1)}) custom-call(bf16[256,1536]{1,0:T(8,128)(2,1)} %get-tuple-element.177.x_first.refs_11_.refs_0_.refs_1_, bf16[256,1536]{1,0:T(8,128)(2,1)} %copy-done.21, ...), custom_call_target="tpu_custom_call" | custom-call | flops 4000000000 | bytes 20000000 | tf_op jit(solution)/shard_map/attn_forward/pallas_call | solution.py:720
  301.8 133.9 %moe_forward.4 = (bf16[256,1536]{1,0:T(8,128)(2,1)}, f32[8,32,256]{2,1,0:T(8,128)}, f32[8,8,256]{2,1,0:T(8,128)}, f32[32,256]{1,0:T(8,128)}, bf16[4,4,192,1536]{...) custom-call(bf16[256,1536]{1,0:T(8,128)(2,1)} %get-tuple-element.103.own_ref.refs_4_.refs_5_, ...), custom_call_target="tpu_custom_call" | custom-call | flops 20000000000 | bytes 45000000 | tf_op jit(solution)/shard_map/moe_forward/pallas_call | solution.py:2082
  435.7 1.3 collective-permute-start.1
  437.0 0.9 broadcast_in_dim.48.own_ref
  438.0 4.1 moe_backward.3
  442.1 1.4 reshape.98.refs_15_
  443.5 20.8 %attn_backward.3 = (bf16[256,1536]{1,0:T(8,128)(2,1)}, bf16[256,1536]{1,0:T(8,128)(2,1)}, bf16[2,256,1280]{2,1,0:T(8,128)(2,1)}, f32[40,1536]{1,0:T(8,128)}) custom-call(bf16[256,1536]{1,0:T(8,128)(2,1)} %copy-done.21, bf16[256,1536]{1,0:T(8,128)(2,1)} %copy-done.21, f32[256,1536]{1,0:T(8,128)} %get-tuple-element.104.h1_ref.refs_2_.refs_3_, ...), custom_call_target="tpu_custom_call" | custom-call | flops 8000000000 | bytes 20000000 | tf_op jit(solution)/shard_map/attn_backward/pallas_call | solution.py:1194
  464.3 1.5 collective-permute-start.2
  465.8 0.9 copy-done.22
  466.7 15.3 %attn_forward.3 = (f32[256,1536]{1,0:T(8,128)}, bf16[256,1536]{1,0:T(8,128)(2,1)}, bf16[2,256,1280]{2,1,0:T(8,128)(2,1)}, bf16[2,256,768]{2,1,0:T(8,128)(2,1)}, bf16[256,1536]{1,0:T(8,128)(2,1)}) custom-call(bf16[256,1536]{1,0:T(8,128)(2,1)} %copy-done.22, bf16[256,1536]{1,0:T(8,128)(2,1)} %copy-done.22, f32[1,1536]{1,0:T(1,128)} %refs_17_.5, ...), custom_call_target="tpu_custom_call" | custom-call | flops 4000000000 | bytes 20000000 | tf_op jit(solution)/shard_map/attn_forward/pallas_call | solution.py:720
  482.0 4.0 moe_forward.5
  486.0 0.9 copy-done.23
  486.9 141.1 %moe_backward.4 = (f32[256,1536]{1,0:T(8,128)}, f32[8,4,256]{2,1,0:T(4,128)}, bf16[4,4,192,1536]{3,2,1,0:T(8,128)(2,1)}, bf16[4,4,192,512]{3,2,1,0:T(8,128)(2,1)...) custom-call(bf16[256,1536]{1,0:T(8,128)(2,1)} %copy-done.23, ...), custom_call_target="tpu_custom_call" | custom-call | flops 20000000000 | bytes 55000000 | tf_op jit(solution)/shard_map/moe_backward/pallas_call | solution.py:2419
  628.0 1.4 reshape.100.refs_15_
  629.3 20.8 %attn_backward.4 = (bf16[256,1536]{1,0:T(8,128)(2,1)}, bf16[256,1536]{1,0:T(8,128)(2,1)}, bf16[2,256,1280]{2,1,0:T(8,128)(2,1)}, f32[40,1536]{1,0:T(8,128)}) custom-call(bf16[256,1536]{1,0:T(8,128)(2,1)} %get-tuple-element.178.x_ref.refs_10_.refs_11_.refs_0_, bf16[256,1536]{1,0:T(8,128)(2,1)} %copy-done.22, f32[256,1536]{1,0:T(8,128)} %copy-done.4, ...), custom_call_target="tpu_custom_call" | custom-call | flops 8000000000 | bytes 20000000 | tf_op jit(solution)/shard_map/attn_backward/pallas_call | solution.py:1194
  650.2 1.3 collective-permute-start.3
  651.5 26.0 %middle_weights.1 = (bf16[4,1536,512]{2,1,0:T(8,128)(2,1)}, bf16[4,1536,512]{2,1,0:T(8,128)(2,1)}, bf16[4,512,1536]{2,1,0:T(8,128)(2,1)}) custom-call(bf16[4,4,192,1536]{3,2,1,0:T(8,128)(2,1)} %get-tuple-element.139.x_first, bf16[4,4,192,1536]{3,2,1,0:T(8,128)(2,1)} %get-tuple-element.140.x_second, bf16[4,4,192,1536]{3,2,1,0:T(8,128)(2,1)} %get-tuple-element.141.dh_ref, ...), custom_call_target="tpu_custom_call" | custom-call | flops 30000001024 | bytes 60000000 | tf_op jit(solution)/shard_map/middle_weights/pallas_call | solution.py:2486
  677.5 54.8 %collective-permute-done.3.own_ref.refs_10_.refs_11_ = bf16[256,1536]{1,0:T(8,128)(2,1)S(1)} collective-permute-done((bf16[256,1536]{1,0:T(8,128)(2,1)}, bf16[256,1536]{1,0:T(8,128)(2,1)S(1)}, u32[]{:S(2)}, u32[]{:S(2)}) %collective-permute-start.3) | collective-permute-done | bytes 786464 | tf_op jit(solution)/shard_map/ppermute | solution.py:25
  732.3 0.9 copy-done.24
  733.2 113.2 %moe_backward.5 = (f32[256,1536]{1,0:T(8,128)}, f32[8,4,256]{2,1,0:T(4,128)}, bf16[4,4,192,1536]{3,2,1,0:T(8,128)(2,1)}, bf16[4,4,192,512]{3,2,1,0:T(8,128)(2,1)...) custom-call(bf16[256,1536]{1,0:T(8,128)(2,1)} %copy-done.24, ...), custom_call_target="tpu_custom_call" | custom-call | flops 20000000000 | bytes 55000000 | tf_op jit(solution)/shard_map/moe_backward/pallas_call | solution.py:2419
  846.4 1.4 reshape.101.refs_15_
  847.8 20.8 %attn_backward.5 = (bf16[256,1536]{1,0:T(8,128)(2,1)}, bf16[256,1536]{1,0:T(8,128)(2,1)}, bf16[2,256,1280]{2,1,0:T(8,128)(2,1)}, f32[40,1536]{1,0:T(8,128)}) custom-call(bf16[256,1536]{1,0:T(8,128)(2,1)} %get-tuple-element.177.x_first.refs_11_.refs_0_.refs_1_, bf16[256,1536]{1,0:T(8,128)(2,1)} %get-tuple-element.177.x_first.refs_11_.refs_0_.refs_1_, ...), custom_call_target="tpu_custom_call" | custom-call | flops 8000000000 | bytes 20000000 | tf_op jit(solution)/shard_map/attn_backward/pallas_call | solution.py:1194
  868.6 13.3 %attn_weights.1 = bf16[2,1536,2048]{2,1,0:T(8,128)(2,1)} custom-call(bf16[256,1536]{1,0:T(8,128)(2,1)} %get-tuple-element.100.refs_0_, bf16[256,1536]{1,0:T(8,128)(2,1)} %get-tuple-element.102.refs_1_, bf16[256,1536]{1,0:T(8,128)(2,1)} %get-tuple-element.106.refs_2_, bf16[2,256,768]{2,1,0:T(8,128)(2,1)} %get-tuple-element.107.refs_3_, ...), custom_call_target="tpu_custom_call" | custom-call | flops 7000000000 | bytes 20000000 | tf_op jit(solution)/shard_map/attn_weights/pallas_call | solution.py:1268
  881.9 192.6 %tail.1 = (bf16[8,4,48,768]{3,2,1,0:T(8,128)(2,1)}, bf16[8,4,48,256]{3,2,1,0:T(8,128)(2,1)}, bf16[8,4,48,256]{3,2,1,0:T(8,128)(2,1)}, bf16[4,4,48,1536]{3,2,1,0:...) custom-call(bf16[2,2,4,4,48,2048]{5,4,3,2,1,0:T(8,128)(2,1)} %bitcas, ...), custom_call_target="tpu_custom_call" | custom-call | flops 60000002048 | bytes 120000000 | tf_op jit(solution)/shard_map/tail/pallas_call | solution.py:3080
  1074.5 1.8 slice_bitcast_fusion
  1076.3 1.5 fusion.3
  1077.8 9.5 bitcast_convert_fusion
  1087.3 6.6 bitcast_convert_fusion.1
  1093.9 6.6 bitcast_convert_fusion.2
  1100.4 2.8 convert.10
  1103.3 2.5 convert.7
  1105.8 1.3 convert.8
  1107.1 1.3 convert.9
  1108.3 0.2 copy-done.6
  1108.6 1.7 copy.44
  (53 shorter events, 0.1 us)
Async XLA Ops:
  0.6 5.2 copy-start.12
  0.7 5.2 copy-start.11
  5.8 4.1 copy-start
  5.8 4.1 copy-start.1
  5.8 3.4 copy-start.13
  5.8 4.0 copy-start.2
  5.8 4.0 copy-start.3
  36.4 1.1 copy-start.4
  37.5 0.9 copy-start.5
  38.4 152.7 %copy-start.14 = (s32[2,512]{1,0:T(2,128)S(1)}, s32[2,512]{1,0:T(2,128)}, u32[]{:S(2)}) copy-start(s32[2,512]{1,0:T(2,128)} %param.14) | copy-start | bytes 12292
  171.2 114.3 %collective-permute-start = (bf16[256,1536]{1,0:T(8,128)(2,1)}, bf16[256,1536]{1,0:T(8,128)(2,1)S(1)}, u32[]{:S(2)}, u32[]{:S(2)}) collective-permute-start(bf16[256,1536]{1,0:T(8,128)(2,1)} %get-tuple-element.96.after), channel_id=1, source_target_pairs={{0,16},{1,17},{2,18},{3,19},{4,20},{5,21},{6,22},{7,23},{8,24},{9,... | collective-permute-start | bytes 2359304 | tf_op jit(solution)/shard_map/ppermute | solution.py:25
  191.2 4.1 copy-start.15
  191.2 78.6 %copy-start.16 = (s32[1,256]{1,0:T(1,128)}, s32[1,256]{1,0:T(1,128)S(1)}, u32[]{:S(2)}) copy-start(s32[1,256]{1,0:T(1,128)S(1)} %get-tuple-element.189.refs_22_) | copy-start | bytes 3076
  191.2 78.6 %copy-start.17 = (s32[1,256]{1,0:T(1,128)}, s32[1,256]{1,0:T(1,128)S(1)}, u32[]{:S(2)}) copy-start(s32[1,256]{1,0:T(1,128)S(1)} %get-tuple-element.186.seg_row_ref) | copy-start | bytes 3076
  191.2 78.6 %copy-start.18 = (s32[1,256]{1,0:T(1,128)}, s32[1,256]{1,0:T(1,128)S(1)}, u32[]{:S(2)}) copy-start(s32[1,256]{1,0:T(1,128)S(1)} %get-tuple-element.185.refs_22_) | copy-start | bytes 3076
  191.2 78.6 %copy-start.19 = (s32[1,256]{1,0:T(1,128)}, s32[1,256]{1,0:T(1,128)S(1)}, u32[]{:S(2)}) copy-start(s32[1,256]{1,0:T(1,128)S(1)} %get-tuple-element.187.seg_row_ref) | copy-start | bytes 3076
  191.2 78.6 %copy-start.20 = (s32[1,256]{1,0:T(1,128)}, s32[1,256]{1,0:T(1,128)S(1)}, u32[]{:S(2)}) copy-start(s32[1,256]{1,0:T(1,128)S(1)} %get-tuple-element.188.seg_row_ref) | copy-start | bytes 3076
  285.5 0.9 copy-start.21
  435.7 30.1 %collective-permute-start.1 = (bf16[256,1536]{1,0:T(8,128)(2,1)}, bf16[256,1536]{1,0:T(8,128)(2,1)S(1)}, u32[]{:S(2)}, u32[]{:S(2)}) collective-permute-start(bf16[256,1536]{1,0:T(8,128)(2,1)} %get-tuple-element.105.ends_forward_one), channel_id=1, source_target_pairs={{0,16},{1,17},{2,18},{3,19},{4,20},{5,21},{6,22},{7,23},{8,24},{9,... | collective-permute-start | bytes 2359304 | tf_op jit(solution)/shard_map/ppermute | solution.py:25
  464.3 21.7 %collective-permute-start.2 = (bf16[256,1536]{1,0:T(8,128)(2,1)}, bf16[256,1536]{1,0:T(8,128)(2,1)S(1)}, u32[]{:S(2)}, u32[]{:S(2)}) collective-permute-start(bf16[256,1536]{1,0:T(8,128)(2,1)} %get-tuple-element.126), channel_id=1, source_target_pairs={{16,0},{17,1},{18,2},{19,3},{20,4},{21,5},{22,6},{23,7},{24,8},{25... | collective-permute-start | bytes 2359304 | tf_op jit(solution)/shard_map/ppermute | solution.py:25
  465.8 0.9 copy-start.22
  486.0 0.9 copy-start.23
  650.2 82.1 %collective-permute-start.3 = (bf16[256,1536]{1,0:T(8,128)(2,1)}, bf16[256,1536]{1,0:T(8,128)(2,1)S(1)}, u32[]{:S(2)}, u32[]{:S(2)}) collective-permute-start(bf16[256,1536]{1,0:T(8,128)(2,1)} %get-tuple-element.138.after.ends_back_one), channel_id=1, source_target_pairs={{16,0},{17,1},{18,2},{19,3},{20,4},{21,5},{22,6},{23,7},{24,8},{25... | collective-permute-start | bytes 2359304 | tf_op jit(solution)/shard_map/ppermute | solution.py:25
  732.3 0.9 copy-start.24
  1074.5 12.7 %slice-start.2 = ((s8[6291456]{0:T(1024)(128)(4,1)}), s8[4194304]{0:T(1024)(128)(4,1)S(1)}, s32[]{:S(2)}) async-start(s8[6291456]{0:T(1024)(128)(4,1)} %bitcast.68), calls=%async_computation.2 | async-start | bytes 8388608
  1077.8 9.5 slice-start.3
  1077.8 16.1 %slice-start = ((s8[6291456]{0:T(1024)(128)(4,1)}), s8[4194304]{0:T(1024)(128)(4,1)S(1)}, s32[]{:S(2)}) async-start(s8[6291456]{0:T(1024)(128)(4,1)} %bitcast.66), calls=%async_computation | async-start | bytes 8388608
  1087.3 6.6 slice-start.1
  1093.9 6.6 copy-start.8
  1100.4 2.8 copy-start.7
  1103.3 2.6 copy-start.10
  1103.3 3.8 copy-start.9
  1105.8 2.7 copy-start.6

commit v2 on v1

--- a/solution.py
+++ b/solution.py
@@ -648,6 +648,7 @@
 
 def attn_forward_kernel(
     group,
+    skipped,
     x_first,
     x_second,
     gain_one_ref,
@@ -669,56 +670,58 @@
     x_sem,
     weight_sem,
 ):
-    parts = wqkv_ref.shape[0]
-
-    def weight_copies(half):
-        return [
-            pltpu.make_async_copy(hbm.at[half], ref.at[half], weight_sem.at[i, half])
-            for i, (hbm, ref) in enumerate(((wqkv_hbm, wqkv_ref), (wo_hbm, wo_ref)))
-        ]
-
-    start_of_section(x_first, x_second, x_ref, x_sem)
-    for copy in weight_copies(0):
-        copy.start()
-    pltpu.make_async_copy(x_first, x_ref, x_sem).wait()
-    rows = x_ref[...].astype(jnp.float32)
-    xn1_ref[...] = (rows * rms_scale(rows) * gain_one_ref[...]).astype(jnp.bfloat16)
-    h1_ref[...] = rows
-
-    def one(half, carry):
-        for copy in weight_copies(half):
-            copy.wait()
-
-        @pl.when(half + 1 < parts)
-        def _():
-            for copy in weight_copies(half + 1):
-                copy.start()
-
-        turned, attended = attend_part(
-            group,
-            xn1_ref[...],
-            wqkv_ref[half],
-            (cos_ref[...], sin_ref[...]),
-            allowed_pairs(seg_col_ref[...], seg_row_ref[...]),
-        )
-        qkv_ref[half] = turned
-        att_ref[half] = attended
-        h1_ref[...] += dot(attended, wo_ref[half])
-        return carry
-
-    lax.fori_loop(0, parts, one, 0)
-    middle = h1_ref[...]
-    xn2_ref[...] = (middle * rms_scale(middle) * gain_two_ref[...]).astype(jnp.bfloat16)
-
-
-def attn_forward(first, second, seg, gains, wqkv, wo, tables, group):
+    @pl.when(lax.axis_index(SECTION) != skipped)
+    def _():
+        parts = wqkv_ref.shape[0]
+
+        def weight_copies(half):
+            return [
+                pltpu.make_async_copy(hbm.at[half], ref.at[half], weight_sem.at[i, half])
+                for i, (hbm, ref) in enumerate(((wqkv_hbm, wqkv_ref), (wo_hbm, wo_ref)))
+            ]
+
+        start_of_section(x_first, x_second, x_ref, x_sem)
+        for copy in weight_copies(0):
+            copy.start()
+        pltpu.make_async_copy(x_first, x_ref, x_sem).wait()
+        rows = x_ref[...].astype(jnp.float32)
+        xn1_ref[...] = (rows * rms_scale(rows) * gain_one_ref[...]).astype(jnp.bfloat16)
+        h1_ref[...] = rows
+
+        def one(half, carry):
+            for copy in weight_copies(half):
+                copy.wait()
+
+            @pl.when(half + 1 < parts)
+            def _():
+                for copy in weight_copies(half + 1):
+                    copy.start()
+
+            turned, attended = attend_part(
+                group,
+                xn1_ref[...],
+                wqkv_ref[half],
+                (cos_ref[...], sin_ref[...]),
+                allowed_pairs(seg_col_ref[...], seg_row_ref[...]),
+            )
+            qkv_ref[half] = turned
+            att_ref[half] = attended
+            h1_ref[...] += dot(attended, wo_ref[half])
+            return carry
+
+        lax.fori_loop(0, parts, one, 0)
+        middle = h1_ref[...]
+        xn2_ref[...] = (middle * rms_scale(middle) * gain_two_ref[...]).astype(jnp.bfloat16)
+
+
+def attn_forward(first, second, seg, gains, wqkv, wo, tables, group, skipped):
     length, width = first.shape
     parts, _, qkv_width = wqkv.shape
     att_width = wo.shape[1]
     vmem = pl.BlockSpec(memory_space=pltpu.VMEM)
     anywhere = pl.BlockSpec(memory_space=pl.ANY)
     return pl.pallas_call(
-        functools.partial(attn_forward_kernel, group),
+        functools.partial(attn_forward_kernel, group, skipped),
         in_specs=[anywhere] * 2 + [vmem] + [anywhere] * 2 + [vmem] * 5,
         out_specs=[vmem] * 5,
         out_shape=[
@@ -1035,100 +1038,102 @@
     )(wqkv, wo, after, *before)
 
 
-def attn_backward_kernel(group, *refs):
-    pairs = [refs[2 * i : 2 * i + 2] for i in range(6)]
-    (
-        wqkv_hbm,
-        wo_hbm,
-        rows_ref,
-        grad_gates_ref,
-        router_ref,
-        gain_one_ref,
-        gain_two_ref,
-        cos_ref,
-        sin_ref,
-        seg_col_ref,
-        seg_row_ref,
-        grad_in_ref,
-        mid_ref,
-        dqkv_ref,
-        small_ref,
-        x_ref,
-        h1_ref,
-        xn2_ref,
-        gates_ref,
-        qkv_ref,
-        top_ref,
-        wqkv_ref,
-        wo_ref,
-        middle_acc,
-        normed_acc,
-        taken_sem,
-        weight_sem,
-    ) = refs[12:]
-    taken = (x_ref, h1_ref, xn2_ref, gates_ref, qkv_ref, top_ref)
-    experts = grad_gates_ref.shape[0]
-    parts = wqkv_ref.shape[0]
-
-    def weight_copies(half):
-        return [
-            pltpu.make_async_copy(hbm.at[half], ref.at[half], weight_sem.at[i, half])
-            for i, (hbm, ref) in enumerate(((wqkv_hbm, wqkv_ref), (wo_hbm, wo_ref)))
-        ]
-
-    for i in (3, 2, 1, 5, 4, 0):
-        start_of_section(*pairs[i], taken[i], taken_sem.at[i])
-
-    def arrived(i):
-        pltpu.make_async_copy(pairs[i][0], taken[i], taken_sem.at[i]).wait()
-        return taken[i]
-
-    gates = arrived(3)[...]
-    grad_gates = grad_gates_ref[...]
-    chosen = gates * (grad_gates - jnp.sum(gates * grad_gates, axis=0, keepdims=True))
-    logits = chosen.astype(jnp.bfloat16)
-    small_ref[0:experts, :] = dot(logits, arrived(2)[...])
-    for copy in weight_copies(0):
-        copy.start()
-    grad_normed = dot(logits, router_ref[...], TN) + rows_ref[...].astype(jnp.float32)
-    middle = arrived(1)[...]
-    grad_middle, gain_grad = norm_back(grad_normed, middle, rms_scale(middle), gain_two_ref[...])
-    small_ref[experts : experts + 1, :] = gain_grad[None, :]
-    grad_middle = grad_middle + arrived(5)[...].astype(jnp.float32)
-    middle_acc[...] = grad_middle
-    mid_ref[...] = grad_middle.astype(jnp.bfloat16)
-    normed_acc[...] = jnp.zeros_like(normed_acc)
-    arrived(4)
-
-    def one(half, carry):
-        for copy in weight_copies(half):
-            copy.wait()
-
-        @pl.when(half + 1 < parts)
-        def _():
-            for copy in weight_copies(half + 1):
-                copy.start()
-
-        attn_backward_part(
-            group,
-            half,
+def attn_backward_kernel(group, skipped, *refs):
+    @pl.when(lax.axis_index(SECTION) != skipped)
+    def _():
+        pairs = [refs[2 * i : 2 * i + 2] for i in range(6)]
+        (
+            wqkv_hbm,
+            wo_hbm,
+            rows_ref,
+            grad_gates_ref,
+            router_ref,
+            gain_one_ref,
+            gain_two_ref,
+            cos_ref,
+            sin_ref,
+            seg_col_ref,
+            seg_row_ref,
+            grad_in_ref,
             mid_ref,
+            dqkv_ref,
+            small_ref,
+            x_ref,
+            h1_ref,
+            xn2_ref,
+            gates_ref,
+            qkv_ref,
+            top_ref,
             wqkv_ref,
             wo_ref,
-            (cos_ref[...], -sin_ref[...]),
-            (seg_col_ref[...], seg_row_ref[...]),
-            qkv_ref,
-            dqkv_ref,
+            middle_acc,
             normed_acc,
-        )
-        return carry
-
-    lax.fori_loop(0, parts, one, 0)
-    rows = arrived(0)[...].astype(jnp.float32)
-    grad_rows, gain_grad = norm_back(normed_acc[...], rows, rms_scale(rows), gain_one_ref[...])
-    grad_in_ref[...] = (grad_rows + middle_acc[...]).astype(jnp.bfloat16)
-    small_ref[experts + 1 : experts + 2, :] = gain_grad[None, :]
-    small_ref[experts + 2 :, :] = jnp.zeros_like(small_ref[experts + 2 :, :])
+            taken_sem,
+            weight_sem,
+        ) = refs[12:]
+        taken = (x_ref, h1_ref, xn2_ref, gates_ref, qkv_ref, top_ref)
+        experts = grad_gates_ref.shape[0]
+        parts = wqkv_ref.shape[0]
+
+        def weight_copies(half):
+            return [
+                pltpu.make_async_copy(hbm.at[half], ref.at[half], weight_sem.at[i, half])
+                for i, (hbm, ref) in enumerate(((wqkv_hbm, wqkv_ref), (wo_hbm, wo_ref)))
+            ]
+
+        for i in (3, 2, 1, 5, 4, 0):
+            start_of_section(*pairs[i], taken[i], taken_sem.at[i])
+
+        def arrived(i):
+            pltpu.make_async_copy(pairs[i][0], taken[i], taken_sem.at[i]).wait()
+            return taken[i]
+
+        gates = arrived(3)[...]
+        grad_gates = grad_gates_ref[...]
+        chosen = gates * (grad_gates - jnp.sum(gates * grad_gates, axis=0, keepdims=True))
+        logits = chosen.astype(jnp.bfloat16)
+        small_ref[0:experts, :] = dot(logits, arrived(2)[...])
+        for copy in weight_copies(0):
+            copy.start()
+        grad_normed = dot(logits, router_ref[...], TN) + rows_ref[...].astype(jnp.float32)
+        middle = arrived(1)[...]
+        grad_middle, gain_grad = norm_back(grad_normed, middle, rms_scale(middle), gain_two_ref[...])
+        small_ref[experts : experts + 1, :] = gain_grad[None, :]
+        grad_middle = grad_middle + arrived(5)[...].astype(jnp.float32)
+        middle_acc[...] = grad_middle
+        mid_ref[...] = grad_middle.astype(jnp.bfloat16)
+        normed_acc[...] = jnp.zeros_like(normed_acc)
+        arrived(4)
+
+        def one(half, carry):
+            for copy in weight_copies(half):
+                copy.wait()
+
+            @pl.when(half + 1 < parts)
+            def _():
+                for copy in weight_copies(half + 1):
+                    copy.start()
+
+            attn_backward_part(
+                group,
+                half,
+                mid_ref,
+                wqkv_ref,
+                wo_ref,
+                (cos_ref[...], -sin_ref[...]),
+                (seg_col_ref[...], seg_row_ref[...]),
+                qkv_ref,
+                dqkv_ref,
+                normed_acc,
+            )
+            return carry
+
+        lax.fori_loop(0, parts, one, 0)
+        rows = arrived(0)[...].astype(jnp.float32)
+        grad_rows, gain_grad = norm_back(normed_acc[...], rows, rms_scale(rows), gain_one_ref[...])
+        grad_in_ref[...] = (grad_rows + middle_acc[...]).astype(jnp.bfloat16)
+        small_ref[experts + 1 : experts + 2, :] = gain_grad[None, :]
+        small_ref[experts + 2 :, :] = jnp.zeros_like(small_ref[experts + 2 :, :])
 
 
 def attn_backward_part(
@@ -1184,7 +1189,9 @@
     normed_acc[...] += dot(dqkv, wqkv_ref[part], NT)
 
 
-def attn_backward(kept, rows, grad_gates, seg, gains, router, wqkv, wo, tables, group):
+def attn_backward(
+    kept, rows, grad_gates, seg, gains, router, wqkv, wo, tables, group, skipped
+):
     length, width = rows.shape
     parts, _, qkv_width = wqkv.shape
     experts = router.shape[0]
@@ -1192,7 +1199,7 @@
     anywhere = pl.BlockSpec(memory_space=pl.ANY)
     dma = pltpu.SemaphoreType.DMA
     return pl.pallas_call(
-        functools.partial(attn_backward_kernel, group),
+        functools.partial(attn_backward_kernel, group, skipped),
         in_specs=[anywhere] * 14 + [vmem] * 9,
         out_specs=[vmem] * 4,
         out_shape=[
@@ -2534,6 +2541,7 @@
     small_out,
     ends_out,
     mine,
+    theirs,
     from_core,
     from_x,
     from_z,
@@ -2554,6 +2562,7 @@
     ends_held,
     ends_came,
     mine_sem,
+    theirs_sem,
     core_send,
     core_recv,
     x_send,
@@ -2594,9 +2603,16 @@
     def mine_copy(half):
         return pltpu.make_async_copy(dense_hbm.at[half, core], mine.at[half], mine_sem.at[half])
 
+    def theirs_copy(half, piece):
+        return pltpu.make_async_copy(
+            dense_hbm.at[half, 1 - core, :, piece],
+            theirs.at[half, :, piece],
+            theirs_sem.at[half, piece],
+        )
+
     def core_copy(half, piece):
         return pltpu.make_async_remote_copy(
-            src_ref=dense_hbm.at[half, 1 - core, :, piece],
+            src_ref=theirs.at[half, :, piece],
             dst_ref=from_core.at[half, :, piece],
             send_sem=core_send.at[half, piece],
             recv_sem=core_recv.at[half, piece],
@@ -2821,9 +2837,9 @@
         for copy in tile_sends(index):
             copy.start()
 
-        @pl.when(index >= 1)
-        def _():
-            sum_tile(index - 1)
+        @pl.when(index >= 2)
+        def _():
+            sum_tile(index - 2)
 
     def tile_run(low, high):
         lax.fori_loop(low, high, lambda index, carry: (one_tile(index), carry)[1], 0)
@@ -2904,6 +2920,9 @@
         at = 1 - x if other else x
         return pltpu.make_async_copy(found.at[m], ends_out.at[m, at], ends_keep.at[m, int(other)])
 
+    for piece in range(TAIL_PIECES):
+        for half in (1 - x, x):
+            theirs_copy(half, piece).start()
     for half in range(2):
         mine_copy(half).start()
     for m in range(2):
@@ -2921,6 +2940,7 @@
 
     def core_start(piece):
         for half in (1 - x, x):
+            theirs_copy(half, piece).wait()
             core_copy(half, piece).start()
 
     for piece in range(2):
@@ -3010,7 +3030,8 @@
     for i in range(steps, steps + 3 * reach):
         late(i)
     tile_run(done, count)
-    sum_tile(count - 1)
+    for index in (count - 2, count - 1):
+        sum_tile(index)
 
     def settle_last(source, carry):
         for piece in range(TAIL_PIECES):
@@ -3096,6 +3117,7 @@
         scratch_shapes=[
             pltpu.VMEM((halves, reach) + block, jnp.bfloat16),
             pltpu.VMEM((halves, reach) + block, jnp.bfloat16),
+            pltpu.VMEM((halves, reach) + block, jnp.bfloat16),
             pltpu.VMEM((reach,) + block, jnp.bfloat16),
             pltpu.VMEM((reach + 1,) + block, jnp.bfloat16),
             pltpu.VMEM((cores, reach) + block, jnp.bfloat16),
@@ -3109,6 +3131,7 @@
         + [pltpu.VMEM((2,) + end, jnp.bfloat16)] * 2
         + [
             dma((halves,)),
+            dma((halves, TAIL_PIECES)),
             dma((halves, TAIL_PIECES)),
             dma((halves, TAIL_PIECES)),
             dma((reach, TAIL_PIECES)),
@@ -3237,6 +3260,7 @@
                 wo,
                 tables,
                 group,
+                0 if tick == micro_count else -1,
             )
         h2, gates, slots, own_gates, picked, gate_pre, up_pre, *firsts = moe_forward_call(
             reach,
@@ -3305,6 +3329,7 @@
             wo,
             tables,
             group,
+            {0: 0, micro_count: 1}.get(tick, -1),
         )
         arrived = shifted(grad_in, SECTION, -1)
         backs.append((grad_in, mid, dqkv, small))

time: 1120 us -> 1090 us (0.973)
  Pallas kernels: 967 us -> 943 us
    pallas_call x5, Pallas kernels: 93.2 us -> 66.2 us  [the longest x3 46.5 us: attn_backward(): pl.pallas_call(functools.partial(attn_backward_kernel, group, skipped), i...]
    pallas_call x1, Pallas kernels: 193 us -> 205 us  [tail_call(): pl.pallas_call(functools.partial(tail_kernel, reach, tiles), in_specs=[an...]
    pallas_call x3, Pallas kernels: 258 us -> 247 us  [moe_backward_call(): pl.pallas_call(functools.partial(moe_backward_kernel, reach, tick, last),...]
  transfers between devices with their start and end apart: 4 -> 4, of which waited for: 1 -> 2; matrix products, arithmetic and copies ran while one was open for 1% -> 1% of each run, Pallas kernels for 14% -> 12%
where the time goes in v2:
time: 1090 us
  Pallas kernels  943 us (87%)
  waiting for transfers between devices  55.9 us (5%)
  other arithmetic  36.4 us (3%)
  local copies, waits for them, and re-layouts  26.5 us (2%)
  starting transfers between devices  23.7 us (2%)
    pallas_call x3, Pallas kernels, moe_forward_call(): pl.pallas_call(functools.partial(moe_forward_kernel, reach, tick, last),...  273 us
    pallas_call x3, Pallas kernels, moe_backward_call(): pl.pallas_call(functools.partial(moe_backward_kernel, reach, tick, last),...  247 us
    pallas_call x1, Pallas kernels, tail_call(): pl.pallas_call(functools.partial(tail_kernel, reach, tiles), in_specs=[an...  205 us
    pallas_call x1, Pallas kernels, both_halves(): pl.pallas_call(functools.partial(both_halves_kernel, chunks), in_specs=[a...  73.8 us
    ppermute x4, waiting for transfers between devices, shifted(): return lax.ppermute(block, axis, route)  55.9 us
    pallas_call x3, Pallas kernels, attn_backward(): pl.pallas_call(functools.partial(attn_backward_kernel, group, skipped), i...  46.5 us
    pallas_call x1, Pallas kernels, attn_split(): pl.pallas_call(functools.partial(attn_split_kernel, group), in_specs=[vme...  26.5 us
    pallas_call x1, Pallas kernels, middle_weights(): pl.pallas_call(middle_weights_kernel, grid=(local, tiles), in_specs=[tile...  26 us
  transfers between devices with their start and end apart: 4, of which 2 were waited for; matrix products, arithmetic and copies ran while one was open for 1% of the time, Pallas kernels for 12%

profile of v2, /device:TPU:25, one launch (start us, length us, event | category | flops | bytes accessed | tf_op | source)
XLA Modules:
  0.0 1087.0 jit_solution(3448550380159768610)
XLA Ops:
  0.7 0.8 fusion.5
  1.5 0.2 broadcast_in_dim_reshape_squeeze.8.seg_col_ref
  1.8 1.5 slice.33
  3.3 1.7 fusion.router_ref.refs_16_
  5.0 0.5 fusion.1
  5.5 0.3 pad_maximum_fusion.1
  5.8 0.0 copy-start
  5.8 0.0 copy-start.13
  5.9 3.4 pad_maximum_fusion.wqkv_ref.refs_1_.wqkv
  9.3 0.6 dynamic-slice_bitcast_fusion.2
  9.9 26.5 %attn_split.1 = (f32[256,1536]{1,0:T(8,128)S(1)}, bf16[256,1536]{1,0:T(8,128)(2,1)S(1)}) custom-call(bf16[2,256,1536]{2,1,0:T(8,128)(2,1)S(1)} %bitcast.64, f32[1,1536]{1,0:T(1,128)S(1)} %copy-done.2, bf16[1536,1280]{1,0:T(8,128)(2,1)} %pad_maximum_fusion.wqkv_ref.refs_1_.wqkv, bf16[768,1536]{1,0:T(8,128)(2,1)} %bitcast.72, ...), custom_call_target="tpu_custom_call" | custom-call | flops 4000000000 | bytes 20000000 | tf_op jit(solution)/shard_map/attn_split/pallas_call | solution.py:886
  36.4 0.0 copy-start.4
  36.4 1.1 copy-done.4
  37.5 0.9 copy-done.5
  38.4 132.8 %moe_forward.3 = (bf16[256,1536]{1,0:T(8,128)(2,1)}, f32[8,32,256]{2,1,0:T(8,128)}, f32[8,8,256]{2,1,0:T(8,128)}, f32[32,256]{1,0:T(8,128)}, bf16[4,4,192,1536]{...) custom-call(bf16[256,1536]{1,0:T(8,128)(2,1)} %copy-done.5, ...), custom_call_target="tpu_custom_call" | custom-call | flops 20000000000 | bytes 45000000 | tf_op jit(solution)/shard_map/moe_forward/pallas_call | solution.py:2089
  171.2 19.8 %collective-permute-start = (bf16[256,1536]{1,0:T(8,128)(2,1)}, bf16[256,1536]{1,0:T(8,128)(2,1)S(1)}, u32[]{:S(2)}, u32[]{:S(2)}) collective-permute-start(bf16[256,1536]{1,0:T(8,128)(2,1)} %get-tuple-element.96.after), channel_id=1, source_target_pairs={{0,16},{1,17},{2,18},{3,19},{4,20},{5,21},{6,22},{7,23},{8,24},{9,... | collective-permute-start | bytes 2359304 | tf_op jit(solution)/shard_map/ppermute | solution.py:25
  191.1 0.1 fusion.4
  191.2 0.0 copy-start.19
  191.3 0.8 copy.36.seg_col_ref
  192.1 0.8 copy.37.seg_col_ref
  192.9 0.8 copy.38.refs_21_
  193.7 0.8 copy.35.seg_col_ref
  194.5 0.8 copy.39.refs_21_
  195.3 0.8 copy.40.refs_21_
  196.0 73.8 %both_halves.1 = (bf16[2,1536,1280]{2,1,0:T(8,128)(2,1)}, bf16[2,768,1536]{2,1,0:T(8,128)(2,1)}) custom-call(bf16[1536,1280]{1,0:T(8,128)(2,1)} %pad_maximum_fusion.wqkv_ref.refs_1_.wqkv, bf16[768,1536]{1,0:T(8,128)(2,1)} %bitcast.74, bf16[256,1536]{1,0:T(8,128)(2,1)} %get-tuple-element.96.after, ...), custom_call_target="tpu_custom_call", output_to_operand_aliasing={{0}: (3, {}), {1}: (4, {})} | custom-call | bytes 30000000 | tf_op jit(solution)/shard_map/both_halves/pallas_call | solution.py:1017
  269.9 2.6 dynamic-slice_bitcast_fusion
  272.5 13.0 %attn_again.1 = (bf16[256,1536]{1,0:T(8,128)(2,1)}, bf16[2,256,1280]{2,1,0:T(8,128)(2,1)}, bf16[2,256,768]{2,1,0:T(8,128)(2,1)}) custom-call(bf16[256,1536]{1,0:T(8,128)(2,1)} %get-tuple-element.178.x_ref.refs_10_.refs_11_.refs_0_, f32[1,1536]{1,0:T(1,128)} %refs_17_.5, bf16[2,1536,1280]{2,1,0:T(8,128)(2,1)} %get-tuple-element.99.wqkv_hbm.refs_12_, ...), custom_call_target="tpu_custom_call" | custom-call | flops 3000000000 | bytes 12000000 | tf_op jit(solution)/shard_map/attn_again/pallas_call | solution.py:794
  285.6 0.9 copy-done.21
  286.4 16.1 %attn_forward.2 = (f32[256,1536]{1,0:T(8,128)}, bf16[256,1536]{1,0:T(8,128)(2,1)}, bf16[2,256,1280]{2,1,0:T(8,128)(2,1)}, bf16[2,256,768]{2,1,0:T(8,128)(2,1)}, bf16[256,1536]{1,0:T(8,128)(2,1)}) custom-call(bf16[256,1536]{1,0:T(8,128)(2,1)} %get-tuple-element.177.x_first.refs_11_.refs_0_.refs_1_, bf16[256,1536]{1,0:T(8,128)(2,1)} %copy-done.21, ...), custom_call_target="tpu_custom_call" | custom-call | flops 4000000000 | bytes 20000000 | tf_op jit(solution)/shard_map/attn_forward/pallas_call | solution.py:723
  302.5 133.9 %moe_forward.4 = (bf16[256,1536]{1,0:T(8,128)(2,1)}, f32[8,32,256]{2,1,0:T(8,128)}, f32[8,8,256]{2,1,0:T(8,128)}, f32[32,256]{1,0:T(8,128)}, bf16[4,4,192,1536]{...) custom-call(bf16[256,1536]{1,0:T(8,128)(2,1)} %get-tuple-element.103.own_ref.refs_4_.refs_5_, ...), custom_call_target="tpu_custom_call" | custom-call | flops 20000000000 | bytes 45000000 | tf_op jit(solution)/shard_map/moe_forward/pallas_call | solution.py:2089
  436.4 1.3 collective-permute-start.1
  437.7 0.9 broadcast_in_dim.48.own_ref
  438.7 4.1 moe_backward.3
  442.8 1.4 reshape.98.refs_15_
  444.1 3.4 attn_backward.3
  447.5 1.3 collective-permute-start.2
  448.8 0.9 copy-done.22
  449.7 3.6 attn_forward.3
  453.3 6.0 moe_forward.5
  459.4 4.4 collective-permute-done.2.own_ref.refs_10_
  463.7 0.9 copy-done.23
  464.6 122.3 %moe_backward.4 = (f32[256,1536]{1,0:T(8,128)}, f32[8,4,256]{2,1,0:T(4,128)}, bf16[4,4,192,1536]{3,2,1,0:T(8,128)(2,1)}, bf16[4,4,192,512]{3,2,1,0:T(8,128)(2,1)...) custom-call(bf16[256,1536]{1,0:T(8,128)(2,1)} %copy-done.23, ...), custom_call_target="tpu_custom_call" | custom-call | flops 20000000000 | bytes 55000000 | tf_op jit(solution)/shard_map/moe_backward/pallas_call | solution.py:2426
  586.9 1.4 reshape.100.refs_15_
  588.3 21.6 %attn_backward.4 = (bf16[256,1536]{1,0:T(8,128)(2,1)}, bf16[256,1536]{1,0:T(8,128)(2,1)}, bf16[2,256,1280]{2,1,0:T(8,128)(2,1)}, f32[40,1536]{1,0:T(8,128)}) custom-call(bf16[256,1536]{1,0:T(8,128)(2,1)} %get-tuple-element.178.x_ref.refs_10_.refs_11_.refs_0_, bf16[256,1536]{1,0:T(8,128)(2,1)} %copy-done.22, f32[256,1536]{1,0:T(8,128)} %copy-done.4, ...), custom_call_target="tpu_custom_call" | custom-call | flops 8000000000 | bytes 20000000 | tf_op jit(solution)/shard_map/attn_backward/pallas_call | solution.py:1201
  609.8 1.3 collective-permute-start.3
  611.1 26.0 %middle_weights.1 = (bf16[4,1536,512]{2,1,0:T(8,128)(2,1)}, bf16[4,1536,512]{2,1,0:T(8,128)(2,1)}, bf16[4,512,1536]{2,1,0:T(8,128)(2,1)}) custom-call(bf16[4,4,192,1536]{3,2,1,0:T(8,128)(2,1)} %get-tuple-element.139.x_first, bf16[4,4,192,1536]{3,2,1,0:T(8,128)(2,1)} %get-tuple-element.140.x_second, bf16[4,4,192,1536]{3,2,1,0:T(8,128)(2,1)} %get-tuple-element.141.dh_ref, ...), custom_call_target="tpu_custom_call" | custom-call | flops 30000001024 | bytes 60000000 | tf_op jit(solution)/shard_map/middle_weights/pallas_call | solution.py:2493
  637.1 51.5 %collective-permute-done.3.own_ref.refs_10_.refs_11_ = bf16[256,1536]{1,0:T(8,128)(2,1)S(1)} collective-permute-done((bf16[256,1536]{1,0:T(8,128)(2,1)}, bf16[256,1536]{1,0:T(8,128)(2,1)S(1)}, u32[]{:S(2)}, u32[]{:S(2)}) %collective-permute-start.3) | collective-permute-done | bytes 786464 | tf_op jit(solution)/shard_map/ppermute | solution.py:25
  688.6 0.9 copy-done.24
  689.5 120.5 %moe_backward.5 = (f32[256,1536]{1,0:T(8,128)}, f32[8,4,256]{2,1,0:T(4,128)}, bf16[4,4,192,1536]{3,2,1,0:T(8,128)(2,1)}, bf16[4,4,192,512]{3,2,1,0:T(8,128)(2,1)...) custom-call(bf16[256,1536]{1,0:T(8,128)(2,1)} %copy-done.24, ...), custom_call_target="tpu_custom_call" | custom-call | flops 20000000000 | bytes 55000000 | tf_op jit(solution)/shard_map/moe_backward/pallas_call | solution.py:2426
  810.0 1.4 reshape.101.refs_15_
  811.4 21.6 %attn_backward.5 = (bf16[256,1536]{1,0:T(8,128)(2,1)}, bf16[256,1536]{1,0:T(8,128)(2,1)}, bf16[2,256,1280]{2,1,0:T(8,128)(2,1)}, f32[40,1536]{1,0:T(8,128)}) custom-call(bf16[256,1536]{1,0:T(8,128)(2,1)} %get-tuple-element.177.x_first.refs_11_.refs_0_.refs_1_, bf16[256,1536]{1,0:T(8,128)(2,1)} %get-tuple-element.177.x_first.refs_11_.refs_0_.refs_1_, ...), custom_call_target="tpu_custom_call" | custom-call | flops 8000000000 | bytes 20000000 | tf_op jit(solution)/shard_map/attn_backward/pallas_call | solution.py:1201
  833.0 13.3 %attn_weights.1 = bf16[2,1536,2048]{2,1,0:T(8,128)(2,1)} custom-call(bf16[256,1536]{1,0:T(8,128)(2,1)} %get-tuple-element.100.refs_0_, bf16[256,1536]{1,0:T(8,128)(2,1)} %get-tuple-element.102.refs_1_, bf16[256,1536]{1,0:T(8,128)(2,1)} %get-tuple-element.106.refs_2_, bf16[2,256,768]{2,1,0:T(8,128)(2,1)} %get-tuple-element.107.refs_3_, ...), custom_call_target="tpu_custom_call" | custom-call | flops 7000000000 | bytes 20000000 | tf_op jit(solution)/shard_map/attn_weights/pallas_call | solution.py:1275
  846.3 204.8 %tail.1 = (bf16[8,4,48,768]{3,2,1,0:T(8,128)(2,1)}, bf16[8,4,48,256]{3,2,1,0:T(8,128)(2,1)}, bf16[8,4,48,256]{3,2,1,0:T(8,128)(2,1)}, bf16[4,4,48,1536]{3,2,1,0:...) custom-call(bf16[2,2,4,4,48,2048]{5,4,3,2,1,0:T(8,128)(2,1)} %bitcas, ...), custom_call_target="tpu_custom_call" | custom-call | flops 60000002048 | bytes 120000000 | tf_op jit(solution)/shard_map/tail/pallas_call | solution.py:3101
  1051.2 1.8 slice_bitcast_fusion
  1052.9 1.5 fusion.3
  1054.4 9.5 bitcast_convert_fusion
  1063.9 6.6 bitcast_convert_fusion.1
  1070.5 6.6 bitcast_convert_fusion.2
  1077.0 2.8 convert.10
  1079.9 2.5 convert.7
  1082.4 1.3 convert.8
  1083.7 1.3 convert.9
  1085.0 0.2 copy-done.6
  1085.2 1.7 copy.44
  (53 shorter events, 0.1 us)
Async XLA Ops:
  0.6 5.2 copy-start.12
  0.7 5.2 copy-start.11
  5.8 4.1 copy-start
  5.8 4.1 copy-start.1
  5.8 3.4 copy-start.13
  5.8 4.0 copy-start.2
  5.8 4.0 copy-start.3
  36.4 1.1 copy-start.4
  37.5 0.9 copy-start.5
  38.4 152.7 %copy-start.14 = (s32[2,512]{1,0:T(2,128)S(1)}, s32[2,512]{1,0:T(2,128)}, u32[]{:S(2)}) copy-start(s32[2,512]{1,0:T(2,128)} %param.14) | copy-start | bytes 12292
  171.2 114.3 %collective-permute-start = (bf16[256,1536]{1,0:T(8,128)(2,1)}, bf16[256,1536]{1,0:T(8,128)(2,1)S(1)}, u32[]{:S(2)}, u32[]{:S(2)}) collective-permute-start(bf16[256,1536]{1,0:T(8,128)(2,1)} %get-tuple-element.96.after), channel_id=1, source_target_pairs={{0,16},{1,17},{2,18},{3,19},{4,20},{5,21},{6,22},{7,23},{8,24},{9,... | collective-permute-start | bytes 2359304 | tf_op jit(solution)/shard_map/ppermute | solution.py:25
  191.2 4.1 copy-start.15
  191.2 78.6 %copy-start.16 = (s32[1,256]{1,0:T(1,128)}, s32[1,256]{1,0:T(1,128)S(1)}, u32[]{:S(2)}) copy-start(s32[1,256]{1,0:T(1,128)S(1)} %get-tuple-element.189.refs_22_) | copy-start | bytes 3076
  191.2 78.6 %copy-start.17 = (s32[1,256]{1,0:T(1,128)}, s32[1,256]{1,0:T(1,128)S(1)}, u32[]{:S(2)}) copy-start(s32[1,256]{1,0:T(1,128)S(1)} %get-tuple-element.186.seg_row_ref) | copy-start | bytes 3076
  191.2 78.6 %copy-start.18 = (s32[1,256]{1,0:T(1,128)}, s32[1,256]{1,0:T(1,128)S(1)}, u32[]{:S(2)}) copy-start(s32[1,256]{1,0:T(1,128)S(1)} %get-tuple-element.185.refs_22_) | copy-start | bytes 3076
  191.2 78.6 %copy-start.19 = (s32[1,256]{1,0:T(1,128)}, s32[1,256]{1,0:T(1,128)S(1)}, u32[]{:S(2)}) copy-start(s32[1,256]{1,0:T(1,128)S(1)} %get-tuple-element.187.seg_row_ref) | copy-start | bytes 3076
  191.2 78.6 %copy-start.20 = (s32[1,256]{1,0:T(1,128)}, s32[1,256]{1,0:T(1,128)S(1)}, u32[]{:S(2)}) copy-start(s32[1,256]{1,0:T(1,128)S(1)} %get-tuple-element.188.seg_row_ref) | copy-start | bytes 3076
  285.5 0.9 copy-start.21
  436.4 12.4 %collective-permute-start.1 = (bf16[256,1536]{1,0:T(8,128)(2,1)}, bf16[256,1536]{1,0:T(8,128)(2,1)S(1)}, u32[]{:S(2)}, u32[]{:S(2)}) collective-permute-start(bf16[256,1536]{1,0:T(8,128)(2,1)} %get-tuple-element.105.ends_forward_one), channel_id=1, source_target_pairs={{0,16},{1,17},{2,18},{3,19},{4,20},{5,21},{6,22},{7,23},{8,24},{9,... | collective-permute-start | bytes 2359304 | tf_op jit(solution)/shard_map/ppermute | solution.py:25
  447.5 16.2 %collective-permute-start.2 = (bf16[256,1536]{1,0:T(8,128)(2,1)}, bf16[256,1536]{1,0:T(8,128)(2,1)S(1)}, u32[]{:S(2)}, u32[]{:S(2)}) collective-permute-start(bf16[256,1536]{1,0:T(8,128)(2,1)} %get-tuple-element.126), channel_id=1, source_target_pairs={{16,0},{17,1},{18,2},{19,3},{20,4},{21,5},{22,6},{23,7},{24,8},{25... | collective-permute-start | bytes 2359304 | tf_op jit(solution)/shard_map/ppermute | solution.py:25
  448.8 0.9 copy-start.22
  463.7 0.9 copy-start.23
  609.8 78.8 %collective-permute-start.3 = (bf16[256,1536]{1,0:T(8,128)(2,1)}, bf16[256,1536]{1,0:T(8,128)(2,1)S(1)}, u32[]{:S(2)}, u32[]{:S(2)}) collective-permute-start(bf16[256,1536]{1,0:T(8,128)(2,1)} %get-tuple-element.138.after.ends_back_one), channel_id=1, source_target_pairs={{16,0},{17,1},{18,2},{19,3},{20,4},{21,5},{22,6},{23,7},{24,8},{25... | collective-permute-start | bytes 2359304 | tf_op jit(solution)/shard_map/ppermute | solution.py:25
  688.6 0.9 copy-start.24
  1051.1 12.7 %slice-start.2 = ((s8[6291456]{0:T(1024)(128)(4,1)}), s8[4194304]{0:T(1024)(128)(4,1)S(1)}, s32[]{:S(2)}) async-start(s8[6291456]{0:T(1024)(128)(4,1)} %bitcast.68), calls=%async_computation.2 | async-start | bytes 8388608
  1054.4 9.5 slice-start.3
  1054.4 16.1 %slice-start = ((s8[6291456]{0:T(1024)(128)(4,1)}), s8[4194304]{0:T(1024)(128)(4,1)S(1)}, s32[]{:S(2)}) async-start(s8[6291456]{0:T(1024)(128)(4,1)} %bitcast.66), calls=%async_computation | async-start | bytes 8388608
  1063.9 6.6 slice-start.1
  1070.5 6.6 copy-start.8
  1077.0 2.8 copy-start.7
  1079.9 2.6 copy-start.10
  1079.9 3.8 copy-start.9
  1082.4 2.7 copy-start.6

commit v3 on v2

--- a/solution.py
+++ b/solution.py
@@ -2163,6 +2163,34 @@
     wd_hbm,
     tops_hbm,
     after,
+    *refs,
+):
+    if tick == last:
+        refs = refs[4:]
+    moe_backward_body(
+        reach,
+        tick,
+        last,
+        own_ref,
+        (slots_first, slots_second),
+        (gates_first, gates_second),
+        (g_first, g_second, u_first, u_second),
+        (wg_hbm, wu_hbm, wd_hbm),
+        tops_hbm,
+        *refs,
+    )
+
+
+def moe_backward_body(
+    reach,
+    tick,
+    last,
+    own_ref,
+    slots_pair,
+    gates_pair,
+    pre_pairs,
+    weights_hbm,
+    tops_hbm,
     out_ref,
     home_gates_ref,
     picked_hbm,
@@ -2202,7 +2230,10 @@
     gate_recv,
     tops_sem,
 ):
-    del after
+    slots_first, slots_second = slots_pair
+    gates_first, gates_second = gates_pair
+    g_first, g_second, u_first, u_second = pre_pairs
+    wg_hbm, wu_hbm, wd_hbm = weights_hbm
     local = wg_ref.shape[0]
     cap = rows_in.shape[2] // 2
     section = lax.axis_index(SECTION)
@@ -2414,7 +2445,7 @@
 
 
 def moe_backward_call(
-    reach, tick, last, own, slots_two, gates_two, g_two, u_two, wg, wu, wd, tops, after
+    reach, tick, last, own, slots_two, gates_two, g_two, u_two, wg, wu, wd, tops, after, over
 ):
     length, width = own.shape
     local, _, hidden = wg.shape
@@ -2425,7 +2456,8 @@
     kept = jax.ShapeDtypeStruct(slot_rows, jnp.bfloat16)
     return pl.pallas_call(
         functools.partial(moe_backward_kernel, reach, tick, last),
-        in_specs=[vmem] * 5 + [anywhere] * 9,
+        in_specs=[vmem] * 5 + [anywhere] * (9 + len(over)),
+        input_output_aliases={14 + i: 2 + i for i in range(len(over))},
         out_specs=[vmem, vmem] + [anywhere] * 4,
         out_shape=[
             jax.ShapeDtypeStruct((length, width), jnp.float32),
@@ -2465,24 +2497,30 @@
             flops=20 * 10**9, bytes_accessed=55 * 10**6, transcendentals=2 * 10**6
         ),
         name="moe_backward",
-    )(own, *slots_two, *gates_two, *g_two, *u_two, wg, wu, wd, tops, after)
-
-
-def middle_weights_kernel(
-    x_first, x_second, dh_ref, gg_ref, gu_ref, hg_ref, after, wg_ref, wu_ref, wd_ref
-):
-    del after
+    )(own, *slots_two, *gates_two, *g_two, *u_two, wg, wu, wd, tops, after, *over)
+
+
+def tick_weights_kernel(sides, *refs):
+    x_refs, (dh_ref, gg_ref, gu_ref, hg_ref, _), refs = (
+        refs[:sides],
+        refs[sides : sides + 5],
+        refs[sides + 5 :],
+    )
+    *before, wg_ref, wu_ref, wd_ref = refs
     hidden = gg_ref.shape[3]
     wide = dh_ref.shape[3]
-    rows = of_section(x_first, x_second).reshape(-1, wide)
-    wg_ref[0] = dot(rows, gg_ref[...].reshape(-1, hidden), TN).astype(jnp.bfloat16)
-    wu_ref[0] = dot(rows, gu_ref[...].reshape(-1, hidden), TN).astype(jnp.bfloat16)
-    wd_ref[0] = dot(
-        hg_ref[...].reshape(-1, hidden), dh_ref[...].reshape(-1, wide), TN
-    ).astype(jnp.bfloat16)
-
-
-def middle_weights(x_two, dh, gg, gu, hg, after):
+    rows = (of_section(*x_refs) if sides == 2 else x_refs[0][...]).reshape(-1, wide)
+    found = (
+        dot(rows, gg_ref[...].reshape(-1, hidden), TN),
+        dot(rows, gu_ref[...].reshape(-1, hidden), TN),
+        dot(hg_ref[...].reshape(-1, hidden), dh_ref[...].reshape(-1, wide), TN),
+    )
+    for i, to in enumerate((wg_ref, wu_ref, wd_ref)):
+        part = found[i] + before[i][0].astype(jnp.float32) if before else found[i]
+        to[0] = part.astype(jnp.bfloat16)
+
+
+def tick_weights(x_sides, dh, gg, gu, hg, after, before=()):
     groups, local, rows, width = dh.shape
     hidden = gg.shape[3]
     tiles = width // hidden
@@ -2490,54 +2528,81 @@
     tiled = pl.BlockSpec((groups, 1, rows, wide), lambda e, t: (0, e, 0, t))
     held = pl.BlockSpec((groups, 1, rows, hidden), lambda e, t: (0, e, 0, 0))
     up = jax.ShapeDtypeStruct((local, width, hidden), jnp.bfloat16)
+    outs = [
+        pl.BlockSpec((1, wide, hidden), lambda e, t: (e, t, 0)),
+        pl.BlockSpec((1, wide, hidden), lambda e, t: (e, t, 0)),
+        pl.BlockSpec((1, hidden, wide), lambda e, t: (e, 0, t)),
+    ]
     return pl.pallas_call(
-        middle_weights_kernel,
+        functools.partial(tick_weights_kernel, len(x_sides)),
         grid=(local, tiles),
-        in_specs=[tiled] * 3 + [held] * 3 + [pl.BlockSpec(memory_space=pl.ANY)],
-        out_specs=[
-            pl.BlockSpec((1, wide, hidden), lambda e, t: (e, t, 0)),
-            pl.BlockSpec((1, wide, hidden), lambda e, t: (e, t, 0)),
-            pl.BlockSpec((1, hidden, wide), lambda e, t: (e, 0, t)),
-        ],
+        in_specs=[tiled] * (len(x_sides) + 1)
+        + [held] * 3
+        + [pl.BlockSpec(memory_space=pl.ANY)]
+        + (outs if before else []),
+        out_specs=outs,
         out_shape=[up, up, jax.ShapeDtypeStruct((local, hidden, width), jnp.bfloat16)],
         compiler_params=pltpu.CompilerParams(vmem_limit_bytes=62 * MIB),
         cost_estimate=pl.CostEstimate(
             flops=30 * 10**9, bytes_accessed=60 * 10**6, transcendentals=0
         ),
-        name="middle_weights",
-    )(*x_two, dh, gg, gu, hg, after)
+        name="tick_weights",
+    )(*x_sides, dh, gg, gu, hg, after, *before)
+
+
+def ends_exchange_kernel(
+    first_hbm, second_hbm, after, out_ref, held, came, load_sem, send_sem, recv_sem
+):
+    del after
+    x = lax.axis_index(TENSOR)
+    aside = {TENSOR: 1 - x}
+    start_of_section(first_hbm, second_hbm, held, load_sem)
+    barrier = pltpu.get_barrier_semaphore()
+    pl.semaphore_signal(barrier, inc=1, device_id=aside, device_id_type=MESH_ID)
+    pl.semaphore_wait(barrier, 1)
+    pltpu.make_async_copy(first_hbm, held, load_sem).wait()
+    copy = pltpu.make_async_remote_copy(
+        src_ref=held,
+        dst_ref=came,
+        send_sem=send_sem,
+        recv_sem=recv_sem,
+        device_id=aside,
+        device_id_type=MESH_ID,
+    )
+    copy.start()
+    out_ref[x] = held[...]
+    copy.wait()
+    out_ref[1 - x] = came[...]
+
+
+def ends_exchange(first, second, after):
+    anywhere = pl.BlockSpec(memory_space=pl.ANY)
+    return pl.pallas_call(
+        ends_exchange_kernel,
+        in_specs=[anywhere] * 3,
+        out_specs=pl.BlockSpec(memory_space=pltpu.VMEM),
+        out_shape=jax.ShapeDtypeStruct((2,) + first.shape, first.dtype),
+        scratch_shapes=[pltpu.VMEM(first.shape, first.dtype)] * 2 + [pltpu.SemaphoreType.DMA] * 3,
+        compiler_params=pltpu.CompilerParams(
+            collective_id=10, has_side_effects=True, vmem_limit_bytes=62 * MIB
+        ),
+        cost_estimate=pl.CostEstimate(flops=0, bytes_accessed=4 * 10**6, transcendentals=0),
+        name="ends_exchange",
+    )(first, second, after)
 
 
 def tail_kernel(
     reach,
-    tiles,
     dense_hbm,
-    x_hbm,
-    dh_first,
-    dh_last,
-    gg_first,
-    gg_last,
-    gu_first,
-    gu_last,
-    hg_first,
-    hg_last,
-    wg_before,
-    wu_before,
-    wd_before,
     small_first,
     small_both,
     small_last,
-    ends_back_one,
-    ends_forward_one,
-    ends_back_two,
-    ends_forward_two,
+    ends_back,
+    ends_forward,
     query_out,
     key_out,
     value_out,
     out_out,
-    wg_out,
-    wu_out,
-    wd_out,
     small_out,
     ends_out,
     mine,
@@ -2546,16 +2611,6 @@
     from_x,
     from_z,
     whole,
-    x_rows,
-    dh_rows,
-    slots,
-    before,
-    wg_tile,
-    wu_tile,
-    wd_tile,
-    wg_from,
-    wu_from,
-    wd_from,
     small_held,
     small_came,
     small_z,
@@ -2574,13 +2629,6 @@
     last_send,
     last_recv,
     out_sem,
-    row_sem,
-    slot_sem,
-    before_sem,
-    tile_sem,
-    tile_send,
-    tile_recv,
-    free_sem,
     small_send,
     small_recv,
     ends_load,
@@ -2595,11 +2643,6 @@
     x = chain.x
     z = chain.z
     quarter = mine.shape[3]
-    local = gg_first.shape[1]
-    width = x_hbm.shape[3]
-    hidden = gg_first.shape[3]
-    wide = width // tiles
-
     def mine_copy(half):
         return pltpu.make_async_copy(dense_hbm.at[half, core], mine.at[half], mine_sem.at[half])
 
@@ -2712,138 +2755,6 @@
             ring_copy(z + distance, piece, 1, chain.above).wait_recv()
             spread_block(z + distance, piece, False, True)
 
-    depth = wg_tile.shape[0]
-
-    def spot(index):
-        expert = index // tiles
-        return expert, pl.ds(pl.multiple_of(lax.rem(index, tiles) * wide, wide), wide)
-
-    def tile_loads(index, first):
-        expert, at = spot(index)
-        slot = lax.rem(index, 2)
-        back = dh_last if first else dh_first
-        return [
-            pltpu.make_async_copy(
-                x_hbm.at[:, expert, :, at], x_rows.at[slot], row_sem.at[slot, 0]
-            ),
-            pltpu.make_async_copy(
-                back.at[:, expert, :, at], dh_rows.at[slot], row_sem.at[slot, 1]
-            ),
-        ] + [
-            pltpu.make_async_copy(ref, before.at[slot, i], before_sem.at[slot, i])
-            for i, ref in enumerate(
-                (wg_before.at[expert, at], wu_before.at[expert, at], wd_before.at[expert, :, at])
-            )
-        ]
-
-    def slot_loads(expert, first):
-        slot = lax.rem(expert, 2)
-        return [
-            pltpu.make_async_copy(
-                (two if first else one).at[:, expert], slots.at[slot, i], slot_sem.at[slot, i]
-            )
-            for i, (one, two) in enumerate(
-                ((gg_first, gg_last), (gu_first, gu_last), (hg_first, hg_last))
-            )
-        ]
-
-    def start(copies):
-        @pl.when(section == 0)
-        def _():
-            for copy in copies(True):
-                copy.start()
-
-        @pl.when(section != 0)
-        def _():
-            for copy in copies(False):
-                copy.start()
-
-    held = ((wg_tile, wg_from), (wu_tile, wu_from), (wd_tile, wd_from))
-
-    def tile_sends(index):
-        slot = lax.rem(index, depth)
-        return [
-            pltpu.make_async_remote_copy(
-                src_ref=tile.at[slot],
-                dst_ref=came.at[slot],
-                send_sem=tile_send.at[slot, i],
-                recv_sem=tile_recv.at[slot, i],
-                device_id=partner,
-                device_id_type=MESH_ID,
-            )
-            for i, (tile, came) in enumerate(held)
-        ]
-
-    def tile_stores(index):
-        expert, at = spot(index)
-        slot = lax.rem(index, depth)
-        outs = (wg_out.at[expert, at], wu_out.at[expert, at], wd_out.at[expert, :, at])
-        return [
-            pltpu.make_async_copy(came.at[slot], out, tile_sem.at[slot, i])
-            for i, ((_, came), out) in enumerate(zip(held, outs))
-        ]
-
-    count = local * tiles
-
-    def sum_tile(index):
-        slot = lax.rem(index, depth)
-        for copy, (tile, came) in zip(tile_sends(index), held):
-            copy.wait_recv()
-            came[slot] = (
-                tile[slot].astype(jnp.float32) + came[slot].astype(jnp.float32)
-            ).astype(jnp.bfloat16)
-        for copy in tile_stores(index):
-            copy.start()
-
-    def one_tile(index):
-        slot = lax.rem(index, 2)
-        expert = index // tiles
-        taken = lax.rem(expert, 2)
-
-        @pl.when(index + 1 < count)
-        def _():
-            start(functools.partial(tile_loads, index + 1))
-
-        @pl.when(jnp.logical_and(lax.rem(index, tiles) == 0, expert + 1 < local))
-        def _():
-            start(functools.partial(slot_loads, expert + 1))
-
-        @pl.when(lax.rem(index, tiles) == 0)
-        def _():
-            for copy in slot_loads(expert, True):
-                copy.wait()
-
-        for copy in tile_loads(index, True):
-            copy.wait()
-
-        @pl.when(index >= depth)
-        def _():
-            for copy in tile_sends(index - depth):
-                copy.wait_send()
-            for copy in tile_stores(index - depth):
-                copy.wait()
-            pl.semaphore_signal(free_sem, inc=1, device_id=partner, device_id_type=MESH_ID)
-            pl.semaphore_wait(free_sem, 1)
-
-        to = lax.rem(index, depth)
-        rows = x_rows[slot].reshape(-1, wide)
-        found = (
-            dot(rows, slots[taken, 0].reshape(-1, hidden), TN),
-            dot(rows, slots[taken, 1].reshape(-1, hidden), TN),
-            dot(slots[taken, 2].reshape(-1, hidden), dh_rows[slot].reshape(-1, wide), TN),
-        )
-        for i, (one, (tile, _)) in enumerate(zip(found, held)):
-            tile[to] = (one + before[slot, i].astype(jnp.float32)).astype(jnp.bfloat16)
-        for copy in tile_sends(index):
-            copy.start()
-
-        @pl.when(index >= 2)
-        def _():
-            sum_tile(index - 2)
-
-    def tile_run(low, high):
-        lax.fori_loop(low, high, lambda index, carry: (one_tile(index), carry)[1], 0)
-
     def small_copy(to, i):
         if i < 2:
             return pltpu.make_async_remote_copy(
@@ -2873,8 +2784,8 @@
     def small_step(stage):
         if stage == 0:
             total = small_both[...] + of_section(small_last, small_first)
-            experts = 2 * reach * local
-            small_held[0, :experts] = pltpu.roll(total[:experts], chain.me * local, 0)
+            experts = (total.shape[0] - 8) // 8 * 8
+            small_held[0, :experts] = pltpu.roll(total[:experts], chain.me * (experts // (2 * reach)), 0)
             small_held[0, experts:] = total[experts:]
             small_copy(partner, 0).start()
         elif stage == 1:
@@ -2903,30 +2814,26 @@
                 total = total + small_z[other]
             small_out[...] = total
 
-    ends_of = ((ends_back_one, ends_forward_one), (ends_back_two, ends_forward_two))
-
-    def ends_copy(m):
+    def ends_copy():
         return pltpu.make_async_remote_copy(
-            src_ref=ends_held.at[m],
-            dst_ref=ends_came.at[m],
-            send_sem=ends_send.at[m],
-            recv_sem=ends_recv.at[m],
+            src_ref=ends_held,
+            dst_ref=ends_came,
+            send_sem=ends_send,
+            recv_sem=ends_recv,
             device_id=chain.aside,
             device_id_type=MESH_ID,
         )
 
-    def ends_store(m, other):
-        found = ends_came if other else ends_held
-        at = 1 - x if other else x
-        return pltpu.make_async_copy(found.at[m], ends_out.at[m, at], ends_keep.at[m, int(other)])
+    def ends_store(other):
+        found, at = (ends_came, 1 - x) if other else (ends_held, x)
+        return pltpu.make_async_copy(found, ends_out.at[at], ends_keep.at[int(other)])
 
     for piece in range(TAIL_PIECES):
         for half in (1 - x, x):
             theirs_copy(half, piece).start()
     for half in range(2):
         mine_copy(half).start()
-    for m in range(2):
-        start_of_section(*ends_of[m], ends_held.at[m], ends_load.at[m])
+    start_of_section(ends_back, ends_forward, ends_held, ends_load)
 
     barrier = pltpu.get_barrier_semaphore()
     pl.semaphore_signal(barrier, inc=1, device_id=partner, device_id_type=MESH_ID)
@@ -2946,12 +2853,8 @@
     for piece in range(2):
         core_start(piece)
     small_step(0)
-    start(functools.partial(slot_loads, 0))
-    start(functools.partial(tile_loads, 0))
-    for m in range(2):
-        pltpu.make_async_copy(ends_of[m][0], ends_held.at[m], ends_load.at[m]).wait()
-        ends_store(m, False).start()
-    ends_copy(0).start()
+    pltpu.make_async_copy(ends_back, ends_held, ends_load).wait()
+    ends_store(False).start()
     for half in range(2):
         mine_copy(half).wait()
 
@@ -3000,10 +2903,6 @@
         def _():
             core_start(piece + 2)
 
-        @pl.when(jnp.logical_and(k > 0, piece * (reach - 1) + reach - 1 - k < count))
-        def _():
-            one_tile(piece * (reach - 1) + reach - 1 - k)
-
         @pl.when(i == reach)
         def _():
             small_step(2)
@@ -3024,15 +2923,10 @@
         return carry
 
     lax.fori_loop(0, steps, step, 0)
-    done = min(count, TAIL_PIECES * (reach - 1))
-    ends_copy(1).start()
+    ends_copy().start()
     small_step(3)
     for i in range(steps, steps + 3 * reach):
         late(i)
-    tile_run(done, count)
-    for index in (count - 2, count - 1):
-        sum_tile(index)
-
     def settle_last(source, carry):
         for piece in range(TAIL_PIECES):
             last_copy(source, piece, 1 - core).wait_recv()
@@ -3041,9 +2935,8 @@
         return carry
 
     lax.fori_loop(0, reach, settle_last, 0)
-    for m in range(2):
-        ends_copy(m).wait_recv()
-        ends_store(m, True).start()
+    ends_copy().wait_recv()
+    ends_store(True).start()
 
     summed.drain()
 
@@ -3068,51 +2961,34 @@
     for piece in range(TAIL_PIECES):
         for half in range(2):
             core_copy(half, piece).wait_send()
-    for m in range(2):
-        ends_copy(m).wait_send()
-        for other in (False, True):
-            ends_store(m, other).wait()
+    ends_copy().wait_send()
+    for other in (False, True):
+        ends_store(other).wait()
     small_copy(partner, 0).wait_send()
     small_copy(chain.aside, 1).wait_send()
     others(lambda other: small_copy(other, 2).wait_send())
-    def settle_tiles(index, carry):
-        for copy in tile_sends(index):
-            copy.wait_send()
-        for copy in tile_stores(index):
-            copy.wait()
-        return carry
-
-    lax.fori_loop(count - depth, count, settle_tiles, 0)
-
-
-def tail_call(reach, widths, dense, x_rows, dh_two, gg_two, gu_two, hg_two, before, smalls, ends):
+
+
+def tail_call(reach, widths, dense, smalls, ends):
     halves, cores, _, _, quarter, columns = dense.shape
-    groups, local, slot_rows, width = x_rows.shape
-    hidden = gg_two[0].shape[3]
-    tiles = width // hidden
-    wide = width // tiles
+    width = ends[0].shape[1]
     anywhere = pl.BlockSpec(memory_space=pl.ANY)
     vmem = pl.BlockSpec(memory_space=pltpu.VMEM)
     end = ends[0].shape
-    up = jax.ShapeDtypeStruct((local, width, hidden), jnp.bfloat16)
-    down = jax.ShapeDtypeStruct((local, hidden, width), jnp.bfloat16)
     block = (TAIL_PIECES, quarter, columns)
     dma = pltpu.SemaphoreType.DMA
     return pl.pallas_call(
-        functools.partial(tail_kernel, reach, tiles),
-        in_specs=[anywhere] * 13 + [vmem] * 3 + [anywhere] * 4,
-        out_specs=[anywhere] * 7 + [vmem, anywhere],
+        functools.partial(tail_kernel, reach),
+        in_specs=[anywhere] + [vmem] * 3 + [anywhere] * 2,
+        out_specs=[anywhere] * 4 + [vmem, anywhere],
         out_shape=[
             jax.ShapeDtypeStruct((cores * reach, TAIL_PIECES, quarter, one), jnp.bfloat16)
             for one in widths
         ]
         + [
             jax.ShapeDtypeStruct((reach, TAIL_PIECES, quarter, width), jnp.bfloat16),
-            up,
-            up,
-            down,
             jax.ShapeDtypeStruct(smalls[0].shape, jnp.float32),
-            jax.ShapeDtypeStruct((2, 2) + end, jnp.bfloat16),
+            jax.ShapeDtypeStruct((2,) + end, jnp.bfloat16),
         ],
         scratch_shapes=[
             pltpu.VMEM((halves, reach) + block, jnp.bfloat16),
@@ -3121,14 +2997,9 @@
             pltpu.VMEM((reach,) + block, jnp.bfloat16),
             pltpu.VMEM((reach + 1,) + block, jnp.bfloat16),
             pltpu.VMEM((cores, reach) + block, jnp.bfloat16),
-            pltpu.VMEM((2, groups, slot_rows, wide), jnp.bfloat16),
-            pltpu.VMEM((2, groups, slot_rows, wide), jnp.bfloat16),
-            pltpu.VMEM((2, 3, groups, slot_rows, hidden), jnp.bfloat16),
-            pltpu.VMEM((2, 3, wide, hidden), jnp.bfloat16),
         ]
-        + [pltpu.VMEM((3, wide, hidden), jnp.bfloat16)] * 6
         + [pltpu.VMEM((count,) + smalls[0].shape, jnp.float32) for count in (2, 2, reach)]
-        + [pltpu.VMEM((2,) + end, jnp.bfloat16)] * 2
+        + [pltpu.VMEM(end, jnp.bfloat16)] * 2
         + [
             dma((halves,)),
             dma((halves, TAIL_PIECES)),
@@ -3143,28 +3014,21 @@
             dma((reach, TAIL_PIECES)),
             dma((reach, TAIL_PIECES)),
             dma((cores, reach, 4)),
-            dma((2, 2)),
-            dma((2, 3)),
-            dma((2, 3)),
-            dma((3, 3)),
-            dma((3, 3)),
-            dma((3, 3)),
-            pltpu.SemaphoreType.REGULAR,
             dma((2 + reach,)),
             dma((2 + reach,)),
+            dma,
             dma((2,)),
-            dma((2, 2)),
-            dma((2,)),
-            dma((2,)),
+            dma,
+            dma,
         ],
         compiler_params=pltpu.CompilerParams(
             collective_id=7, has_side_effects=True, vmem_limit_bytes=62 * MIB
         ),
         cost_estimate=pl.CostEstimate(
-            flops=60 * 10**9, bytes_accessed=120 * 10**6, transcendentals=0
+            flops=10**9, bytes_accessed=300 * 10**6, transcendentals=0
         ),
         name="tail",
-    )(dense, x_rows, *dh_two, *gg_two, *gu_two, *hg_two, *before, *smalls, *ends)
+    )(dense, *smalls, *ends)
 
 
 GROUP = (EXPERT, TENSOR)
@@ -3303,7 +3167,7 @@
             pairs.insert(5, (own_rows[0], own_rows[0]))
         else:
             pairs.insert(5, (arrived, own_rows[1]))
-        rows, grad_gates, picked, gg, gu, hg = moe_backward_call(
+        rows, grad_gates, *found = moe_backward_call(
             reach,
             tick,
             micro_count,
@@ -3316,8 +3180,12 @@
             wu,
             wd,
             tops,
-            before[0] if tick == micro_count else tops,
-        )
+            ends[0] if tick == micro_count else tops,
+            slotted[0] if tick == micro_count else (),
+        )
+        if tick == micro_count:
+            expert_grads = tick_weights([wide[1][0]], *found, rows, before)
+            expert_grads = [lax.psum(one, DP) for one in expert_grads]
         grad_in, mid, dqkv, small = attn_backward(
             pairs[:6],
             rows,
@@ -3333,9 +3201,12 @@
         )
         arrived = shifted(grad_in, SECTION, -1)
         backs.append((grad_in, mid, dqkv, small))
-        slotted.append((picked, gg, gu, hg))
+        slotted.append(found)
         if tick == 1:
-            before = middle_weights([side[0] for side in sides], picked, gg, gu, hg, grad_in)
+            before = tick_weights(
+                [side[0] for side in sides], *found, grad_in
+            )
+            ends = [ends_exchange(grad_in, outputs[1], before[0])]
 
     grads_in, mids, dqkvs, smalls = zip(*backs)
     dense = attn_weights([one[7] for one in kept], [one[8] for one in kept], mids, dqkvs)
@@ -3344,17 +3215,17 @@
         2, 2, reach, TAIL_PIECES, width // (2 * reach * TAIL_PIECES), dense.shape[2]
     )
     widths = [one.shape[2] for one in (query_weight, key_weight, value_weight)]
-    ends = (grads_in[1], outputs[1], grads_in[2], outputs[2])
-    *dense, wg_sum, wu_sum, wd_sum, small, ends = tail_call(
-        reach, widths, dense, wide[1][0], *zip(slotted[0], slotted[2]), before, smalls, ends
-    )
+    *dense, small, last_end = tail_call(
+        reach, widths, dense, smalls, (grads_in[2], outputs[2])
+    )
+    ends = jnp.stack([ends[0], last_end])
     return (
         ends.reshape(1, micro_count, 2 * share_rows, -1),
         small[EXPERTS + 1][None],
         *[one.astype(jnp.float32).reshape(1, -1, one.shape[3]) for one in dense],
         small[EXPERTS][None],
         small[:EXPERTS].T[None],
-        *[one.astype(jnp.float32)[None] for one in (wg_sum, wu_sum, wd_sum)],
+        *[one.astype(jnp.float32)[None] for one in expert_grads],
     )
 
 

time: 1090 us -> 1100 us (level)
  waiting for transfers between devices: 55.9 us -> 41.7 us
  between operations: 1.36 us -> 14.8 us
    ppermute x4, waiting for transfers between devices: 55.9 us -> 41.6 us  [shifted(): return lax.ppermute(block, axis, route)]
    pallas_call x2 -> x4, Pallas kernels: 231 us -> 239 us  [the longest x1 172 us: tail_call(): pl.pallas_call(functools.partial(tail_kernel, reach), in_specs=[anywhere]...]
  transfers between devices with their start and end apart: 4 -> 5, of which waited for: 2 -> 2; matrix products, arithmetic and copies ran while one was open for 1% -> 2% of each run, Pallas kernels for 12% -> 32%
where the time goes in v3:
time: 1100 us; the launch traced here: 1090 us
  Pallas kernels  951 us (86%)
  waiting for transfers between devices  41.7 us (4%)
  other arithmetic  39.2 us (4%)
  starting transfers between devices  23.8 us (2%)
  local copies, waits for them, and re-layouts  23.2 us (2%)
  between operations  14.8 us (1%)
    pallas_call x3, Pallas kernels, moe_forward_call(): pl.pallas_call(functools.partial(moe_forward_kernel, reach, tick, last),...  273 us
    pallas_call x3, Pallas kernels, moe_backward_call(): pl.pallas_call(functools.partial(moe_backward_kernel, reach, tick, last),...  246 us
    pallas_call x1, Pallas kernels, tail_call(): pl.pallas_call(functools.partial(tail_kernel, reach), in_specs=[anywhere]...  172 us
    pallas_call x1, Pallas kernels, both_halves(): pl.pallas_call(functools.partial(both_halves_kernel, chunks), in_specs=[a...  73.8 us
    pallas_call x2, Pallas kernels, tick_weights(): pl.pallas_call(functools.partial(tick_weights_kernel, len(x_sides)), grid...  53.1 us
    pallas_call x3, Pallas kernels, attn_backward(): pl.pallas_call(functools.partial(attn_backward_kernel, group, skipped), i...  46.7 us
    ppermute x4, waiting for transfers between devices, shifted(): return lax.ppermute(block, axis, route)  41.6 us
    pallas_call x1, Pallas kernels, attn_split(): pl.pallas_call(functools.partial(attn_split_kernel, group), in_specs=[vme...  26.5 us
  transfers between devices with their start and end apart: 5, of which 2 were waited for; matrix products, arithmetic and copies ran while one was open for 2% of the time, Pallas kernels for 32%

profile of v3, /device:TPU:25, one launch (start us, length us, event | category | flops | bytes accessed | tf_op | source)
XLA Modules:
  0.0 1093.7 jit_solution(2893692867072637917)
XLA Ops:
  7.2 0.0 all-reduce.3.cloned.1.call-start
  7.3 0.8 fusion.5
  8.1 0.2 broadcast_in_dim_reshape_squeeze.8.seg_col_ref
  8.3 1.5 slice.34
  9.9 0.7 fusion.router_ref.refs_16_
  10.6 0.5 fusion.1
  11.1 0.3 pad_maximum_fusion.2
  11.5 3.4 pad_maximum_fusion.wqkv_ref.refs_1_.wqkv
  14.9 0.6 dynamic-slice_bitcast_fusion.2
  15.5 26.5 %attn_split.1 = (f32[256,1536]{1,0:T(8,128)S(1)}, bf16[256,1536]{1,0:T(8,128)(2,1)S(1)}) custom-call(bf16[2,256,1536]{2,1,0:T(8,128)(2,1)S(1)} %bitcast.59, f32[1,1536]{1,0:T(1,128)S(1)} %copy-done.2, bf16[1536,1280]{1,0:T(8,128)(2,1)} %pad_maximum_fusion.wqkv_ref.refs_1_.wqkv, bf16[768,1536]{1,0:T(8,128)(2,1)} %bitcast.69, ...), custom_call_target="tpu_custom_call" | custom-call | flops 4000000000 | bytes 20000000 | tf_op jit(solution)/shard_map/attn_split/pallas_call | solution.py:886
  42.0 1.1 copy-done.4
  43.2 0.9 copy-done.5
  44.0 132.8 %moe_forward.3 = (bf16[256,1536]{1,0:T(8,128)(2,1)}, f32[8,32,256]{2,1,0:T(8,128)}, f32[8,8,256]{2,1,0:T(8,128)}, f32[32,256]{1,0:T(8,128)}, bf16[4,4,192,1536]{...) custom-call(bf16[256,1536]{1,0:T(8,128)(2,1)} %copy-done.5, ...), custom_call_target="tpu_custom_call" | custom-call | flops 20000000000 | bytes 45000000 | tf_op jit(solution)/shard_map/moe_forward/pallas_call | solution.py:2089
  176.8 19.9 %collective-permute-start = (bf16[256,1536]{1,0:T(8,128)(2,1)}, bf16[256,1536]{1,0:T(8,128)(2,1)S(1)}, u32[]{:S(2)}, u32[]{:S(2)}) collective-permute-start(bf16[256,1536]{1,0:T(8,128)(2,1)} %get-tuple-element.96.after), channel_id=1, source_target_pairs={{0,16},{1,17},{2,18},{3,19},{4,20},{5,21},{6,22},{7,23},{8,24},{9,... | collective-permute-start | bytes 2359304 | tf_op jit(solution)/shard_map/ppermute | solution.py:25
  196.7 0.7 fusion.4
  197.4 0.8 copy.39.seg_col_ref
  198.2 0.8 copy.40.seg_col_ref
  199.0 0.8 copy.42.refs_21_
  199.8 0.8 copy.41.seg_col_ref
  200.6 0.8 copy.43.refs_21_
  201.4 73.8 %both_halves.1 = (bf16[2,1536,1280]{2,1,0:T(8,128)(2,1)}, bf16[2,768,1536]{2,1,0:T(8,128)(2,1)}) custom-call(bf16[1536,1280]{1,0:T(8,128)(2,1)} %pad_maximum_fusion.wqkv_ref.refs_1_.wqkv, bf16[768,1536]{1,0:T(8,128)(2,1)} %bitcast.71, bf16[256,1536]{1,0:T(8,128)(2,1)} %get-tuple-element.96.after, ...), custom_call_target="tpu_custom_call", output_to_operand_aliasing={{0}: (3, {}), {1}: (4, {})} | custom-call | bytes 30000000 | tf_op jit(solution)/shard_map/both_halves/pallas_call | solution.py:1017
  275.3 2.6 dynamic-slice_bitcast_fusion
  277.9 13.1 %attn_again.1 = (bf16[256,1536]{1,0:T(8,128)(2,1)}, bf16[2,256,1280]{2,1,0:T(8,128)(2,1)}, bf16[2,256,768]{2,1,0:T(8,128)(2,1)}) custom-call(bf16[256,1536]{1,0:T(8,128)(2,1)} %get-tuple-element.181.x_ref.refs_10_.refs_11_.refs_0_, f32[1,1536]{1,0:T(1,128)} %refs_17_.5, bf16[2,1536,1280]{2,1,0:T(8,128)(2,1)} %get-tuple-element.99.wqkv_hbm.refs_12_, ...), custom_call_target="tpu_custom_call" | custom-call | flops 3000000000 | bytes 12000000 | tf_op jit(solution)/shard_map/attn_again/pallas_call | solution.py:794
  291.0 0.9 copy-done.25
  291.9 16.1 %attn_forward.2 = (f32[256,1536]{1,0:T(8,128)}, bf16[256,1536]{1,0:T(8,128)(2,1)}, bf16[2,256,1280]{2,1,0:T(8,128)(2,1)}, bf16[2,256,768]{2,1,0:T(8,128)(2,1)}, bf16[256,1536]{1,0:T(8,128)(2,1)}) custom-call(bf16[256,1536]{1,0:T(8,128)(2,1)} %get-tuple-element.180.x_first.refs_11_.refs_0_.refs_1_, bf16[256,1536]{1,0:T(8,128)(2,1)} %copy-done.25, ...), custom_call_target="tpu_custom_call" | custom-call | flops 4000000000 | bytes 20000000 | tf_op jit(solution)/shard_map/attn_forward/pallas_call | solution.py:723
  308.0 133.8 %moe_forward.4 = (bf16[256,1536]{1,0:T(8,128)(2,1)}, f32[8,32,256]{2,1,0:T(8,128)}, f32[8,8,256]{2,1,0:T(8,128)}, f32[32,256]{1,0:T(8,128)}, bf16[4,4,192,1536]{...) custom-call(bf16[256,1536]{1,0:T(8,128)(2,1)} %get-tuple-element.101.own_ref.refs_4_.refs_5_, ...), custom_call_target="tpu_custom_call" | custom-call | flops 20000000000 | bytes 45000000 | tf_op jit(solution)/shard_map/moe_forward/pallas_call | solution.py:2089
  441.8 1.3 collective-permute-start.1
  443.1 0.9 broadcast_in_dim.48.own_ref
  444.0 4.1 moe_backward.3
  448.1 1.4 reshape.101.refs_15_
  449.5 3.3 attn_backward.3
  452.9 1.3 collective-permute-start.2
  454.2 0.9 copy-done.27
  455.1 3.6 attn_forward.3
  458.7 6.0 moe_forward.5
  464.7 4.6 collective-permute-done.2.own_ref.refs_10_
  469.3 0.9 copy-done.28
  470.1 122.5 %moe_backward.4 = (f32[256,1536]{1,0:T(8,128)}, f32[8,4,256]{2,1,0:T(4,128)}, bf16[4,4,192,1536]{3,2,1,0:T(8,128)(2,1)}, bf16[4,4,192,512]{3,2,1,0:T(8,128)(2,1)...) custom-call(bf16[256,1536]{1,0:T(8,128)(2,1)} %copy-done.28, ...), custom_call_target="tpu_custom_call" | custom-call | flops 20000000000 | bytes 55000000 | tf_op jit(solution)/shard_map/moe_backward/pallas_call | solution.py:2457
  592.6 1.4 reshape.102.refs_15_
  594.0 21.6 %attn_backward.4 = (bf16[256,1536]{1,0:T(8,128)(2,1)}, bf16[256,1536]{1,0:T(8,128)(2,1)}, bf16[2,256,1280]{2,1,0:T(8,128)(2,1)}, f32[40,1536]{1,0:T(8,128)}) custom-call(bf16[256,1536]{1,0:T(8,128)(2,1)} %get-tuple-element.181.x_ref.refs_10_.refs_11_.refs_0_, bf16[256,1536]{1,0:T(8,128)(2,1)} %copy-done.27, f32[256,1536]{1,0:T(8,128)} %copy-done.4, ...), custom_call_target="tpu_custom_call" | custom-call | flops 8000000000 | bytes 20000000 | tf_op jit(solution)/shard_map/attn_backward/pallas_call | solution.py:1201
  615.6 1.3 collective-permute-start.3
  616.9 25.9 %tick_weights.2 = (bf16[4,1536,512]{2,1,0:T(8,128)(2,1)}, bf16[4,1536,512]{2,1,0:T(8,128)(2,1)}, bf16[4,512,1536]{2,1,0:T(8,128)(2,1)}) custom-call(bf16[4,4,192,1536]{3,2,1,0:T(8,128)(2,1)} %get-tuple-element.131.refs_0_, bf16[4,4,192,1536]{3,2,1,0:T(8,128)(2,1)} %get-tuple-element.132.refs_1_, bf16[4,4,192,1536]{3,2,1,0:T(8,128)(2,1)} %get-tuple-element.133.refs_2_, ...), custom_call_target="tpu_custom_call" | custom-call | flops 30000001024 | bytes 60000000 | tf_op jit(solution)/shard_map/tick_weights/pallas_call | solution.py:2536
  642.8 14.2 %ends_exchange.1.after = bf16[2,256,1536]{2,1,0:T(8,128)(2,1)} custom-call(bf16[256,1536]{1,0:T(8,128)(2,1)} %get-tuple-element.130.refs_6_.first_hbm, bf16[256,1536]{1,0:T(8,128)(2,1)} %get-tuple-element.103.second_hbm, bf16[4,1536,512]{2,1,0:T(8,128)(2,1)} %get-tuple-element.137.after.refs_6_), custom_call_target="tpu_custom_call" | custom-call | bytes 4000000 | tf_op jit(solution)/shard_map/ends_exchange/pallas_call | solution.py:2580
  657.0 37.1 %collective-permute-done.3.own_ref.refs_10_.refs_11_ = bf16[256,1536]{1,0:T(8,128)(2,1)S(1)} collective-permute-done((bf16[256,1536]{1,0:T(8,128)(2,1)}, bf16[256,1536]{1,0:T(8,128)(2,1)S(1)}, u32[]{:S(2)}, u32[]{:S(2)}) %collective-permute-start.3) | collective-permute-done | bytes 786464 | tf_op jit(solution)/shard_map/ppermute | solution.py:25
  694.1 0.9 copy-done.26
  694.9 119.5 %moe_backward.5 = (f32[256,1536]{1,0:T(8,128)}, f32[8,4,256]{2,1,0:T(4,128)}, bf16[4,4,192,1536]{3,2,1,0:T(8,128)(2,1)}, bf16[4,4,192,512]{3,2,1,0:T(8,128)(2,1)...) custom-call(bf16[256,1536]{1,0:T(8,128)(2,1)} %copy-done.26, ...), custom_call_target="tpu_custom_call", output_to_operand_aliasing={{2}: (14, {}), {3}: (15, {}), {4}: (16, {}), {5}: (17, {})} | custom-call | flops 20000000000 | bytes 55000000 | tf_op jit(solution)/shard_map/moe_backward/pallas_call | solution.py:2457
  814.4 27.2 %tick_weights.3 = (bf16[4,1536,512]{2,1,0:T(8,128)(2,1)}, bf16[4,1536,512]{2,1,0:T(8,128)(2,1)}, bf16[4,512,1536]{2,1,0:T(8,128)(2,1)}) custom-call(bf16[4,4,192,1536]{3,2,1,0:T(8,128)(2,1)} %get-tuple-element.167.refs_0_, bf16[4,4,192,1536]{3,2,1,0:T(8,128)(2,1)} %get-tuple-element.168.refs_1_, bf16[4,4,192,512]{3,2,1,0:T(8,128)(2,1)} %get-tuple-element.169.refs_2_, ...), custom_call_target="tpu_custom_call" | custom-call | flops 30000001024 | bytes 60000000 | tf_op jit(solution)/shard_map/tick_weights/pallas_call | solution.py:2536
  841.6 0.6 copy-done.19
  842.3 0.8 copy.44.refs_21_
  843.1 0.6 reshape.103.refs_15_
  843.7 21.8 %attn_backward.5 = (bf16[256,1536]{1,0:T(8,128)(2,1)}, bf16[256,1536]{1,0:T(8,128)(2,1)}, bf16[2,256,1280]{2,1,0:T(8,128)(2,1)}, f32[40,1536]{1,0:T(8,128)}) custom-call(bf16[256,1536]{1,0:T(8,128)(2,1)} %get-tuple-element.180.x_first.refs_11_.refs_0_.refs_1_, bf16[256,1536]{1,0:T(8,128)(2,1)} %get-tuple-element.180.x_first.refs_11_.refs_0_.refs_1_, ...), custom_call_target="tpu_custom_call" | custom-call | flops 8000000000 | bytes 20000000 | tf_op jit(solution)/shard_map/attn_backward/pallas_call | solution.py:1201
  865.5 13.3 %attn_weights.1 = bf16[2,1536,2048]{2,1,0:T(8,128)(2,1)} custom-call(bf16[256,1536]{1,0:T(8,128)(2,1)} %get-tuple-element.138.refs_0_, bf16[256,1536]{1,0:T(8,128)(2,1)} %get-tuple-element.139.refs_1_, bf16[256,1536]{1,0:T(8,128)(2,1)} %get-tuple-element.140.refs_2_, bf16[2,256,768]{2,1,0:T(8,128)(2,1)} %get-tuple-element.141.refs_3_, ...), custom_call_target="tpu_custom_call" | custom-call | flops 7000000000 | bytes 20000000 | tf_op jit(solution)/shard_map/attn_weights/pallas_call | solution.py:1275
  878.8 172.1 %tail.1 = (bf16[8,4,48,768]{3,2,1,0:T(8,128)(2,1)}, bf16[8,4,48,256]{3,2,1,0:T(8,128)(2,1)}, bf16[8,4,48,256]{3,2,1,0:T(8,128)(2,1)}, bf16[4,4,48,1536]{3,2,1,0:...) custom-call(bf16[2,2,4,4,48,2048]{5,4,3,2,1,0:T(8,128)(2,1)} %bitcast.61, ...), custom_call_target="tpu_custom_call" | custom-call | flops 1000000000 | bytes 300000000 | tf_op jit(solution)/shard_map/tail/pallas_call | solution.py:2980
  1050.9 4.6 convert.10
  1055.5 2.5 convert.7
  1058.1 1.3 convert.8
  1059.4 1.3 convert.9
  1060.6 0.2 copy-done.9
  1060.8 1.9 pad_maximum_fusion.1
  1062.7 0.6 fusion.3
  1063.3 0.7 slice_bitcast_fusion
  1064.0 9.5 broadcast_in_dim.54
  1073.5 6.6 broadcast_in_dim.56
  1080.1 6.6 broadcast_in_dim.58
  (61 shorter events, 0.2 us)
Async XLA Ops:
  7.2 2.7 copy-start.15
  7.2 4.3 copy-start.13
  7.2 4.3 copy-start.12
  7.2 1056.8 %all-reduce.3.cloned.1.call-start = ((), (), s32[]{:S(2)}) async-start(), calls=%async_computation | async-start | bytes 37748736 | tf_op jit(solution)/shard_map/psum | solution.py:3188
  11.4 4.1 copy-start
  11.4 4.1 copy-start.1
  11.5 3.4 copy-start.16
  11.5 4.0 copy-start.2
  11.5 4.0 copy-start.3
  42.0 1.1 copy-start.4
  43.2 0.9 copy-start.5
  44.0 152.7 %copy-start.18 = (s32[2,512]{1,0:T(2,128)S(1)}, s32[2,512]{1,0:T(2,128)}, u32[]{:S(2)}) copy-start(s32[2,512]{1,0:T(2,128)} %param.14) | copy-start | bytes 12292
  176.8 114.2 %collective-permute-start = (bf16[256,1536]{1,0:T(8,128)(2,1)}, bf16[256,1536]{1,0:T(8,128)(2,1)S(1)}, u32[]{:S(2)}, u32[]{:S(2)}) collective-permute-start(bf16[256,1536]{1,0:T(8,128)(2,1)} %get-tuple-element.96.after), channel_id=1, source_target_pairs={{0,16},{1,17},{2,18},{3,19},{4,20},{5,21},{6,22},{7,23},{8,24},{9,... | collective-permute-start | bytes 2359304 | tf_op jit(solution)/shard_map/ppermute | solution.py:25
  197.4 77.8 %copy-start.20 = (s32[1,256]{1,0:T(1,128)}, s32[1,256]{1,0:T(1,128)S(1)}, u32[]{:S(2)}) copy-start(s32[1,256]{1,0:T(1,128)S(1)} %get-tuple-element.192.refs_22_) | copy-start | bytes 3076
  197.4 77.8 %copy-start.21 = (s32[1,256]{1,0:T(1,128)}, s32[1,256]{1,0:T(1,128)S(1)}, u32[]{:S(2)}) copy-start(s32[1,256]{1,0:T(1,128)S(1)} %get-tuple-element.190.seg_row_ref) | copy-start | bytes 3076
  197.4 77.9 %copy-start.22 = (s32[1,256]{1,0:T(1,128)}, s32[1,256]{1,0:T(1,128)S(1)}, u32[]{:S(2)}) copy-start(s32[1,256]{1,0:T(1,128)S(1)} %get-tuple-element.188.refs_22_) | copy-start | bytes 3076
  197.4 77.9 %copy-start.23 = (s32[1,256]{1,0:T(1,128)}, s32[1,256]{1,0:T(1,128)S(1)}, u32[]{:S(2)}) copy-start(s32[1,256]{1,0:T(1,128)S(1)} %get-tuple-element.191.seg_row_ref) | copy-start | bytes 3076
  197.4 77.9 %copy-start.24 = (s32[1,256]{1,0:T(1,128)}, s32[1,256]{1,0:T(1,128)S(1)}, u32[]{:S(2)}) copy-start(s32[1,256]{1,0:T(1,128)S(1)} %get-tuple-element.189.seg_row_ref) | copy-start | bytes 3076
  291.0 0.9 copy-start.25
  441.8 12.4 %collective-permute-start.1 = (bf16[256,1536]{1,0:T(8,128)(2,1)}, bf16[256,1536]{1,0:T(8,128)(2,1)S(1)}, u32[]{:S(2)}, u32[]{:S(2)}) collective-permute-start(bf16[256,1536]{1,0:T(8,128)(2,1)} %get-tuple-element.103.second_hbm), channel_id=1, source_target_pairs={{0,16},{1,17},{2,18},{3,19},{4,20},{5,21},{6,22},{7,23},{8,24},{9,... | collective-permute-start | bytes 2359304 | tf_op jit(solution)/shard_map/ppermute | solution.py:25
  452.9 16.4 %collective-permute-start.2 = (bf16[256,1536]{1,0:T(8,128)(2,1)}, bf16[256,1536]{1,0:T(8,128)(2,1)S(1)}, u32[]{:S(2)}, u32[]{:S(2)}) collective-permute-start(bf16[256,1536]{1,0:T(8,128)(2,1)} %get-tuple-element.119), channel_id=1, source_target_pairs={{16,0},{17,1},{18,2},{19,3},{20,4},{21,5},{22,6},{23,7},{24,8},{25... | collective-permute-start | bytes 2359304 | tf_op jit(solution)/shard_map/ppermute | solution.py:25
  454.2 0.9 copy-start.27
  469.3 0.9 copy-start.28
  615.6 78.5 %collective-permute-start.3 = (bf16[256,1536]{1,0:T(8,128)(2,1)}, bf16[256,1536]{1,0:T(8,128)(2,1)S(1)}, u32[]{:S(2)}, u32[]{:S(2)}) collective-permute-start(bf16[256,1536]{1,0:T(8,128)(2,1)} %get-tuple-element.130.refs_6_.first_hbm), channel_id=1, source_target_pairs={{16,0},{17,1},{18,2},{19,3},{20,4},{21,5},{22,6},{23,7},{24,8},{25... | collective-permute-start | bytes 2359304 | tf_op jit(solution)/shard_map/ppermute | solution.py:25
  694.1 0.9 copy-start.26
  841.6 0.7 copy-start.19
  841.6 1.5 copy-start.17
  1050.9 4.7 copy-start.8
  1055.5 2.6 copy-start.11
  1055.5 3.8 copy-start.10
  1058.1 2.5 copy-start.6
  1058.1 2.7 copy-start.9
  1060.8 1.9 copy-start.14
  1064.0 9.5 copy-start.7
  1064.0 16.1 %slice-start = ((s8[6291456]{0:T(1024)(128)(4,1)}), s8[4194304]{0:T(1024)(128)(4,1)S(1)}, s32[]{:S(2)}) async-start(s8[6291456]{0:T(1024)(128)(4,1)} %bitcast.66), calls=%async_computation.1 | async-start | bytes 8388608
  1073.5 6.6 slice-start.1
Sparse Core Ops, SparseCore 0:
  841.8 101.7 all-reduce.2

commit v4 on v2

--- a/solution.py
+++ b/solution.py
@@ -2508,6 +2508,47 @@
     )(*x_two, dh, gg, gu, hg, after)
 
 
+def ends_exchange_kernel(
+    first_hbm, second_hbm, after, out_ref, held, came, load_sem, send_sem, recv_sem
+):
+    del after
+    x = lax.axis_index(TENSOR)
+    aside = {TENSOR: 1 - x}
+    start_of_section(first_hbm, second_hbm, held, load_sem)
+    barrier = pltpu.get_barrier_semaphore()
+    pl.semaphore_signal(barrier, inc=1, device_id=aside, device_id_type=MESH_ID)
+    pl.semaphore_wait(barrier, 1)
+    pltpu.make_async_copy(first_hbm, held, load_sem).wait()
+    copy = pltpu.make_async_remote_copy(
+        src_ref=held,
+        dst_ref=came,
+        send_sem=send_sem,
+        recv_sem=recv_sem,
+        device_id=aside,
+        device_id_type=MESH_ID,
+    )
+    copy.start()
+    out_ref[x] = held[...]
+    copy.wait()
+    out_ref[1 - x] = came[...]
+
+
+def ends_exchange(first, second, after):
+    anywhere = pl.BlockSpec(memory_space=pl.ANY)
+    return pl.pallas_call(
+        ends_exchange_kernel,
+        in_specs=[anywhere] * 3,
+        out_specs=pl.BlockSpec(memory_space=pltpu.VMEM),
+        out_shape=jax.ShapeDtypeStruct((2,) + first.shape, first.dtype),
+        scratch_shapes=[pltpu.VMEM(first.shape, first.dtype)] * 2 + [pltpu.SemaphoreType.DMA] * 3,
+        compiler_params=pltpu.CompilerParams(
+            collective_id=10, has_side_effects=True, vmem_limit_bytes=62 * MIB
+        ),
+        cost_estimate=pl.CostEstimate(flops=0, bytes_accessed=4 * 10**6, transcendentals=0),
+        name="ends_exchange",
+    )(first, second, after)
+
+
 def tail_kernel(
     reach,
     tiles,
@@ -2527,10 +2568,8 @@
     small_first,
     small_both,
     small_last,
-    ends_back_one,
-    ends_forward_one,
-    ends_back_two,
-    ends_forward_two,
+    ends_back,
+    ends_forward,
     query_out,
     key_out,
     value_out,
@@ -2837,9 +2876,9 @@
         for copy in tile_sends(index):
             copy.start()
 
-        @pl.when(index >= 2)
-        def _():
-            sum_tile(index - 2)
+        @pl.when(index >= 3)
+        def _():
+            sum_tile(index - 3)
 
     def tile_run(low, high):
         lax.fori_loop(low, high, lambda index, carry: (one_tile(index), carry)[1], 0)
@@ -2903,30 +2942,26 @@
                 total = total + small_z[other]
             small_out[...] = total
 
-    ends_of = ((ends_back_one, ends_forward_one), (ends_back_two, ends_forward_two))
-
-    def ends_copy(m):
+    def ends_copy():
         return pltpu.make_async_remote_copy(
-            src_ref=ends_held.at[m],
-            dst_ref=ends_came.at[m],
-            send_sem=ends_send.at[m],
-            recv_sem=ends_recv.at[m],
+            src_ref=ends_held,
+            dst_ref=ends_came,
+            send_sem=ends_send,
+            recv_sem=ends_recv,
             device_id=chain.aside,
             device_id_type=MESH_ID,
         )
 
-    def ends_store(m, other):
-        found = ends_came if other else ends_held
-        at = 1 - x if other else x
-        return pltpu.make_async_copy(found.at[m], ends_out.at[m, at], ends_keep.at[m, int(other)])
+    def ends_store(other):
+        found, at = (ends_came, 1 - x) if other else (ends_held, x)
+        return pltpu.make_async_copy(found, ends_out.at[at], ends_keep.at[int(other)])
 
     for piece in range(TAIL_PIECES):
         for half in (1 - x, x):
             theirs_copy(half, piece).start()
     for half in range(2):
         mine_copy(half).start()
-    for m in range(2):
-        start_of_section(*ends_of[m], ends_held.at[m], ends_load.at[m])
+    start_of_section(ends_back, ends_forward, ends_held, ends_load)
 
     barrier = pltpu.get_barrier_semaphore()
     pl.semaphore_signal(barrier, inc=1, device_id=partner, device_id_type=MESH_ID)
@@ -2948,10 +2983,8 @@
     small_step(0)
     start(functools.partial(slot_loads, 0))
     start(functools.partial(tile_loads, 0))
-    for m in range(2):
-        pltpu.make_async_copy(ends_of[m][0], ends_held.at[m], ends_load.at[m]).wait()
-        ends_store(m, False).start()
-    ends_copy(0).start()
+    pltpu.make_async_copy(ends_back, ends_held, ends_load).wait()
+    ends_store(False).start()
     for half in range(2):
         mine_copy(half).wait()
 
@@ -2991,15 +3024,13 @@
 
     for i in range(ahead):
         launch(i)
+    for piece in range(2, TAIL_PIECES):
+        core_start(piece)
     small_step(1)
 
     def step(i, carry):
         k, piece = place(i)
 
-        @pl.when(jnp.logical_and(k == reach - 1, piece + 2 < TAIL_PIECES))
-        def _():
-            core_start(piece + 2)
-
         @pl.when(jnp.logical_and(k > 0, piece * (reach - 1) + reach - 1 - k < count))
         def _():
             one_tile(piece * (reach - 1) + reach - 1 - k)
@@ -3025,12 +3056,12 @@
 
     lax.fori_loop(0, steps, step, 0)
     done = min(count, TAIL_PIECES * (reach - 1))
-    ends_copy(1).start()
+    ends_copy().start()
     small_step(3)
     for i in range(steps, steps + 3 * reach):
         late(i)
     tile_run(done, count)
-    for index in (count - 2, count - 1):
+    for index in range(count - 3, count):
         sum_tile(index)
 
     def settle_last(source, carry):
@@ -3041,9 +3072,8 @@
         return carry
 
     lax.fori_loop(0, reach, settle_last, 0)
-    for m in range(2):
-        ends_copy(m).wait_recv()
-        ends_store(m, True).start()
+    ends_copy().wait_recv()
+    ends_store(True).start()
 
     summed.drain()
 
@@ -3068,10 +3098,9 @@
     for piece in range(TAIL_PIECES):
         for half in range(2):
             core_copy(half, piece).wait_send()
-    for m in range(2):
-        ends_copy(m).wait_send()
-        for other in (False, True):
-            ends_store(m, other).wait()
+    ends_copy().wait_send()
+    for other in (False, True):
+        ends_store(other).wait()
     small_copy(partner, 0).wait_send()
     small_copy(chain.aside, 1).wait_send()
     others(lambda other: small_copy(other, 2).wait_send())
@@ -3100,7 +3129,7 @@
     dma = pltpu.SemaphoreType.DMA
     return pl.pallas_call(
         functools.partial(tail_kernel, reach, tiles),
-        in_specs=[anywhere] * 13 + [vmem] * 3 + [anywhere] * 4,
+        in_specs=[anywhere] * 13 + [vmem] * 3 + [anywhere] * 2,
         out_specs=[anywhere] * 7 + [vmem, anywhere],
         out_shape=[
             jax.ShapeDtypeStruct((cores * reach, TAIL_PIECES, quarter, one), jnp.bfloat16)
@@ -3112,7 +3141,7 @@
             up,
             down,
             jax.ShapeDtypeStruct(smalls[0].shape, jnp.float32),
-            jax.ShapeDtypeStruct((2, 2) + end, jnp.bfloat16),
+            jax.ShapeDtypeStruct((2,) + end, jnp.bfloat16),
         ],
         scratch_shapes=[
             pltpu.VMEM((halves, reach) + block, jnp.bfloat16),
@@ -3126,9 +3155,9 @@
             pltpu.VMEM((2, 3, groups, slot_rows, hidden), jnp.bfloat16),
             pltpu.VMEM((2, 3, wide, hidden), jnp.bfloat16),
         ]
-        + [pltpu.VMEM((3, wide, hidden), jnp.bfloat16)] * 6
+        + [pltpu.VMEM((4, wide, hidden), jnp.bfloat16)] * 6
         + [pltpu.VMEM((count,) + smalls[0].shape, jnp.float32) for count in (2, 2, reach)]
-        + [pltpu.VMEM((2,) + end, jnp.bfloat16)] * 2
+        + [pltpu.VMEM(end, jnp.bfloat16)] * 2
         + [
             dma((halves,)),
             dma((halves, TAIL_PIECES)),
@@ -3146,16 +3175,16 @@
             dma((2, 2)),
             dma((2, 3)),
             dma((2, 3)),
-            dma((3, 3)),
-            dma((3, 3)),
-            dma((3, 3)),
+            dma((4, 3)),
+            dma((4, 3)),
+            dma((4, 3)),
             pltpu.SemaphoreType.REGULAR,
             dma((2 + reach,)),
             dma((2 + reach,)),
+            dma,
             dma((2,)),
-            dma((2, 2)),
-            dma((2,)),
-            dma((2,)),
+            dma,
+            dma,
         ],
         compiler_params=pltpu.CompilerParams(
             collective_id=7, has_side_effects=True, vmem_limit_bytes=62 * MIB
@@ -3316,7 +3345,7 @@
             wu,
             wd,
             tops,
-            before[0] if tick == micro_count else tops,
+            first_end if tick == micro_count else tops,
         )
         grad_in, mid, dqkv, small = attn_backward(
             pairs[:6],
@@ -3336,6 +3365,7 @@
         slotted.append((picked, gg, gu, hg))
         if tick == 1:
             before = middle_weights([side[0] for side in sides], picked, gg, gu, hg, grad_in)
+            first_end = ends_exchange(grad_in, outputs[1], before[0])
 
     grads_in, mids, dqkvs, smalls = zip(*backs)
     dense = attn_weights([one[7] for one in kept], [one[8] for one in kept], mids, dqkvs)
@@ -3344,12 +3374,12 @@
         2, 2, reach, TAIL_PIECES, width // (2 * reach * TAIL_PIECES), dense.shape[2]
     )
     widths = [one.shape[2] for one in (query_weight, key_weight, value_weight)]
-    ends = (grads_in[1], outputs[1], grads_in[2], outputs[2])
-    *dense, wg_sum, wu_sum, wd_sum, small, ends = tail_call(
+    ends = (grads_in[2], outputs[2])
+    *dense, wg_sum, wu_sum, wd_sum, small, last_end = tail_call(
         reach, widths, dense, wide[1][0], *zip(slotted[0], slotted[2]), before, smalls, ends
     )
     return (
-        ends.reshape(1, micro_count, 2 * share_rows, -1),
+        jnp.stack([first_end, last_end]).reshape(1, micro_count, 2 * share_rows, -1),
         small[EXPERTS + 1][None],
         *[one.astype(jnp.float32).reshape(1, -1, one.shape[3]) for one in dense],
         small[EXPERTS][None],

time: 1090 us -> 1070 us (0.982)
  waiting for transfers between devices: 55.9 us -> 41.5 us
    pallas_call x1, Pallas kernels: 205 us -> 188 us  [tail_call(): pl.pallas_call(functools.partial(tail_kernel, reach, tiles), in_specs=[an...]
    ppermute x4, waiting for transfers between devices: 55.9 us -> 41.5 us  [shifted(): return lax.ppermute(block, axis, route)]
    pallas_call x0 -> x1, Pallas kernels: none -> 14.3 us  [ends_exchange(): pl.pallas_call(ends_exchange_kernel, in_specs=[anywhere] * 3, out_specs=p...]
  transfers between devices with their start and end apart: 4 -> 4, of which waited for: 2 -> 2; matrix products, arithmetic and copies ran while one was open for 1% -> 1% of each run, Pallas kernels for 12% -> 13%
where the time goes in v4:
time: 1070 us
  Pallas kernels  940 us (88%)
  waiting for transfers between devices  41.5 us (4%)
  other arithmetic  37.4 us (3%)
  local copies, waits for them, and re-layouts  24.8 us (2%)
  starting transfers between devices  23.8 us (2%)
    pallas_call x3, Pallas kernels, moe_forward_call(): pl.pallas_call(functools.partial(moe_forward_kernel, reach, tick, last),...  273 us
    pallas_call x3, Pallas kernels, moe_backward_call(): pl.pallas_call(functools.partial(moe_backward_kernel, reach, tick, last),...  245 us
    pallas_call x1, Pallas kernels, tail_call(): pl.pallas_call(functools.partial(tail_kernel, reach, tiles), in_specs=[an...  188 us
    pallas_call x1, Pallas kernels, both_halves(): pl.pallas_call(functools.partial(both_halves_kernel, chunks), in_specs=[a...  73.8 us
    pallas_call x3, Pallas kernels, attn_backward(): pl.pallas_call(functools.partial(attn_backward_kernel, group, skipped), i...  46.5 us
    ppermute x4, waiting for transfers between devices, shifted(): return lax.ppermute(block, axis, route)  41.5 us
    pallas_call x1, Pallas kernels, attn_split(): pl.pallas_call(functools.partial(attn_split_kernel, group), in_specs=[vme...  26.5 us
    pallas_call x1, Pallas kernels, middle_weights(): pl.pallas_call(middle_weights_kernel, grid=(local, tiles), in_specs=[tile...  26 us
  transfers between devices with their start and end apart: 4, of which 2 were waited for; matrix products, arithmetic and copies ran while one was open for 1% of the time, Pallas kernels for 13%

profile of v4, /device:TPU:25, one launch (start us, length us, event | category | flops | bytes accessed | tf_op | source)
XLA Modules:
  0.0 1068.4 jit_solution(11479503802584873705)
XLA Ops:
  0.7 0.8 fusion.5
  1.6 0.2 broadcast_in_dim_reshape_squeeze.8.seg_col_ref
  1.8 1.5 slice.34
  3.3 0.7 fusion.router_ref.refs_16_
  4.0 0.5 fusion.1
  4.6 0.3 pad_maximum_fusion.2
  4.8 0.0 copy-start
  4.9 0.0 copy-start.15
  4.9 3.4 pad_maximum_fusion.wqkv_ref.refs_1_.wqkv
  8.3 0.6 dynamic-slice_bitcast_fusion.2
  9.0 26.5 %attn_split.1 = (f32[256,1536]{1,0:T(8,128)S(1)}, bf16[256,1536]{1,0:T(8,128)(2,1)S(1)}) custom-call(bf16[2,256,1536]{2,1,0:T(8,128)(2,1)S(1)} %bitcast.65, f32[1,1536]{1,0:T(1,128)S(1)} %copy-done.2, bf16[1536,1280]{1,0:T(8,128)(2,1)} %pad_maximum_fusion.wqkv_ref.refs_1_.wqkv, bf16[768,1536]{1,0:T(8,128)(2,1)} %bitcast.73, ...), custom_call_target="tpu_custom_call" | custom-call | flops 4000000000 | bytes 20000000 | tf_op jit(solution)/shard_map/attn_split/pallas_call | solution.py:886
  35.5 1.1 copy-done.4
  36.6 0.9 copy-done.5
  37.5 132.8 %moe_forward.3 = (bf16[256,1536]{1,0:T(8,128)(2,1)}, f32[8,32,256]{2,1,0:T(8,128)}, f32[8,8,256]{2,1,0:T(8,128)}, f32[32,256]{1,0:T(8,128)}, bf16[4,4,192,1536]{...) custom-call(bf16[256,1536]{1,0:T(8,128)(2,1)} %copy-done.5, ...), custom_call_target="tpu_custom_call" | custom-call | flops 20000000000 | bytes 45000000 | tf_op jit(solution)/shard_map/moe_forward/pallas_call | solution.py:2089
  170.3 19.9 %collective-permute-start = (bf16[256,1536]{1,0:T(8,128)(2,1)}, bf16[256,1536]{1,0:T(8,128)(2,1)S(1)}, u32[]{:S(2)}, u32[]{:S(2)}) collective-permute-start(bf16[256,1536]{1,0:T(8,128)(2,1)} %get-tuple-element.96.after), channel_id=1, source_target_pairs={{0,16},{1,17},{2,18},{3,19},{4,20},{5,21},{6,22},{7,23},{8,24},{9,... | collective-permute-start | bytes 2359304 | tf_op jit(solution)/shard_map/ppermute | solution.py:25
  190.2 0.1 fusion.4
  190.3 0.0 copy-start.21
  190.4 0.8 copy.35.seg_col_ref
  191.2 0.8 copy.36.seg_col_ref
  192.0 0.8 copy.38.refs_21_
  192.8 0.8 copy.37.seg_col_ref
  193.6 0.8 copy.39.refs_21_
  194.4 0.8 copy.40.refs_21_
  195.2 73.8 %both_halves.1 = (bf16[2,1536,1280]{2,1,0:T(8,128)(2,1)}, bf16[2,768,1536]{2,1,0:T(8,128)(2,1)}) custom-call(bf16[1536,1280]{1,0:T(8,128)(2,1)} %pad_maximum_fusion.wqkv_ref.refs_1_.wqkv, bf16[768,1536]{1,0:T(8,128)(2,1)} %bitcast.75, bf16[256,1536]{1,0:T(8,128)(2,1)} %get-tuple-element.96.after, ...), custom_call_target="tpu_custom_call", output_to_operand_aliasing={{0}: (3, {}), {1}: (4, {})} | custom-call | bytes 30000000 | tf_op jit(solution)/shard_map/both_halves/pallas_call | solution.py:1017
  269.0 2.6 dynamic-slice_bitcast_fusion
  271.6 13.1 %attn_again.1 = (bf16[256,1536]{1,0:T(8,128)(2,1)}, bf16[2,256,1280]{2,1,0:T(8,128)(2,1)}, bf16[2,256,768]{2,1,0:T(8,128)(2,1)}) custom-call(bf16[256,1536]{1,0:T(8,128)(2,1)} %get-tuple-element.178.x_ref.refs_10_.refs_11_.refs_0_, f32[1,1536]{1,0:T(1,128)} %refs_17_.5, bf16[2,1536,1280]{2,1,0:T(8,128)(2,1)} %get-tuple-element.99.wqkv_hbm.refs_12_, ...), custom_call_target="tpu_custom_call" | custom-call | flops 3000000000 | bytes 12000000 | tf_op jit(solution)/shard_map/attn_again/pallas_call | solution.py:794
  284.7 0.9 copy-done.23
  285.6 16.1 %attn_forward.2 = (f32[256,1536]{1,0:T(8,128)}, bf16[256,1536]{1,0:T(8,128)(2,1)}, bf16[2,256,1280]{2,1,0:T(8,128)(2,1)}, bf16[2,256,768]{2,1,0:T(8,128)(2,1)}, bf16[256,1536]{1,0:T(8,128)(2,1)}) custom-call(bf16[256,1536]{1,0:T(8,128)(2,1)} %get-tuple-element.177.x_first.refs_11_.refs_0_.refs_1_, bf16[256,1536]{1,0:T(8,128)(2,1)} %copy-done.23, ...), custom_call_target="tpu_custom_call" | custom-call | flops 4000000000 | bytes 20000000 | tf_op jit(solution)/shard_map/attn_forward/pallas_call | solution.py:723
  301.7 133.9 %moe_forward.4 = (bf16[256,1536]{1,0:T(8,128)(2,1)}, f32[8,32,256]{2,1,0:T(8,128)}, f32[8,8,256]{2,1,0:T(8,128)}, f32[32,256]{1,0:T(8,128)}, bf16[4,4,192,1536]{...) custom-call(bf16[256,1536]{1,0:T(8,128)(2,1)} %get-tuple-element.101.own_ref.refs_4_.refs_5_, ...), custom_call_target="tpu_custom_call" | custom-call | flops 20000000000 | bytes 45000000 | tf_op jit(solution)/shard_map/moe_forward/pallas_call | solution.py:2089
  435.6 1.3 collective-permute-start.1
  436.9 0.9 broadcast_in_dim.48.own_ref
  437.8 4.1 moe_backward.3
  441.9 1.4 reshape.101.refs_15_
  443.3 3.3 attn_backward.3
  446.6 1.3 collective-permute-start.2
  448.0 0.9 copy-done.24
  448.9 3.6 attn_forward.3
  452.5 6.0 moe_forward.5
  458.5 4.3 collective-permute-done.2.own_ref.refs_10_
  462.8 0.9 copy-done.25
  463.7 122.1 %moe_backward.4 = (f32[256,1536]{1,0:T(8,128)}, f32[8,4,256]{2,1,0:T(4,128)}, bf16[4,4,192,1536]{3,2,1,0:T(8,128)(2,1)}, bf16[4,4,192,512]{3,2,1,0:T(8,128)(2,1)...) custom-call(bf16[256,1536]{1,0:T(8,128)(2,1)} %copy-done.25, ...), custom_call_target="tpu_custom_call" | custom-call | flops 20000000000 | bytes 55000000 | tf_op jit(solution)/shard_map/moe_backward/pallas_call | solution.py:2426
  585.8 1.4 reshape.102.refs_15_
  587.1 21.6 %attn_backward.4 = (bf16[256,1536]{1,0:T(8,128)(2,1)}, bf16[256,1536]{1,0:T(8,128)(2,1)}, bf16[2,256,1280]{2,1,0:T(8,128)(2,1)}, f32[40,1536]{1,0:T(8,128)}) custom-call(bf16[256,1536]{1,0:T(8,128)(2,1)} %get-tuple-element.178.x_ref.refs_10_.refs_11_.refs_0_, bf16[256,1536]{1,0:T(8,128)(2,1)} %copy-done.24, f32[256,1536]{1,0:T(8,128)} %copy-done.4, ...), custom_call_target="tpu_custom_call" | custom-call | flops 8000000000 | bytes 20000000 | tf_op jit(solution)/shard_map/attn_backward/pallas_call | solution.py:1201
  608.7 1.3 collective-permute-start.3
  610.0 26.0 %middle_weights.1 = (bf16[4,1536,512]{2,1,0:T(8,128)(2,1)}, bf16[4,1536,512]{2,1,0:T(8,128)(2,1)}, bf16[4,512,1536]{2,1,0:T(8,128)(2,1)}) custom-call(bf16[4,4,192,1536]{3,2,1,0:T(8,128)(2,1)} %get-tuple-element.131.x_first, bf16[4,4,192,1536]{3,2,1,0:T(8,128)(2,1)} %get-tuple-element.132.x_second, bf16[4,4,192,1536]{3,2,1,0:T(8,128)(2,1)} %get-tuple-element.133.dh_ref, ...), custom_call_target="tpu_custom_call" | custom-call | flops 30000001024 | bytes 60000000 | tf_op jit(solution)/shard_map/middle_weights/pallas_call | solution.py:2493
  636.0 14.3 %ends_exchange.1.after = bf16[2,256,1536]{2,1,0:T(8,128)(2,1)} custom-call(bf16[256,1536]{1,0:T(8,128)(2,1)} %get-tuple-element.130.after.first_hbm, bf16[256,1536]{1,0:T(8,128)(2,1)} %get-tuple-element.103.second_hbm, bf16[4,1536,512]{2,1,0:T(8,128)(2,1)} %get-tuple-element.137.after.wg_before), custom_call_target="tpu_custom_call" | custom-call | bytes 4000000 | tf_op jit(solution)/shard_map/ends_exchange/pallas_call | solution.py:2538
  650.3 37.1 %collective-permute-done.3.own_ref.refs_10_.refs_11_ = bf16[256,1536]{1,0:T(8,128)(2,1)S(1)} collective-permute-done((bf16[256,1536]{1,0:T(8,128)(2,1)}, bf16[256,1536]{1,0:T(8,128)(2,1)S(1)}, u32[]{:S(2)}, u32[]{:S(2)}) %collective-permute-start.3) | collective-permute-done | bytes 786464 | tf_op jit(solution)/shard_map/ppermute | solution.py:25
  687.5 0.9 copy-done.26
  688.3 119.1 %moe_backward.5 = (f32[256,1536]{1,0:T(8,128)}, f32[8,4,256]{2,1,0:T(4,128)}, bf16[4,4,192,1536]{3,2,1,0:T(8,128)(2,1)}, bf16[4,4,192,512]{3,2,1,0:T(8,128)(2,1)...) custom-call(bf16[256,1536]{1,0:T(8,128)(2,1)} %copy-done.26, ...), custom_call_target="tpu_custom_call" | custom-call | flops 20000000000 | bytes 55000000 | tf_op jit(solution)/shard_map/moe_backward/pallas_call | solution.py:2426
  807.5 1.4 reshape.103.refs_15_
  808.9 21.6 %attn_backward.5 = (bf16[256,1536]{1,0:T(8,128)(2,1)}, bf16[256,1536]{1,0:T(8,128)(2,1)}, bf16[2,256,1280]{2,1,0:T(8,128)(2,1)}, f32[40,1536]{1,0:T(8,128)}) custom-call(bf16[256,1536]{1,0:T(8,128)(2,1)} %get-tuple-element.177.x_first.refs_11_.refs_0_.refs_1_, bf16[256,1536]{1,0:T(8,128)(2,1)} %get-tuple-element.177.x_first.refs_11_.refs_0_.refs_1_, ...), custom_call_target="tpu_custom_call" | custom-call | flops 8000000000 | bytes 20000000 | tf_op jit(solution)/shard_map/attn_backward/pallas_call | solution.py:1201
  830.5 13.3 %attn_weights.1 = bf16[2,1536,2048]{2,1,0:T(8,128)(2,1)} custom-call(bf16[256,1536]{1,0:T(8,128)(2,1)} %get-tuple-element.138.refs_0_, bf16[256,1536]{1,0:T(8,128)(2,1)} %get-tuple-element.139.refs_1_, bf16[256,1536]{1,0:T(8,128)(2,1)} %get-tuple-element.140.refs_2_, bf16[2,256,768]{2,1,0:T(8,128)(2,1)} %get-tuple-element.141.refs_3_, ...), custom_call_target="tpu_custom_call" | custom-call | flops 7000000000 | bytes 20000000 | tf_op jit(solution)/shard_map/attn_weights/pallas_call | solution.py:1275
  843.8 188.5 %tail.1 = (bf16[8,4,48,768]{3,2,1,0:T(8,128)(2,1)}, bf16[8,4,48,256]{3,2,1,0:T(8,128)(2,1)}, bf16[8,4,48,256]{3,2,1,0:T(8,128)(2,1)}, bf16[4,4,48,1536]{3,2,1,0:...) custom-call(bf16[2,2,4,4,48,2048]{5,4,3,2,1,0:T(8,128)(2,1)} %bitcas, ...), custom_call_target="tpu_custom_call" | custom-call | flops 60000002048 | bytes 120000000 | tf_op jit(solution)/shard_map/tail/pallas_call | solution.py:3130
  1032.3 1.8 slice_bitcast_fusion
  1034.0 1.5 fusion.3
  1035.5 9.5 bitcast_convert_fusion
  1045.0 6.6 bitcast_convert_fusion.1
  1051.6 6.6 bitcast_convert_fusion.2
  1058.2 2.8 convert.10
  1061.0 2.5 convert.7
  1063.5 1.3 convert.8
  1064.8 1.3 convert.9
  1066.1 0.2 copy-done.9
  1066.3 1.9 pad_maximum_fusion.1
  (58 shorter events, 0.1 us)
Async XLA Ops:
  0.6 2.7 copy-start.14
  0.7 4.2 copy-start.13
  0.7 4.2 copy-start.12
  4.8 4.1 copy-start
  4.9 4.1 copy-start.1
  4.9 3.4 copy-start.15
  4.9 4.0 copy-start.2
  4.9 4.0 copy-start.3
  35.4 1.1 copy-start.4
  36.6 0.9 copy-start.5
  37.5 152.7 %copy-start.16 = (s32[2,512]{1,0:T(2,128)S(1)}, s32[2,512]{1,0:T(2,128)}, u32[]{:S(2)}) copy-start(s32[2,512]{1,0:T(2,128)} %param.14) | copy-start | bytes 12292
  170.3 114.4 %collective-permute-start = (bf16[256,1536]{1,0:T(8,128)(2,1)}, bf16[256,1536]{1,0:T(8,128)(2,1)S(1)}, u32[]{:S(2)}, u32[]{:S(2)}) collective-permute-start(bf16[256,1536]{1,0:T(8,128)(2,1)} %get-tuple-element.96.after), channel_id=1, source_target_pairs={{0,16},{1,17},{2,18},{3,19},{4,20},{5,21},{6,22},{7,23},{8,24},{9,... | collective-permute-start | bytes 2359304 | tf_op jit(solution)/shard_map/ppermute | solution.py:25
  190.3 4.1 copy-start.17
  190.3 78.6 %copy-start.18 = (s32[1,256]{1,0:T(1,128)}, s32[1,256]{1,0:T(1,128)S(1)}, u32[]{:S(2)}) copy-start(s32[1,256]{1,0:T(1,128)S(1)} %get-tuple-element.189.refs_22_) | copy-start | bytes 3076
  190.3 78.6 %copy-start.19 = (s32[1,256]{1,0:T(1,128)}, s32[1,256]{1,0:T(1,128)S(1)}, u32[]{:S(2)}) copy-start(s32[1,256]{1,0:T(1,128)S(1)} %get-tuple-element.187.seg_row_ref) | copy-start | bytes 3076
  190.3 78.6 %copy-start.20 = (s32[1,256]{1,0:T(1,128)}, s32[1,256]{1,0:T(1,128)S(1)}, u32[]{:S(2)}) copy-start(s32[1,256]{1,0:T(1,128)S(1)} %get-tuple-element.185.refs_22_) | copy-start | bytes 3076
  190.3 78.6 %copy-start.21 = (s32[1,256]{1,0:T(1,128)}, s32[1,256]{1,0:T(1,128)S(1)}, u32[]{:S(2)}) copy-start(s32[1,256]{1,0:T(1,128)S(1)} %get-tuple-element.188.seg_row_ref) | copy-start | bytes 3076
  190.3 78.6 %copy-start.22 = (s32[1,256]{1,0:T(1,128)}, s32[1,256]{1,0:T(1,128)S(1)}, u32[]{:S(2)}) copy-start(s32[1,256]{1,0:T(1,128)S(1)} %get-tuple-element.186.seg_row_ref) | copy-start | bytes 3076
  284.7 0.9 copy-start.23
  435.6 12.4 %collective-permute-start.1 = (bf16[256,1536]{1,0:T(8,128)(2,1)}, bf16[256,1536]{1,0:T(8,128)(2,1)S(1)}, u32[]{:S(2)}, u32[]{:S(2)}) collective-permute-start(bf16[256,1536]{1,0:T(8,128)(2,1)} %get-tuple-element.103.second_hbm), channel_id=1, source_target_pairs={{0,16},{1,17},{2,18},{3,19},{4,20},{5,21},{6,22},{7,23},{8,24},{9,... | collective-permute-start | bytes 2359304 | tf_op jit(solution)/shard_map/ppermute | solution.py:25
  446.6 16.2 %collective-permute-start.2 = (bf16[256,1536]{1,0:T(8,128)(2,1)}, bf16[256,1536]{1,0:T(8,128)(2,1)S(1)}, u32[]{:S(2)}, u32[]{:S(2)}) collective-permute-start(bf16[256,1536]{1,0:T(8,128)(2,1)} %get-tuple-element.119), channel_id=1, source_target_pairs={{16,0},{17,1},{18,2},{19,3},{20,4},{21,5},{22,6},{23,7},{24,8},{25... | collective-permute-start | bytes 2359304 | tf_op jit(solution)/shard_map/ppermute | solution.py:25
  447.9 0.9 copy-start.24
  462.8 0.9 copy-start.25
  608.7 78.7 %collective-permute-start.3 = (bf16[256,1536]{1,0:T(8,128)(2,1)}, bf16[256,1536]{1,0:T(8,128)(2,1)S(1)}, u32[]{:S(2)}, u32[]{:S(2)}) collective-permute-start(bf16[256,1536]{1,0:T(8,128)(2,1)} %get-tuple-element.130.after.first_hbm), channel_id=1, source_target_pairs={{16,0},{17,1},{18,2},{19,3},{20,4},{21,5},{22,6},{23,7},{24,8},{25... | collective-permute-start | bytes 2359304 | tf_op jit(solution)/shard_map/ppermute | solution.py:25
  687.5 0.9 copy-start.26
  1032.3 12.7 %slice-start.2 = ((s8[6291456]{0:T(1024)(128)(4,1)}), s8[4194304]{0:T(1024)(128)(4,1)S(1)}, s32[]{:S(2)}) async-start(s8[6291456]{0:T(1024)(128)(4,1)} %bitcast.70), calls=%async_computation.2 | async-start | bytes 8388608
  1035.5 9.5 slice-start.3
  1035.5 16.1 %slice-start = ((s8[6291456]{0:T(1024)(128)(4,1)}), s8[4194304]{0:T(1024)(128)(4,1)S(1)}, s32[]{:S(2)}) async-start(s8[6291456]{0:T(1024)(128)(4,1)} %bitcast.68), calls=%async_computation | async-start | bytes 8388608
  1045.0 6.6 slice-start.1
  1051.6 6.6 copy-start.8
  1058.2 2.8 copy-start.7
  1061.0 2.6 copy-start.11
  1061.0 3.8 copy-start.10
  1063.5 2.5 copy-start.6
  1063.5 2.7 copy-start.9
